TPU v7x, 32 devices: a whole 2x2x4 slice. The times are simulated.
32 devices in a mesh: dp: 4 (over z), expert: 4 (over x, core), stream: 2 (over y).
Axes of the slice: x: 2, y: 2, z: 4, core: 2. Of those that a mesh axis runs over, the one named last changes fastest.
Arguments:
- patches: bfloat16 [32768, 768], P(('dp', 'expert', 'stream')), may hold values from -6 to 6
- cond: bfloat16 [128, 768], P(('dp', 'expert', 'stream')), may hold values from -6 to 6
- long_pack: int32 [32], P(('dp', 'expert', 'stream')), may hold values from 0 to 1
- routes: int32 [32768, 2], P(('dp', 'expert', 'stream')), may hold values from 0 to 7, all different within a row; in each aligned block of 1024 rows (0 to 1023, 1024 to 2047, ...) at most 320 rows name the same one
- ada_weight: bfloat16 [768, 4608], P('dp'), may hold values from -0.21875 to 0.21875
- qkv_weight: bfloat16 [768, 2304], P('dp'), may hold values from -0.21875 to 0.21875
- out_weight: bfloat16 [768, 768], P('dp'), may hold values from -0.625 to 0.625
- router_weight: bfloat16 [768, 8], P('dp'), may hold values from -0.15625 to 0.15625
- shared_up: bfloat16 [768, 3072], P('dp'), may hold values from -0.21875 to 0.21875
- shared_down: bfloat16 [3072, 768], P('dp'), may hold values from -0.109375 to 0.109375
- expert_up: bfloat16 [8, 768, 3072], P(('expert', 'stream'), 'dp'), may hold values from -0.21875 to 0.21875
- expert_down: bfloat16 [8, 3072, 768], P(('expert', 'stream'), 'dp'), may hold values from -0.109375 to 0.109375
- out_grad: bfloat16 [32768, 768], P(('dp', 'expert', 'stream')), may hold values from -6 to 6
Outputs:
- block_out: bfloat16 [32768, 768], P(('dp', 'expert', 'stream'))
- patches_grad: float32 [32768, 768], P(('dp', 'expert', 'stream'))
- cond_grad: float32 [128, 768], P(('dp', 'expert', 'stream'))
- ada_weight_grad: float32 [768, 4608], P('dp', ('expert', 'stream'))
- qkv_weight_grad: float32 [768, 2304], P('dp', ('expert', 'stream'))
- out_weight_grad: float32 [768, 768], P('dp', ('expert', 'stream'))
- router_weight_grad: float32 [768, 8], P('dp', ('expert', 'stream'))
- shared_up_grad: float32 [768, 3072], P('dp', ('expert', 'stream'))
- shared_down_grad: float32 [3072, 768], P('dp', ('expert', 'stream'))
- expert_up_grad: float32 [8, 768, 3072], P(('expert', 'stream'), 'dp')
- expert_down_grad: float32 [8, 3072, 768], P(('expert', 'stream'), 'dp')
Inputs may be any that keep to these rules, and one draw needn't show every extreme that they name: `long_pack`: 1: pack of one image of 1024 patches; 0: four images of 256 patches. `routes`: each row names 2 different experts; among the rows of one device no expert is named more than 320 times, and that number is reached.
All inputs are finite; a program needn't handle non-finite values.
Results may differ from a plain program's by a relative error of at most 0.02.
The roundings to bfloat16 on the way count: a program that leaves them out, or rounds other values in their place, can miss the bound.
Values may be sent and summed in bfloat16 or wider, within the bound.
No kernel may reach another device: no remote copies, remote signals or barrier semaphores. Data moves between devices by JAX's collectives and lax.ppermute only.
A program may use at most 256 MiB of HBM per device.

v0:
```python
import math

import jax
import jax.numpy as jnp
from jax import lax
from jax.sharding import PartitionSpec as P

HEADS = 12
HEAD = 64
TOP = 2
CAP = 320


EPSILON = 1e-06
MASKED = -1e30
WIDE_TYPE = jnp.float32
NARROW_TYPE = jnp.bfloat16


def product_plain_operands(left_side, right_side):
    return jnp.dot(left_side, right_side, preferred_element_type=WIDE_TYPE)


def product_left_operand(left_side, right_side):
    return lax.dot_general(
        left_side, right_side, (((0,), (0,)), ((), ())), preferred_element_type=WIDE_TYPE
    )


def product_right_operand(left_side, right_side):
    return lax.dot_general(
        left_side, right_side, (((1,), (1,)), ((), ())), preferred_element_type=WIDE_TYPE
    )


def normalize(values):
    centre = values - jnp.mean(values, axis=-1, keepdims=True)
    spread = jnp.mean(centre * centre, axis=-1, keepdims=True)
    reciprocal = lax.rsqrt(spread + EPSILON)
    return (centre * reciprocal, reciprocal)


def normalize_back(gradient, normed, reciprocal):
    return reciprocal * (
        gradient
        - jnp.mean(gradient, axis=-1, keepdims=True)
        - normed * jnp.mean(gradient * normed, axis=-1, keepdims=True)
    )


def gelu_tanh(values):
    return jax.nn.gelu(values, approximate=True)


def gelu_back(values, gradient):
    return jax.vjp(gelu_tanh, values)[1](gradient)[0]


def slot_places(route_rows, expert_count, capacity):
    pair_ids = route_rows.reshape(-1)
    onehot = (pair_ids[:, None] == jnp.arange(expert_count, dtype=jnp.int32)[None, :]).astype(
        jnp.int32
    )
    rank_values = jnp.cumsum(onehot, axis=0) - onehot
    slot_index = jnp.sum(rank_values * onehot, axis=1)
    destinations = pair_ids * capacity + slot_index
    pair_count = pair_ids.shape[0]
    sources = (
        jnp.full((expert_count * capacity,), pair_count, jnp.int32)
        .at[destinations]
        .set(jnp.arange(pair_count, dtype=jnp.int32))
    )
    return (destinations, sources)


def to_units(flat, pack_count):
    length = flat.shape[0] // pack_count
    shaped = flat.reshape(pack_count, length, HEADS // 2, 2, HEAD)
    return jnp.transpose(shaped, (0, 2, 1, 3, 4)).reshape(-1, length, 2, HEAD)


def from_units(units, pack_count):
    length = units.shape[1]
    shaped = units.reshape(pack_count, HEADS // 2, length, 2, HEAD)
    return jnp.transpose(shaped, (0, 2, 1, 3, 4)).reshape(pack_count * length, HEADS * HEAD)


def masked_scores(queries, keys, long_flag):
    length = queries.shape[0]
    position = jnp.arange(length, dtype=jnp.int32)
    image = jnp.where(long_flag == 1, 0, position // (length // 4))
    same = image[:, None] == image[None, :]
    scores = jnp.einsum("qhd,khd->hqk", queries, keys, preferred_element_type=WIDE_TYPE) * (
        1.0 / math.sqrt(HEAD)
    )
    return jnp.where(same[None], scores, MASKED)


def attend_forward(block_unit):
    queries, keys, values, long_flag = block_unit
    scores = masked_scores(queries, keys, long_flag)
    summit = jnp.max(scores, axis=-1, keepdims=True)
    weights = jnp.exp(scores - summit)
    row_total = jnp.sum(weights, axis=-1, keepdims=True)
    probabilities = (weights / row_total).astype(NARROW_TYPE)
    attended = jnp.einsum("hqk,khd->qhd", probabilities, values, preferred_element_type=WIDE_TYPE)
    return (attended.astype(NARROW_TYPE), summit[..., 0] + jnp.log(row_total[..., 0]))


def attend_backward(block_unit):
    queries, keys, values, long_flag, log_total, grad_attended = block_unit
    scale_factor = 1.0 / math.sqrt(HEAD)
    scores = masked_scores(queries, keys, long_flag)
    probabilities = jnp.exp(scores - log_total[..., None])
    grad_values = jnp.einsum(
        "hqk,qhd->khd",
        probabilities.astype(NARROW_TYPE),
        grad_attended,
        preferred_element_type=WIDE_TYPE,
    )
    grad_probs = jnp.einsum("qhd,khd->hqk", grad_attended, values, preferred_element_type=WIDE_TYPE)
    centre = jnp.sum(probabilities * grad_probs, axis=-1, keepdims=True)
    grad_scores = (probabilities * (grad_probs - centre)).astype(NARROW_TYPE)
    grad_queries = (
        jnp.einsum("hqk,khd->qhd", grad_scores, keys, preferred_element_type=WIDE_TYPE)
        * scale_factor
    )
    grad_keys = (
        jnp.einsum("hqk,qhd->khd", grad_scores, queries, preferred_element_type=WIDE_TYPE)
        * scale_factor
    )
    return (grad_queries, grad_keys, grad_values)


def on_device(
    patches,
    cond,
    long_pack,
    routes,
    ada_weight,
    qkv_weight,
    out_weight,
    router_weight,
    shared_up,
    shared_down,
    expert_up,
    expert_down,
    out_grad,
):
    collected_rows = (
        lax.all_gather(ada_weight, "dp", axis=0, tiled=True),
        lax.all_gather(qkv_weight, "dp", axis=0, tiled=True),
        lax.all_gather(out_weight, "dp", axis=0, tiled=True),
        lax.all_gather(router_weight, "dp", axis=0, tiled=True),
        lax.all_gather(shared_up, "dp", axis=0, tiled=True),
        lax.all_gather(shared_down, "dp", axis=0, tiled=True),
        lax.all_gather(expert_up, "dp", axis=1, tiled=True),
        lax.all_gather(expert_down, "dp", axis=1, tiled=True),
    )
    (
        modulation_weight_forward,
        query_key_value_forward,
        output_weight_forward,
        routing_weight_forward,
        shared_up_forward,
        shared_down_forward,
        expert_up_forward,
        expert_down_forward,
    ) = collected_rows
    feature_rows = patches.shape[1]
    row_count = patches.shape[0]
    pack_count = long_pack.shape[0]
    quarter = row_count // (4 * pack_count)
    experts = lax.axis_size(("expert", "stream"))
    capacity = CAP
    cond_wide = cond.astype(WIDE_TYPE)
    silu_cond = jax.nn.silu(cond_wide).astype(NARROW_TYPE)
    modulation = product_plain_operands(silu_cond, modulation_weight_forward)
    blocks = modulation.reshape(pack_count, 4, 6 * feature_rows)
    is_long = (long_pack == 1)[:, None, None]
    chosen = jnp.where(is_long, blocks[:, :1, :], blocks)[:, :, None, :]
    shift_one, scale_one, gate_one, shift_two, scale_two, gate_two = [
        chosen[..., part_index * feature_rows : (part_index + 1) * feature_rows]
        for part_index in range(6)
    ]
    tokens = patches.astype(WIDE_TYPE).reshape(pack_count, 4, quarter, feature_rows)
    normed_one, recip_one = normalize(tokens)
    first_in = (
        (normed_one * (1.0 + scale_one) + shift_one)
        .astype(NARROW_TYPE)
        .reshape(row_count, feature_rows)
    )
    joined = product_plain_operands(first_in, query_key_value_forward).astype(NARROW_TYPE)
    queries, keys, values = [
        to_units(joined[:, part_index * feature_rows : (part_index + 1) * feature_rows], pack_count)
        for part_index in range(3)
    ]
    long_flags = jnp.repeat(long_pack, HEADS // 2)
    attended_units, log_total = lax.map(attend_forward, (queries, keys, values, long_flags))
    attended = from_units(attended_units, pack_count)
    attention = product_plain_operands(attended, output_weight_forward).reshape(
        pack_count, 4, quarter, feature_rows
    )
    middle = tokens + gate_one * attention
    normed_two, recip_two = normalize(middle)
    second_in = (
        (normed_two * (1.0 + scale_two) + shift_two)
        .astype(NARROW_TYPE)
        .reshape(row_count, feature_rows)
    )
    shared_pre = product_plain_operands(second_in, shared_up_forward)
    shared_hidden = gelu_tanh(shared_pre).astype(NARROW_TYPE)
    shared = product_plain_operands(shared_hidden, shared_down_forward)
    logits = product_plain_operands(second_in, routing_weight_forward)
    onehot = (routes[:, :, None] == jnp.arange(experts, dtype=jnp.int32)[None, None, :]).astype(
        WIDE_TYPE
    )
    picked = jnp.sum(onehot * logits[:, None, :], axis=2)
    gate_values = jax.nn.softmax(picked, axis=1)
    destinations, sources = slot_places(routes, experts, capacity)
    padded = jnp.concatenate([second_in, jnp.zeros((1, feature_rows), NARROW_TYPE)], axis=0)
    outgoing = padded[sources // TOP].reshape(experts, capacity, feature_rows)
    single_expert_up = expert_up_forward[0]
    edown_one = expert_down_forward[0]
    incoming_rows = lax.all_to_all(
        outgoing, ("expert", "stream"), split_axis=0, concat_axis=0, tiled=True
    )
    item_count = incoming_rows.shape[1]
    flattened_rows = incoming_rows.reshape(-1, feature_rows)
    preactivation_rows = product_plain_operands(flattened_rows, single_expert_up)
    result_rows = (
        product_plain_operands(gelu_tanh(preactivation_rows).astype(NARROW_TYPE), edown_one)
        .astype(NARROW_TYPE)
        .reshape(experts, item_count, feature_rows)
    )
    came_back = lax.all_to_all(
        result_rows, ("expert", "stream"), split_axis=0, concat_axis=0, tiled=True
    )
    expert_pre = preactivation_rows.reshape(experts, item_count, -1)
    expert_out = (
        came_back.reshape(experts * capacity, feature_rows)[destinations]
        .reshape(row_count, TOP, feature_rows)
        .astype(WIDE_TYPE)
    )
    mixture = shared + jnp.sum(gate_values[:, :, None] * expert_out, axis=1)
    mixture_blocks = mixture.reshape(pack_count, 4, quarter, feature_rows)
    block_out = (
        (middle + gate_two * mixture_blocks).reshape(row_count, feature_rows).astype(NARROW_TYPE)
    )
    recollected_rows = (
        lax.all_gather(ada_weight, "dp", axis=0, tiled=True),
        lax.all_gather(qkv_weight, "dp", axis=0, tiled=True),
        lax.all_gather(out_weight, "dp", axis=0, tiled=True),
        lax.all_gather(router_weight, "dp", axis=0, tiled=True),
        lax.all_gather(shared_up, "dp", axis=0, tiled=True),
        lax.all_gather(shared_down, "dp", axis=0, tiled=True),
        lax.all_gather(expert_up, "dp", axis=1, tiled=True),
        lax.all_gather(expert_down, "dp", axis=1, tiled=True),
    )
    (
        modulation_weight_backward,
        query_key_value_backward,
        output_weight_backward,
        routing_weight_backward,
        shared_up_backward,
        shared_down_backward,
        expert_up_backward,
        expert_down_backward,
    ) = recollected_rows
    grad_out = out_grad.astype(WIDE_TYPE).reshape(pack_count, 4, quarter, feature_rows)
    grad_gate_two = jnp.sum(grad_out * mixture_blocks, axis=2)
    grad_mixture = (grad_out * gate_two).reshape(row_count, feature_rows)
    grad_shared = grad_mixture.astype(NARROW_TYPE)
    grad_expert_out = (gate_values[:, :, None] * grad_mixture[:, None, :]).astype(NARROW_TYPE)
    grad_gate = jnp.sum(grad_mixture[:, None, :] * expert_out, axis=2)
    grad_picked = gate_values * (
        grad_gate - jnp.sum(gate_values * grad_gate, axis=1, keepdims=True)
    )
    grad_logits = jnp.sum(onehot * grad_picked[:, :, None], axis=1).astype(NARROW_TYPE)
    pair_rows = jnp.concatenate(
        [
            grad_expert_out.reshape(TOP * row_count, feature_rows),
            jnp.zeros((1, feature_rows), NARROW_TYPE),
        ],
        axis=0,
    )
    grad_outgoing = pair_rows[sources].reshape(experts, capacity, feature_rows)
    grad_arrived = lax.all_to_all(
        grad_outgoing, ("expert", "stream"), split_axis=0, concat_axis=0, tiled=True
    )
    flat_grad = grad_arrived.reshape(-1, feature_rows)
    pre_flat = expert_pre.reshape(experts * capacity, -1)
    hidden_rows = gelu_tanh(pre_flat).astype(NARROW_TYPE)
    grad_edown = product_left_operand(hidden_rows, flat_grad)
    preactivation_rows_gradient = gelu_back(
        pre_flat, product_right_operand(flat_grad, expert_down_backward[0])
    ).astype(NARROW_TYPE)
    expert_up_gradient = product_left_operand(
        incoming_rows.reshape(-1, feature_rows), preactivation_rows_gradient
    )
    grad_rows = (
        product_right_operand(preactivation_rows_gradient, expert_up_backward[0])
        .astype(NARROW_TYPE)
        .reshape(experts, capacity, feature_rows)
    )
    grad_came_back = lax.all_to_all(
        grad_rows, ("expert", "stream"), split_axis=0, concat_axis=0, tiled=True
    )
    grad_from_experts = (
        grad_came_back.reshape(experts * capacity, feature_rows)[destinations]
        .reshape(row_count, TOP, feature_rows)
        .astype(WIDE_TYPE)
    )
    grad_shared_pre = gelu_back(
        shared_pre, product_right_operand(grad_shared, shared_down_backward)
    ).astype(NARROW_TYPE)
    grad_down = product_left_operand(shared_hidden, grad_shared)
    grad_up = product_left_operand(second_in, grad_shared_pre)
    grad_router = product_left_operand(second_in, grad_logits)
    grad_second = (
        product_right_operand(grad_shared_pre, shared_up_backward)
        + product_right_operand(grad_logits, routing_weight_backward)
        + jnp.sum(grad_from_experts, axis=1)
    )
    grad_second_blocks = grad_second.reshape(pack_count, 4, quarter, feature_rows)
    grad_shift_two = jnp.sum(grad_second_blocks, axis=2)
    grad_scale_two = jnp.sum(grad_second_blocks * normed_two, axis=2)
    grad_middle = grad_out + normalize_back(
        grad_second_blocks * (1.0 + scale_two), normed_two, recip_two
    )
    grad_gate_one = jnp.sum(grad_middle * attention, axis=2)
    grad_attention = (grad_middle * gate_one).reshape(row_count, feature_rows).astype(NARROW_TYPE)
    grad_out_weight = product_left_operand(attended, grad_attention)
    grad_attended = product_right_operand(grad_attention, output_weight_backward).astype(
        NARROW_TYPE
    )
    grad_units = to_units(grad_attended, pack_count)
    grad_queries, grad_keys, grad_values = lax.map(
        attend_backward, (queries, keys, values, long_flags, log_total, grad_units)
    )
    grad_joined = jnp.concatenate(
        [
            from_units(grad_queries, pack_count),
            from_units(grad_keys, pack_count),
            from_units(grad_values, pack_count),
        ],
        axis=1,
    ).astype(NARROW_TYPE)
    grad_qkv_weight = product_left_operand(first_in, grad_joined)
    grad_first = product_right_operand(grad_joined, query_key_value_backward).reshape(
        pack_count, 4, quarter, feature_rows
    )
    grad_shift_one = jnp.sum(grad_first, axis=2)
    grad_scale_one = jnp.sum(grad_first * normed_one, axis=2)
    patches_grad = (
        grad_middle + normalize_back(grad_first * (1.0 + scale_one), normed_one, recip_one)
    ).reshape(row_count, feature_rows)
    grad_chosen = jnp.concatenate(
        [
            grad_shift_one,
            grad_scale_one,
            grad_gate_one,
            grad_shift_two,
            grad_scale_two,
            grad_gate_two,
        ],
        axis=-1,
    )
    long_total = jnp.sum(grad_chosen, axis=1, keepdims=True)
    first_slot = (jnp.arange(4, dtype=jnp.int32) == 0)[None, :, None]
    grad_blocks = jnp.where(is_long, jnp.where(first_slot, long_total, 0.0), grad_chosen)
    grad_modulation = grad_blocks.reshape(4 * pack_count, 6 * feature_rows).astype(NARROW_TYPE)
    grad_ada = product_left_operand(silu_cond, grad_modulation)
    grad_silu = product_right_operand(grad_modulation, modulation_weight_backward)
    cond_grad = jax.vjp(jax.nn.silu, cond_wide)[1](grad_silu)[0]
    summed = (
        lax.psum_scatter(
            grad_ada.astype(jnp.bfloat16), "dp", scatter_dimension=0, tiled=True
        ).astype(jnp.float32),
        lax.psum_scatter(
            grad_qkv_weight.astype(jnp.bfloat16), "dp", scatter_dimension=0, tiled=True
        ).astype(jnp.float32),
        lax.psum_scatter(
            grad_out_weight.astype(jnp.bfloat16), "dp", scatter_dimension=0, tiled=True
        ).astype(jnp.float32),
        lax.psum_scatter(
            grad_router.astype(jnp.bfloat16), "dp", scatter_dimension=0, tiled=True
        ).astype(jnp.float32),
        lax.psum_scatter(
            grad_up.astype(jnp.bfloat16), "dp", scatter_dimension=0, tiled=True
        ).astype(jnp.float32),
        lax.psum_scatter(
            grad_down.astype(jnp.bfloat16), "dp", scatter_dimension=0, tiled=True
        ).astype(jnp.float32),
        lax.psum_scatter(
            expert_up_gradient[None].astype(jnp.bfloat16), "dp", scatter_dimension=1, tiled=True
        ).astype(jnp.float32),
        lax.psum_scatter(
            grad_edown[None].astype(jnp.bfloat16), "dp", scatter_dimension=1, tiled=True
        ).astype(jnp.float32),
    )
    final_shared = (
        lax.psum_scatter(
            summed[0].astype(jnp.bfloat16), ("expert", "stream"), scatter_dimension=1, tiled=True
        ).astype(jnp.float32),
        lax.psum_scatter(
            summed[1].astype(jnp.bfloat16), ("expert", "stream"), scatter_dimension=1, tiled=True
        ).astype(jnp.float32),
        lax.psum_scatter(
            summed[2].astype(jnp.bfloat16), ("expert", "stream"), scatter_dimension=1, tiled=True
        ).astype(jnp.float32),
        lax.psum_scatter(
            summed[3].astype(jnp.bfloat16), ("expert", "stream"), scatter_dimension=1, tiled=True
        ).astype(jnp.float32),
        lax.psum_scatter(
            summed[4].astype(jnp.bfloat16), ("expert", "stream"), scatter_dimension=1, tiled=True
        ).astype(jnp.float32),
        lax.psum_scatter(
            summed[5].astype(jnp.bfloat16), ("expert", "stream"), scatter_dimension=1, tiled=True
        ).astype(jnp.float32),
    )
    expert_up_grad = summed[6]
    expert_down_grad = summed[7]
    return (
        block_out,
        patches_grad,
        cond_grad,
        final_shared[0],
        final_shared[1],
        final_shared[2],
        final_shared[3],
        final_shared[4],
        final_shared[5],
        expert_up_grad,
        expert_down_grad,
    )


def solution(mesh):
    in_specs = (
        P(("dp", "expert", "stream"), None),
        P(("dp", "expert", "stream"), None),
        P(("dp", "expert", "stream")),
        P(("dp", "expert", "stream"), None),
        P("dp", None),
        P("dp", None),
        P("dp", None),
        P("dp", None),
        P("dp", None),
        P("dp", None),
        P(("expert", "stream"), "dp", None),
        P(("expert", "stream"), "dp", None),
        P(("dp", "expert", "stream"), None),
    )
    out_specs = (
        P(("dp", "expert", "stream"), None),
        P(("dp", "expert", "stream"), None),
        P(("dp", "expert", "stream"), None),
        P("dp", ("expert", "stream")),
        P("dp", ("expert", "stream")),
        P("dp", ("expert", "stream")),
        P("dp", ("expert", "stream")),
        P("dp", ("expert", "stream")),
        P("dp", ("expert", "stream")),
        P(("expert", "stream"), "dp", None),
        P(("expert", "stream"), "dp", None),
    )
    return jax.shard_map(
        on_device, mesh=mesh, in_specs=in_specs, out_specs=out_specs, check_vma=False
    )
```

profile of v0, /device:TPU:0, one launch (start us, length us, event | category | flops | bytes accessed | tf_op | source)
XLA Modules:
  0.0 1527.1 jit_solution(12666326027181546379)
XLA Ops:
  17.1 8.1 scatter_custom_fusion
  25.2 115.4 %all-gather.9.cloned.1.call-done = bf16[768,4608]{1,0:T(8,128)(2,1)} async-done(((bf16[192,4608]{1,0:T(8,128)(2,1)}), bf16[768,4608]{1,0:T(8,128)(2,1)}) %all-gather.9.cloned.1.call-update) | async-done | bytes 7077904 | tf_op jit(solution)/shard_map/all_gather | solution.py:151
  146.0 64.3 %all-gather.11.cloned.1.call-done = bf16[768,2304]{1,0:T(8,128)(2,1)} async-done(((bf16[192,2304]{1,0:T(8,128)(2,1)}), bf16[768,2304]{1,0:T(8,128)(2,1)}) %all-gather.11.cloned.1.call-update) | async-done | bytes 3538960 | tf_op jit(solution)/shard_map/all_gather | solution.py:152
  210.4 6.2 convolution_convert_fusion.1
  224.5 70.6 %while.30 = (s32[]{:T(128)}, bf16[6,1024,2,64]{1,3,2,0:T(8,128)(2,1)}, f32[6,2,1024]{2,1,0:T(2,128)}, bf16[6,1024,2,64]{1,3,2,0:T(8,128)(2,1)}, s32[6]{0:T(128)S...) while((s32[]{:T(128)}, ...), condition=%wide.region_5.6_spmd, body=%wide.region_2.5_spmd.sunk | while | flops 563223552 | bytes 30485108 | solution.py:199
  295.7 5.1 fusion.122
  307.1 8.6 gather_fusion
  321.1 13.8 all-gather
  345.3 8.5 mul.633
  357.3 8.5 gather_fusion.2
  365.8 10.1 fusion.125
  380.5 40.0 %all-gather.19.cloned.1.call-done = bf16[1,768,3072]{2,1,0:T(8,128)(2,1)} async-done(((bf16[1,192,3072]{2,1,0:T(8,128)(2,1)}), bf16[1,768,3072]{2,1,0:T(8,128)(2,1)}) %all-gather.19.cloned.1.call-update) | async-done | bytes 4718608 | tf_op jit(solution)/shard_map/all_gather | solution.py:157
  420.5 27.2 %multiply_convert_fusion.1 = (bf16[2560,3072]{1,0:T(8,128)(2,1)}, f32[2560,3072]{1,0:T(8,128)}) fusion(bf16[2560,768]{1,0:T(8,128)(2,1)} %bitcast.52, bf16[1,768,3072]{2,1,0:T(8,128)(2,1)} %all-gather.19.cloned.1.call-done), kind=kOutput, calls=%fused_computation.91 | convolution fusion | flops 12150374400 | bytes 55836672 | tf_op jit(solution)/shard_map/dot_general | solution.py:21
  447.7 62.1 %all-gather.21.cloned.1.call-done = bf16[1,3072,768]{2,1,0:T(8,128)(2,1)} async-done(((bf16[1,768,768]{2,1,0:T(8,128)(2,1)}), bf16[1,3072,768]{2,1,0:T(8,128)(2,1)}) %all-gather.21.cloned.1.call-update) | async-done | bytes 4718608 | tf_op jit(solution)/shard_map/all_gather | solution.py:158
  509.8 17.7 %convolution_convert_fusion.8 = bf16[2560,768]{1,0:T(8,128)(2,1)} fusion(bf16[2560,3072]{1,0:T(8,128)(2,1)} %get-tuple-element.355, bf16[1,3072,768]{2,1,0:T(8,128)(2,1)} %all-gather.21.cloned.1.call-done), kind=kOutput, calls=%fused_computation.113 | convolution fusion | flops 12081561600 | bytes 24379392 | tf_op jit(solution)/shard_map/dot_general | solution.py:21
  532.2 38.5 %fusion.68 = bf16[2560,3072]{1,0:T(8,128)(2,1)} fusion(f32[2560,3072]{1,0:T(8,128)} %get-tuple-element.356, bf16[2560,768]{1,0:T(8,128)(2,1)} %bitcast.58, bf16[1,3072,768]{2,1,0:T(8,128)(2,1)} %all-gather.21.cloned.1.call-done), kind=kOutput, calls=%fused_computation.90 | convolution fusion | flops 12236881920 | bytes 55836672 | tf_op jit(solution)/shard_map/dot_general | solution.py:31
  570.7 17.8 %convolution_convert_fusion.7 = bf16[2560,768]{1,0:T(8,128)(2,1)} fusion(bf16[2560,3072]{1,0:T(8,128)(2,1)} %fusion.68, bf16[1,768,3072]{2,1,0:T(8,128)(2,1)} %all-gather.19.cloned.1.call-done), kind=kOutput, calls=%fused_computation.112 | convolution fusion | flops 12081561600 | bytes 24379392 | tf_op jit(solution)/shard_map/dot_general | solution.py:31
  588.5 4.8 all-to-all-start.3
  593.4 5.9 all-gather.17.cloned.1.call-done
  599.3 14.2 fusion.75
  613.5 11.4 fusion.127
  624.9 12.7 gather_fusion.1
  637.6 7.8 reshape.964
  645.4 17.1 %multiply_reduce_fusion.1 = (f32[1024,2]{1,0:T(8,128)}, f32[1024,768]{1,0:T(8,128)}) fusion(f32[1024,2,768]{2,1,0:T(2,128)} %reshape.964, f32[1024,768]{1,0:T(8,128)S(1)} %copy-done.7, f32[1024,2]{1,0:T(8,128)} %copy.84), kind=kLoop, calls=%fused_computation.104 | loop fusion | flops 5502976 | bytes 12599296 | tf_op jit(solution)/shard_map/reduce_sum | solution.py:275
  663.9 11.5 gather_fusion.3
  680.1 12.1 reduce_sum.257
  696.5 15.2 fusion.84
  716.9 9.6 convolution_convert_fusion.5
  728.4 11.7 convolution_convert_fusion.4
  744.5 127.7 %while.31 = (s32[]{:T(128)}, bf16[6,1024,2,64]{1,3,2,0:T(8,128)(2,1)}, bf16[6,1024,2,64]{1,3,2,0:T(8,128)(2,1)}, bf16[6,1024,2,64]{1,3,2,0:T(8,128)(2,1)}, bf16[...) while((s32[]{:T(128)}, ...), condition=%wide.region_24.25_spmd, body=%wide.region_22.24_spmd.sunk | while | flops 1374952448 | bytes 83170504 | solution.py:338
  872.3 8.0 convolution_convert_fusion.6
  882.2 7.7 fusion.91
  896.4 4.9 convolution_convert_fusion
  908.6 10.3 reduce-scatter.34.cloned.1.call-done
  921.3 18.7 %fusion.82 = bf16[1,3072,768]{2,1,0:T(8,128)(2,1)} fusion(bf16[2560,3072]{1,0:T(8,128)(2,1)} %get-tuple-element.355, bf16[2560,768]{1,0:T(8,128)(2,1)} %bitcast.58), kind=kOutput, calls=%fused_computation.129 | convolution fusion | flops 12081954816 | bytes 24379392 | tf_op jit(solution)/shard_map/dot_general | solution.py:25
  940.1 18.8 %fusion.81 = bf16[1,768,3072]{2,1,0:T(8,128)(2,1)} fusion(bf16[2560,768]{1,0:T(8,128)(2,1)} %bitcast.52, bf16[2560,3072]{1,0:T(8,128)(2,1)} %fusion.68), kind=kOutput, calls=%fused_computation.128 | convolution fusion | flops 12081954816 | bytes 24379392 | tf_op jit(solution)/shard_map/dot_general | solution.py:25
  958.9 29.2 %reduce-scatter.28.cloned.1.call-done = bf16[192,2304]{1,0:T(8,128)(2,1)} async-done(((bf16[768,2304]{1,0:T(8,128)(2,1)}), bf16[192,2304]{1,0:T(8,128)(2,1)}) %reduce-scatter.28.cloned.1.call-update) | async-done | bytes 884752 | tf_op jit(solution)/shard_map/reduce_scatter | solution.py:380
  990.6 123.5 %reduce-scatter.26.cloned.1.call-done = bf16[192,4608]{1,0:T(8,128)(2,1)} async-done(((bf16[768,4608]{1,0:T(8,128)(2,1)}), bf16[192,4608]{1,0:T(8,128)(2,1)}) %reduce-scatter.26.cloned.1.call-update) | async-done | bytes 1769488 | tf_op jit(solution)/shard_map/reduce_scatter | solution.py:377
  1123.3 5.6 fusion.105
  1128.8 8.0 reduce-scatter.46.cloned.1.call-done
  1137.7 13.4 all-reduce.2
  1152.4 20.3 %reduce-scatter.44.cloned.1.call-done = bf16[96,192]{1,0:T(8,128)(2,1)} async-done(((bf16[768,192]{1,0:T(8,128)(2,1)}), bf16[96,192]{1,0:T(8,128)(2,1)}) %reduce-scatter.44.cloned.1.call-update) | async-done | bytes 36880
  1174.3 41.0 %reduce-scatter.48.cloned.1.call-done = bf16[384,192]{1,0:T(8,128)(2,1)} async-done(((bf16[3072,192]{1,0:T(8,128)(2,1)}), bf16[384,192]{1,0:T(8,128)(2,1)}) %reduce-scatter.48.cloned.1.call-update) | async-done | bytes 147472
  1217.1 39.0 %reduce-scatter.50.cloned.1.call-done = bf16[96,768]{1,0:T(8,128)(2,1)} async-done(((bf16[768,768]{1,0:T(8,128)(2,1)}), bf16[96,768]{1,0:T(8,128)(2,1)}) %reduce-scatter.50.cloned.1.call-update) | async-done | bytes 147472
  1258.0 85.5 %reduce-scatter.38.cloned.1.call-done = bf16[1,768,768]{2,1,0:T(8,128)(2,1)} async-done(((bf16[1,3072,768]{2,1,0:T(8,128)(2,1)}), bf16[1,768,768]{2,1,0:T(8,128)(2,1)}) %reduce-scatter.38.cloned.1.call-update) | async-done | bytes 1179664 | tf_op jit(solution)/shard_map/reduce_scatter | solution.py:398
  1346.3 85.1 %reduce-scatter.36.cloned.1.call-done = bf16[1,192,3072]{2,1,0:T(8,128)(2,1)} async-done(((bf16[1,768,3072]{2,1,0:T(8,128)(2,1)}), bf16[1,192,3072]{2,1,0:T(8,128)(2,1)}) %reduce-scatter.36.cloned.1.call-update) | async-done | bytes 1179664 | tf_op jit(solution)/shard_map/reduce_scatter | solution.py:395
  1434.4 37.6 %reduce-scatter.42.cloned.1.call-done = bf16[288,192]{1,0:T(8,128)(2,1)} async-done(((bf16[2304,192]{1,0:T(8,128)(2,1)}), bf16[288,192]{1,0:T(8,128)(2,1)}) %reduce-scatter.42.cloned.1.call-update) | async-done | bytes 110608
  1473.8 44.3 %reduce-scatter.40.cloned.1.call-done = bf16[576,192]{1,0:T(8,128)(2,1)} async-done(((bf16[4608,192]{1,0:T(8,128)(2,1)}), bf16[576,192]{1,0:T(8,128)(2,1)}) %reduce-scatter.40.cloned.1.call-update) | async-done | bytes 221200
  (416 shorter events, 315.3 us)
Async XLA Ops:
  7.2 133.3 %all-gather.9.cloned.1.call-start = ((), (), s32[]{:S(2)}) async-start(), calls=%async_computation.17 | async-start | bytes 8847360 | tf_op jit(solution)/shard_map/all_gather | solution.py:151
  7.9 202.4 %all-gather.11.cloned.1.call-start = ((), (), s32[]{:S(2)}) async-start(), calls=%async_computation.18 | async-start | bytes 4423680 | tf_op jit(solution)/shard_map/all_gather | solution.py:152
  8.7 286.5 %all-gather.13.cloned.1.call-start = ((), (), s32[]{:S(2)}) async-start(), calls=%async_computation.19 | async-start | bytes 1474560 | tf_op jit(solution)/shard_map/all_gather | solution.py:153
  9.4 356.4 %all-gather.15.cloned.1.call-start = ((), (), s32[]{:S(2)}) async-start(), calls=%async_computation.20 | async-start | bytes 5898240 | tf_op jit(solution)/shard_map/all_gather | solution.py:155
  10.0 410.5 %all-gather.19.cloned.1.call-start = ((), (), s32[]{:S(2)}) async-start(), calls=%async_computation.22 | async-start | bytes 5898240 | tf_op jit(solution)/shard_map/all_gather | solution.py:157
  10.6 499.2 %all-gather.21.cloned.1.call-start = ((), (), s32[]{:S(2)}) async-start(), calls=%async_computation.23 | async-start | bytes 5898240 | tf_op jit(solution)/shard_map/all_gather | solution.py:158
  11.2 129.4 %copy-start.51 = (bf16[4,768]{1,0:T(4,128)(2,1)S(1)}, bf16[4,768]{1,0:T(4,128)(2,1)}, u32[]{:S(2)}) copy-start(bf16[4,768]{1,0:T(4,128)(2,1)} %param.18) | copy-start | bytes 18436
  12.9 131.8 %copy-start.45 = (f32[1024]{0:T(1024)}, f32[1024]{0:T(1024)S(1)}, u32[]{:S(2)}) copy-start(f32[1024]{0:T(1024)S(1)} %broadcast_multiply_fusion.6) | copy-start | bytes 12292
  13.6 131.2 %copy-start.54 = (f32[1024]{0:T(1024)}, f32[1024]{0:T(1024)S(1)}, u32[]{:S(2)}) copy-start(f32[1024]{0:T(1024)S(1)} %add_rsqrt_fusion.1) | copy-start | bytes 12292
  144.7 151.0 %copy-start.30 = (f32[4,768]{1,0:T(4,128)}, f32[4,768]{1,0:T(4,128)S(1)}, u32[]{:S(2)}) copy-start(f32[4,768]{1,0:T(4,128)S(1)} %get-tuple-element.351) | copy-start | bytes 36868
  144.7 156.6 %copy-start.25 = (f32[4,768]{1,0:T(4,128)}, f32[4,768]{1,0:T(4,128)S(1)}, u32[]{:S(2)}) copy-start(f32[4,768]{1,0:T(4,128)S(1)} %get-tuple-element.348) | copy-start | bytes 36868
  144.7 156.6 %copy-start.41 = (f32[4,768]{1,0:T(4,128)}, f32[4,768]{1,0:T(4,128)S(1)}, u32[]{:S(2)}) copy-start(f32[4,768]{1,0:T(4,128)S(1)} %get-tuple-element.346) | copy-start | bytes 36868
  146.0 64.3 %copy-start.20 = (bf16[1024,768]{1,0:T(8,128)(2,1)}, bf16[1024,768]{1,0:T(8,128)(2,1)S(1)}, u32[]{:S(2)}) copy-start(bf16[1024,768]{1,0:T(8,128)(2,1)S(1)} %fusion.86) | copy-start | bytes 4718596
  315.7 60.2 %all-to-all-start = ((bf16[8,320,768]{2,1,0:T(8,128)(2,1)}), bf16[8,320,768]{2,1,0:T(8,128)(2,1)}, u32[]{:S(2)}, u32[]{:S(2)}) async-start(bf16[8,320,768]{2,1,0:T(8,128)(2,1)} %bitcast.332), calls=%async_computation | async-start | bytes 7864320 | tf_op jit(solution)/shard_map/all_to_all | solution.py:225
  320.4 20.3 %copy-start.6 = (f32[1024,768]{1,0:T(8,128)S(1)}, f32[1024,768]{1,0:T(8,128)}, u32[]{:S(2)}) copy-start(f32[1024,768]{1,0:T(8,128)} %get-tuple-element.360) | copy-start | bytes 9437188
  320.4 278.9 %all-gather.17.cloned.1.call-start = ((), (), s32[]{:S(2)}) async-start(), calls=%async_computation.21 | async-start | bytes 5898240 | tf_op jit(solution)/shard_map/all_gather | solution.py:156
  375.9 151.6 %all-to-all-start.2 = ((bf16[8,320,768]{2,1,0:T(8,128)(2,1)}), bf16[8,320,768]{2,1,0:T(8,128)(2,1)}, u32[]{:S(2)}, u32[]{:S(2)}) async-start(bf16[8,320,768]{2,1,0:T(8,128)(2,1)} %bitcast.333), calls=%async_computation.2 | async-start | bytes 7864320 | tf_op jit(solution)/shard_map/all_to_all | solution.py:288
  527.5 61.0 %all-to-all-start.1 = ((bf16[8,320,768]{2,1,0:T(8,128)(2,1)}), bf16[8,320,768]{2,1,0:T(8,128)(2,1)}, u32[]{:S(2)}, u32[]{:S(2)}) async-start(bf16[8,320,768]{2,1,0:T(8,128)(2,1)} %bitcast.345), calls=%async_computation.1 | async-start | bytes 7864320 | tf_op jit(solution)/shard_map/all_to_all | solution.py:236
  588.5 10.7 copy-start.7
  588.5 75.3 %all-to-all-start.3 = ((bf16[8,320,768]{2,1,0:T(8,128)(2,1)}), bf16[8,320,768]{2,1,0:T(8,128)(2,1)}, u32[]{:S(2)}, u32[]{:S(2)}) async-start(bf16[8,320,768]{2,1,0:T(8,128)(2,1)} %bitcast.344), calls=%async_computation.3 | async-start | bytes 7864320 | tf_op jit(solution)/shard_map/all_to_all | solution.py:306
  593.4 310.6 %reduce-scatter.30.cloned.1.call-start = ((), (), s32[]{:S(2)}) async-start(), calls=%async_computation.26 | async-start | bytes 1474560 | tf_op jit(solution)/shard_map/reduce_scatter | solution.py:383
  613.5 11.4 copy-start.65
  613.5 11.4 copy-start.53
  645.4 18.4 %copy-start.29 = (f32[1024,2]{0,1:T(2,128)S(1)}, f32[1024,2]{0,1:T(2,128)}, u32[]{:S(2)}) copy-start(f32[1024,2]{0,1:T(2,128)} %copy-done.28) | copy-start | bytes 24580
  645.4 18.4 %copy-start.48 = (f32[1024]{0:T(1024)S(1)}, f32[1024]{0:T(1024)}, u32[]{:S(2)}) copy-start(f32[1024]{0:T(1024)} %copy-done.47) | copy-start | bytes 12292
  645.4 18.4 %copy-start.57 = (f32[1024]{0:T(1024)S(1)}, f32[1024]{0:T(1024)}, u32[]{:S(2)}) copy-start(f32[1024]{0:T(1024)} %copy-done.56) | copy-start | bytes 12292
  645.4 18.5 %copy-start.38 = (s32[1024,2]{0,1:T(2,128)S(1)}, s32[1024,2]{0,1:T(2,128)}, u32[]{:S(2)}) copy-start(s32[1024,2]{0,1:T(2,128)} %param.20) | copy-start | bytes 24580
  663.9 28.4 %copy-start.33 = (bf16[1024,8]{0,1:T(8,128)(2,1)}, bf16[1024,8]{0,1:T(8,128)(2,1)S(1)}, u32[]{:S(2)}) copy-start(bf16[1024,8]{0,1:T(8,128)(2,1)S(1)} %select_reduce_fusion) | copy-start | bytes 49156
  680.1 12.1 copy-start.1
  680.1 12.1 copy-start.26
  680.1 12.1 copy-start.36
  680.1 12.1 copy-start.44
  680.1 12.1 copy-start.50
  696.2 15.5 %copy-start.4 = (f32[1024,768]{1,0:T(8,128)}, f32[1024,768]{1,0:T(8,128)S(1)}, u32[]{:S(2)}) copy-start(f32[1024,768]{1,0:T(8,128)S(1)} %get-tuple-element.357) | copy-start | bytes 9437188
  716.8 189.1 %reduce-scatter.32.cloned.1.call-start = ((), (), s32[]{:S(2)}) async-start(), calls=%async_computation.27 | async-start | bytes 5898240 | tf_op jit(solution)/shard_map/reduce_scatter | solution.py:389
  726.5 192.4 %reduce-scatter.34.cloned.1.call-start = ((), (), s32[]{:S(2)}) async-start(), calls=%async_computation.28 | async-start | bytes 5898240 | tf_op jit(solution)/shard_map/reduce_scatter | solution.py:392
  740.2 247.9 %reduce-scatter.28.cloned.1.call-start = ((), (), s32[]{:S(2)}) async-start(), calls=%async_computation.25 | async-start | bytes 4423680 | tf_op jit(solution)/shard_map/reduce_scatter | solution.py:380
  744.5 127.8 %copy-start.21 = (bf16[1024,768]{1,0:T(8,128)(2,1)S(1)}, bf16[1024,768]{1,0:T(8,128)(2,1)}, u32[]{:S(2)}) copy-start(bf16[1024,768]{1,0:T(8,128)(2,1)} %copy-done.20) | copy-start | bytes 4718596
  880.3 233.8 %reduce-scatter.26.cloned.1.call-start = ((), (), s32[]{:S(2)}) async-start(), calls=%async_computation.24 | async-start | bytes 8847360 | tf_op jit(solution)/shard_map/reduce_scatter | solution.py:377
  901.4 235.5 %reduce-scatter.46.cloned.1.call-start = ((), (), s32[]{:S(2)}) async-start(), calls=%async_computation.34 | async-start | bytes 245760
  903.9 268.8 %reduce-scatter.44.cloned.1.call-start = ((), (), s32[]{:S(2)}) async-start(), calls=%async_computation.33 | async-start | bytes 442368
  905.9 309.4 %reduce-scatter.48.cloned.1.call-start = ((), (), s32[]{:S(2)}) async-start(), calls=%async_computation.35 | async-start | bytes 1769472
  908.5 347.5 %reduce-scatter.50.cloned.1.call-start = ((), (), s32[]{:S(2)}) async-start(), calls=%async_computation.36 | async-start | bytes 1327104
  921.3 422.2 %reduce-scatter.38.cloned.1.call-start = ((), (), s32[]{:S(2)}) async-start(), calls=%async_computation.30 | async-start | bytes 5898240 | tf_op jit(solution)/shard_map/reduce_scatter | solution.py:398
  940.0 491.4 %reduce-scatter.36.cloned.1.call-start = ((), (), s32[]{:S(2)}) async-start(), calls=%async_computation.29 | async-start | bytes 5898240 | tf_op jit(solution)/shard_map/reduce_scatter | solution.py:395
  958.9 513.1 %reduce-scatter.42.cloned.1.call-start = ((), (), s32[]{:S(2)}) async-start(), calls=%async_computation.32 | async-start | bytes 1327104
  990.5 127.6 %copy-start.62 = (u32[32]{0:T(128)S(1)}, u32[32]{0:T(128)}, u32[]{:S(2)}) copy-start(u32[32]{0:T(128)} %constant.231) | copy-start | bytes 388
  990.5 527.6 %reduce-scatter.40.cloned.1.call-start = ((), (), s32[]{:S(2)}) async-start(), calls=%async_computation.31 | async-start | bytes 2654208
  (52 other events, 193.8 us)
Sparse Core Ops, SparseCore 0:
  9.6 130.8 all-gather.8
  142.1 68.2 all-gather.10
  211.9 29.0 all-gather.12
  242.4 88.7 all-gather.14
  332.6 87.8 all-gather.18
  421.9 87.8 all-gather.20
  511.4 87.8 all-gather.16
  716.9 27.5 reduce-scatter.29
  746.9 83.9 reduce-scatter.31
  833.1 85.7 reduce-scatter.33
  921.2 66.8 reduce-scatter.27
  990.3 123.7 reduce-scatter.25
  1116.9 19.8 reduce-scatter.45
  1140.6 32.0 reduce-scatter.43
  1176.8 38.4 reduce-scatter.47
  1219.3 36.7 reduce-scatter.49
  1258.2 85.2 reduce-scatter.37
  1345.6 85.7 reduce-scatter.35
  1434.7 37.2 reduce-scatter.41
  1475.6 42.4 reduce-scatter.39
where the time goes:
time: 1530 us
  waiting for transfers between devices  816 us (53%)
  matrix products  403 us (26%)
  local copies, waits for them, and re-layouts  137 us (9%)
  other arithmetic  98.4 us (6%)
  blocking collectives  27.2 us (2%)
  starting transfers between devices  19.8 us (1%)
  between operations  16.2 us (1%)
    unnamed x26, waiting for transfers between devices  195 us
    reduce_scatter x1, waiting for transfers between devices, on_device(): lax.psum_scatter(grad_ada.astype(jnp.bfloat16), 'dp', scatter_dimension=0...  124 us
    all_gather x1, waiting for transfers between devices, on_device(): lax.all_gather(ada_weight, 'dp', axis=0, tiled=True)  115 us
    dot_general x8, matrix products, product_right_operand(): lax.dot_general(left_side, right_side, (((1,), (1,)), ((), ())), preferre...  102 us
    dot_general x8, matrix products, product_plain_operands(): return jnp.dot(left_side, right_side, preferred_element_type=WIDE_TYPE)  87.4 us
    reduce_scatter x1, waiting for transfers between devices, on_device(): lax.psum_scatter(grad_edown[None].astype(jnp.bfloat16), 'dp', scatter_dim...  85.5 us
    reduce_scatter x1, waiting for transfers between devices, on_device(): lax.psum_scatter(expert_up_gradient[None].astype(jnp.bfloat16), 'dp', sca...  85.1 us
    dot_general x8, matrix products, product_left_operand(): lax.dot_general(left_side, right_side, (((0,), (0,)), ((), ())), preferre...  75.9 us
  transfers between devices with their start and end apart: 24, of which 16 were waited for; matrix products, arithmetic and copies ran while one was open for 37% of the time, Pallas kernels for 0%

commit v1 on v0

v1 whole, which is shorter than its diff:
```python
import math

import jax
import jax.numpy as jnp
from jax import lax
from jax.sharding import PartitionSpec as P

HEADS = 12
HEAD = 64
TOP = 2
CAP = 320


EPSILON = 1e-06
MASKED = -1e30
WIDE_TYPE = jnp.float32
NARROW_TYPE = jnp.bfloat16


def product_plain_operands(left_side, right_side):
    return jnp.dot(left_side, right_side, preferred_element_type=WIDE_TYPE)


def product_left_operand(left_side, right_side):
    return lax.dot_general(
        left_side, right_side, (((0,), (0,)), ((), ())), preferred_element_type=WIDE_TYPE
    )


def product_right_operand(left_side, right_side):
    return lax.dot_general(
        left_side, right_side, (((1,), (1,)), ((), ())), preferred_element_type=WIDE_TYPE
    )


def normalize(values):
    centre = values - jnp.mean(values, axis=-1, keepdims=True)
    spread = jnp.mean(centre * centre, axis=-1, keepdims=True)
    reciprocal = lax.rsqrt(spread + EPSILON)
    return (centre * reciprocal, reciprocal)


def normalize_back(gradient, normed, reciprocal):
    return reciprocal * (
        gradient
        - jnp.mean(gradient, axis=-1, keepdims=True)
        - normed * jnp.mean(gradient * normed, axis=-1, keepdims=True)
    )


def gelu_tanh(values):
    return jax.nn.gelu(values, approximate=True)


def gelu_back(values, gradient):
    return jax.vjp(gelu_tanh, values)[1](gradient)[0]


PLANE = ("expert", "stream")
CORE, SIDES = 2, (4, 1, 5)


def flip(value, mask):
    count = lax.axis_size(PLANE)
    return lax.ppermute(value, PLANE, [(index, index ^ mask) for index in range(count)])


def plane_gather(piece):
    me = lax.axis_index(PLANE)
    near = jnp.stack([piece] + [flip(piece, mask) for mask in SIDES])
    far = flip(near, CORE)
    result = jnp.zeros((8,) + piece.shape, piece.dtype)
    for place, mask in enumerate((0,) + SIDES):
        result = lax.dynamic_update_index_in_dim(result, near[place], me ^ mask, 0)
        result = lax.dynamic_update_index_in_dim(result, far[place], me ^ mask ^ CORE, 0)
    return result


def plane_scatter(parts):
    me = lax.axis_index(PLANE)
    chip_x, core, chip_y = me // 4, (me // 2) % 2, me % 2
    grid = parts.reshape((2, 2, 2) + parts.shape[1:])
    kept = lax.dynamic_index_in_dim(grid, core, 1, keepdims=False)
    sent = lax.dynamic_index_in_dim(grid, 1 - core, 1, keepdims=False)
    pair = kept.astype(WIDE_TYPE) + flip(sent, CORE).astype(WIDE_TYPE)
    pair = pair.reshape((4,) + parts.shape[1:])
    narrow = pair.astype(NARROW_TYPE)
    place = 2 * chip_x + chip_y
    total = lax.dynamic_index_in_dim(pair, place, 0, keepdims=False)
    for mask, other in ((4, 2), (1, 1), (5, 3)):
        piece = lax.dynamic_index_in_dim(narrow, place ^ other, 0, keepdims=False)
        total = total + flip(piece, mask).astype(WIDE_TYPE)
    return total


def slot_of_routes(route_rows, expert_count, capacity):
    pair_ids = route_rows.reshape(-1)
    onehot = (pair_ids[:, None] == jnp.arange(expert_count, dtype=jnp.int32)[None, :]).astype(
        jnp.int32
    )
    rank_values = jnp.cumsum(onehot, axis=0) - onehot
    slot_index = jnp.sum(rank_values * onehot, axis=1)
    return (pair_ids * capacity + slot_index).reshape(route_rows.shape)


def to_units(flat, pack_count):
    length = flat.shape[0] // pack_count
    shaped = flat.reshape(pack_count, length, HEADS // 2, 2, HEAD)
    return jnp.transpose(shaped, (0, 2, 1, 3, 4)).reshape(-1, length, 2, HEAD)


def from_units(units, pack_count):
    length = units.shape[1]
    shaped = units.reshape(pack_count, HEADS // 2, length, 2, HEAD)
    return jnp.transpose(shaped, (0, 2, 1, 3, 4)).reshape(pack_count * length, HEADS * HEAD)


def masked_scores(queries, keys, long_flag):
    length = queries.shape[0]
    position = jnp.arange(length, dtype=jnp.int32)
    image = jnp.where(long_flag == 1, 0, position // (length // 4))
    same = image[:, None] == image[None, :]
    scores = jnp.einsum("qhd,khd->hqk", queries, keys, preferred_element_type=WIDE_TYPE) * (
        1.0 / math.sqrt(HEAD)
    )
    return jnp.where(same[None], scores, MASKED)


def attend_forward(block_unit):
    queries, keys, values, long_flag = block_unit
    scores = masked_scores(queries, keys, long_flag)
    summit = jnp.max(scores, axis=-1, keepdims=True)
    weights = jnp.exp(scores - summit)
    row_total = jnp.sum(weights, axis=-1, keepdims=True)
    probabilities = (weights / row_total).astype(NARROW_TYPE)
    attended = jnp.einsum("hqk,khd->qhd", probabilities, values, preferred_element_type=WIDE_TYPE)
    return (attended.astype(NARROW_TYPE), summit[..., 0] + jnp.log(row_total[..., 0]))


def attend_backward(block_unit):
    queries, keys, values, long_flag, log_total, grad_attended = block_unit
    scale_factor = 1.0 / math.sqrt(HEAD)
    scores = masked_scores(queries, keys, long_flag)
    probabilities = jnp.exp(scores - log_total[..., None])
    grad_values = jnp.einsum(
        "hqk,qhd->khd",
        probabilities.astype(NARROW_TYPE),
        grad_attended,
        preferred_element_type=WIDE_TYPE,
    )
    grad_probs = jnp.einsum("qhd,khd->hqk", grad_attended, values, preferred_element_type=WIDE_TYPE)
    centre = jnp.sum(probabilities * grad_probs, axis=-1, keepdims=True)
    grad_scores = (probabilities * (grad_probs - centre)).astype(NARROW_TYPE)
    grad_queries = (
        jnp.einsum("hqk,khd->qhd", grad_scores, keys, preferred_element_type=WIDE_TYPE)
        * scale_factor
    )
    grad_keys = (
        jnp.einsum("hqk,qhd->khd", grad_scores, queries, preferred_element_type=WIDE_TYPE)
        * scale_factor
    )
    return (grad_queries, grad_keys, grad_values)


def on_device(
    patches,
    cond,
    long_pack,
    routes,
    ada_weight,
    qkv_weight,
    out_weight,
    router_weight,
    shared_up,
    shared_down,
    expert_up,
    expert_down,
    out_grad,
):
    row_count, width = patches.shape
    pack_count = long_pack.shape[0]
    quarter = row_count // (4 * pack_count)
    hidden = shared_up.shape[1]
    depth = lax.axis_size("dp")
    experts = lax.axis_size(PLANE)
    capacity = CAP
    slots = experts * capacity
    local = qkv_weight.shape[0]
    slice_rows = local // experts
    plane_index = lax.axis_index(PLANE)

    def own(rows):
        return lax.dynamic_slice_in_dim(rows, plane_index * slice_rows, slice_rows, 0)

    down_rows = lax.dynamic_slice_in_dim(
        shared_down.reshape(4, local, width), plane_index * slice_rows, slice_rows, 1
    )
    first_group = lax.all_gather(own(qkv_weight), "dp", axis=0)
    second_group = lax.all_gather(
        jnp.concatenate(
            [
                own(out_weight),
                own(shared_up),
                jnp.transpose(down_rows, (1, 0, 2)).reshape(slice_rows, 4 * width),
                jnp.pad(own(router_weight), ((0, 0), (0, 128 - router_weight.shape[1]))),
            ],
            axis=1,
        ),
        "dp",
        axis=0,
    )

    def whole(group):
        gathered = plane_gather(group)
        return jnp.transpose(gathered, (1, 0, 2, 3)).reshape(width, -1)

    cond_wide = cond.astype(WIDE_TYPE)
    silu_cond = jax.nn.silu(cond_wide).astype(NARROW_TYPE)
    cond_rows = silu_cond.shape[0]
    silu_parts = lax.all_to_all(
        jnp.transpose(silu_cond.reshape(cond_rows, depth, local), (1, 0, 2)),
        "dp",
        split_axis=0,
        concat_axis=0,
        tiled=True,
    ).reshape(depth * cond_rows, local)
    partial = product_plain_operands(silu_parts, ada_weight)
    modulation = jnp.sum(
        lax.all_to_all(
            partial.reshape(depth, cond_rows, 6 * width), "dp", split_axis=0, concat_axis=0, tiled=True
        ),
        axis=0,
    )
    blocks = modulation.reshape(pack_count, 4, 6 * width)
    is_long = (long_pack == 1)[:, None, None]
    chosen = jnp.where(is_long, blocks[:, :1, :], blocks)[:, :, None, :]
    shift_one, scale_one, gate_one, shift_two, scale_two, gate_two = [
        chosen[..., part_index * width : (part_index + 1) * width] for part_index in range(6)
    ]

    places = slot_of_routes(routes, experts, capacity)
    slot_ids = jnp.arange(slots, dtype=jnp.int32)
    take_one = places[:, 0][:, None] == slot_ids[None, :]
    take_two = places[:, 1][:, None] == slot_ids[None, :]
    spread = jnp.logical_or(
        slot_ids[:, None] == places[:, 0][None, :], slot_ids[:, None] == places[:, 1][None, :]
    ).astype(NARROW_TYPE)

    def exchange(rows):
        return lax.all_to_all(
            rows.reshape((experts, capacity) + rows.shape[1:]),
            PLANE,
            split_axis=0,
            concat_axis=0,
            tiled=True,
        ).reshape(rows.shape)

    grad_out = out_grad.astype(WIDE_TYPE).reshape(pack_count, 4, quarter, width)
    grad_mixture = (grad_out * gate_two).reshape(row_count, width)
    grad_shared = grad_mixture.astype(NARROW_TYPE)
    mixture_rows = exchange(product_plain_operands(spread, grad_shared).astype(NARROW_TYPE))

    qkv_full = whole(first_group)
    tokens = patches.astype(WIDE_TYPE).reshape(pack_count, 4, quarter, width)
    normed_one, recip_one = normalize(tokens)
    first_in = (
        (normed_one * (1.0 + scale_one) + shift_one).astype(NARROW_TYPE).reshape(row_count, width)
    )
    joined = product_plain_operands(first_in, qkv_full).astype(NARROW_TYPE)
    queries, keys, values = [
        to_units(joined[:, part_index * width : (part_index + 1) * width], pack_count)
        for part_index in range(3)
    ]
    long_flags = jnp.repeat(long_pack, HEADS // 2)
    attended_units, log_total = lax.map(attend_forward, (queries, keys, values, long_flags))
    attended = from_units(attended_units, pack_count)
    rest = whole(second_group)
    out_full = rest[:, :width]
    up_full = rest[:, width : width + hidden]
    down_full = jnp.transpose(
        rest[:, width + hidden : width + 2 * hidden].reshape(depth, local, 4, width), (0, 2, 1, 3)
    ).reshape(hidden, width)
    router_full = rest[:, width + 2 * hidden : width + 2 * hidden + experts]
    attention = product_plain_operands(attended, out_full).reshape(pack_count, 4, quarter, width)
    middle = tokens + gate_one * attention
    normed_two, recip_two = normalize(middle)
    second_in = (
        (normed_two * (1.0 + scale_two) + shift_two).astype(NARROW_TYPE).reshape(row_count, width)
    )
    logits = product_plain_operands(second_in, router_full)
    onehot = (routes[:, :, None] == jnp.arange(experts, dtype=jnp.int32)[None, None, :]).astype(
        WIDE_TYPE
    )
    picked = jnp.sum(onehot * logits[:, None, :], axis=2)
    gate_values = jax.nn.softmax(picked, axis=1)
    slot_gates = jnp.sum(
        jnp.where(take_one, gate_values[:, :1], 0.0) + jnp.where(take_two, gate_values[:, 1:], 0.0),
        axis=0,
    )
    gates_there = exchange(slot_gates)
    expert_rows = exchange(product_plain_operands(spread, second_in).astype(NARROW_TYPE))

    expert_up_full = lax.all_gather(expert_up[0], "dp", axis=0, tiled=True)
    expert_down_full = lax.all_gather(expert_down[0], "dp", axis=0, tiled=True)
    expert_pre = product_plain_operands(expert_rows, expert_up_full)
    expert_hidden = gelu_tanh(expert_pre).astype(NARROW_TYPE)
    result_rows = product_plain_operands(expert_hidden, expert_down_full).astype(NARROW_TYPE)
    wide_rows = mixture_rows.astype(WIDE_TYPE)
    gate_dots = jnp.sum(result_rows.astype(WIDE_TYPE) * wide_rows, axis=1)
    expert_grad = (gates_there[:, None] * wide_rows).astype(NARROW_TYPE)
    grad_expert_pre = gelu_back(
        expert_pre, product_right_operand(expert_grad, expert_down_full)
    ).astype(NARROW_TYPE)
    grad_rows = product_right_operand(grad_expert_pre, expert_up_full).astype(NARROW_TYPE)
    grad_rows_back = exchange(grad_rows)
    gate_dots_back = exchange(gate_dots)
    result_back = exchange(result_rows)
    grad_expert_up = product_left_operand(expert_rows, grad_expert_pre)
    grad_expert_down = product_left_operand(expert_hidden, expert_grad)
    expert_up_grad = lax.psum_scatter(
        grad_expert_up.astype(NARROW_TYPE), "dp", scatter_dimension=0, tiled=True
    ).astype(WIDE_TYPE)[None]
    expert_down_grad = lax.psum_scatter(
        grad_expert_down.astype(NARROW_TYPE), "dp", scatter_dimension=0, tiled=True
    ).astype(WIDE_TYPE)[None]

    shared_pre = product_plain_operands(second_in, up_full)
    shared_hidden = gelu_tanh(shared_pre).astype(NARROW_TYPE)
    shared = product_plain_operands(shared_hidden, down_full)
    grad_shared_pre = gelu_back(shared_pre, product_right_operand(grad_shared, down_full)).astype(
        NARROW_TYPE
    )
    grad_up = product_left_operand(grad_shared_pre, second_in).astype(NARROW_TYPE)
    grad_down = product_left_operand(grad_shared, shared_hidden).astype(NARROW_TYPE)
    middle_parts = jnp.concatenate(
        [
            grad_up.reshape(experts, hidden // experts, width),
            jnp.transpose(
                grad_down.reshape(experts, width // experts, 4, hidden // 4), (0, 2, 1, 3)
            ).reshape(experts, 4 * width // experts, hidden // 4),
        ],
        axis=1,
    )
    middle_sum = plane_scatter(middle_parts).astype(NARROW_TYPE)
    up_sum = middle_sum[: hidden // experts].T
    down_sum = jnp.transpose(
        middle_sum[hidden // experts :].reshape(4, width // experts, hidden // 4), (0, 2, 1)
    ).reshape(hidden, width // experts)
    down_sum = jnp.transpose(
        down_sum.reshape(depth, 4, local, width // experts), (0, 2, 1, 3)
    ).reshape(width, 4 * width // experts)
    middle_final = lax.psum_scatter(
        jnp.concatenate([up_sum, down_sum], axis=1), "dp", scatter_dimension=0, tiled=True
    ).astype(WIDE_TYPE)
    shared_up_grad = middle_final[:, : hidden // experts]
    shared_down_grad = jnp.transpose(
        middle_final[:, hidden // experts :].reshape(local, 4, width // experts), (1, 0, 2)
    ).reshape(4 * local, width // experts)

    grad_gate = jnp.stack(
        [
            jnp.sum(jnp.where(take_one, gate_dots_back[None, :], 0.0), axis=1),
            jnp.sum(jnp.where(take_two, gate_dots_back[None, :], 0.0), axis=1),
        ],
        axis=1,
    )
    grad_picked = gate_values * (
        grad_gate - jnp.sum(gate_values * grad_gate, axis=1, keepdims=True)
    )
    grad_logits = jnp.sum(onehot * grad_picked[:, :, None], axis=1).astype(NARROW_TYPE)
    grad_router = product_left_operand(grad_logits, second_in)
    collect = jnp.logical_or(take_one, take_two).astype(NARROW_TYPE)
    grad_second = (
        product_right_operand(grad_shared_pre, up_full)
        + product_right_operand(grad_logits, router_full)
        + product_plain_operands(collect, grad_rows_back)
    )

    mixture = (
        shared
        + gate_values[:, :1] * product_plain_operands(take_one.astype(NARROW_TYPE), result_back)
        + gate_values[:, 1:] * product_plain_operands(take_two.astype(NARROW_TYPE), result_back)
    )
    mixture_blocks = mixture.reshape(pack_count, 4, quarter, width)
    block_out = (middle + gate_two * mixture_blocks).reshape(row_count, width).astype(NARROW_TYPE)
    grad_gate_two = jnp.sum(grad_out * mixture_blocks, axis=2)

    grad_second_blocks = grad_second.reshape(pack_count, 4, quarter, width)
    grad_shift_two = jnp.sum(grad_second_blocks, axis=2)
    grad_scale_two = jnp.sum(grad_second_blocks * normed_two, axis=2)
    grad_middle = grad_out + normalize_back(
        grad_second_blocks * (1.0 + scale_two), normed_two, recip_two
    )
    grad_gate_one = jnp.sum(grad_middle * attention, axis=2)
    grad_attention = (grad_middle * gate_one).reshape(row_count, width).astype(NARROW_TYPE)
    grad_out_weight = product_left_operand(grad_attention, attended)
    grad_attended = product_right_operand(grad_attention, out_full).astype(NARROW_TYPE)
    grad_units = to_units(grad_attended, pack_count)
    grad_queries, grad_keys, grad_values = lax.map(
        attend_backward, (queries, keys, values, long_flags, log_total, grad_units)
    )
    grad_joined = jnp.concatenate(
        [
            from_units(grad_queries, pack_count),
            from_units(grad_keys, pack_count),
            from_units(grad_values, pack_count),
        ],
        axis=1,
    ).astype(NARROW_TYPE)
    grad_qkv = product_left_operand(grad_joined, first_in)
    last_parts = jnp.concatenate(
        [
            grad_qkv.astype(NARROW_TYPE).reshape(experts, 3 * width // experts, width),
            grad_out_weight.astype(NARROW_TYPE).reshape(experts, width // experts, width),
            jnp.pad(grad_router.astype(NARROW_TYPE)[:, None, :], ((0, 0), (0, 15), (0, 0))),
        ],
        axis=1,
    )
    last_sum = plane_scatter(last_parts).astype(NARROW_TYPE)
    last_final = lax.psum_scatter(last_sum.T, "dp", scatter_dimension=0, tiled=True).astype(
        WIDE_TYPE
    )
    edge_one, edge_two = 3 * width // experts, 4 * width // experts
    qkv_weight_grad = last_final[:, :edge_one]
    out_weight_grad = last_final[:, edge_one:edge_two]
    router_weight_grad = last_final[:, edge_two : edge_two + 1]

    grad_first = product_right_operand(grad_joined, qkv_full).reshape(
        pack_count, 4, quarter, width
    )
    grad_shift_one = jnp.sum(grad_first, axis=2)
    grad_scale_one = jnp.sum(grad_first * normed_one, axis=2)
    patches_grad = (
        grad_middle + normalize_back(grad_first * (1.0 + scale_one), normed_one, recip_one)
    ).reshape(row_count, width)
    grad_chosen = jnp.concatenate(
        [
            grad_shift_one,
            grad_scale_one,
            grad_gate_one,
            grad_shift_two,
            grad_scale_two,
            grad_gate_two,
        ],
        axis=-1,
    )
    long_total = jnp.sum(grad_chosen, axis=1, keepdims=True)
    first_slot = (jnp.arange(4, dtype=jnp.int32) == 0)[None, :, None]
    grad_blocks = jnp.where(is_long, jnp.where(first_slot, long_total, 0.0), grad_chosen)
    grad_modulation = grad_blocks.reshape(cond_rows, 6 * width).astype(NARROW_TYPE)
    grad_all = lax.all_gather(grad_modulation, "dp", axis=0, tiled=True)
    silu_parts_grad = lax.all_to_all(
        product_right_operand(grad_all, ada_weight).reshape(depth, cond_rows, local),
        "dp",
        split_axis=0,
        concat_axis=0,
        tiled=True,
    )
    grad_silu = jnp.transpose(silu_parts_grad, (1, 0, 2)).reshape(cond_rows, width)
    cond_grad = jax.vjp(jax.nn.silu, cond_wide)[1](grad_silu)[0]
    silu_all = lax.all_gather(silu_parts, PLANE, axis=0, tiled=True)
    grad_columns = lax.all_to_all(
        jnp.transpose(
            grad_all.reshape(depth * cond_rows, experts, 6 * width // experts), (1, 0, 2)
        ),
        PLANE,
        split_axis=0,
        concat_axis=0,
        tiled=True,
    ).reshape(experts * depth * cond_rows, 6 * width // experts)
    ada_weight_grad = product_left_operand(silu_all, grad_columns)
    return (
        block_out,
        patches_grad,
        cond_grad,
        ada_weight_grad,
        qkv_weight_grad,
        out_weight_grad,
        router_weight_grad,
        shared_up_grad,
        shared_down_grad,
        expert_up_grad,
        expert_down_grad,
    )


def solution(mesh):
    in_specs = (
        P(("dp", "expert", "stream"), None),
        P(("dp", "expert", "stream"), None),
        P(("dp", "expert", "stream")),
        P(("dp", "expert", "stream"), None),
        P("dp", None),
        P("dp", None),
        P("dp", None),
        P("dp", None),
        P("dp", None),
        P("dp", None),
        P(("expert", "stream"), "dp", None),
        P(("expert", "stream"), "dp", None),
        P(("dp", "expert", "stream"), None),
    )
    out_specs = (
        P(("dp", "expert", "stream"), None),
        P(("dp", "expert", "stream"), None),
        P(("dp", "expert", "stream"), None),
        P("dp", ("expert", "stream")),
        P("dp", ("expert", "stream")),
        P("dp", ("expert", "stream")),
        P("dp", ("expert", "stream")),
        P("dp", ("expert", "stream")),
        P("dp", ("expert", "stream")),
        P(("expert", "stream"), "dp", None),
        P(("expert", "stream"), "dp", None),
    )
    return jax.shard_map(
        on_device, mesh=mesh, in_specs=in_specs, out_specs=out_specs, check_vma=False
    )
```

time: 1530 us -> 1040 us (0.68)
  waiting for transfers between devices: 816 us -> 203 us
  starting transfers between devices: 19.8 us -> 58.6 us
  blocking collectives: 27.2 us -> 54.5 us
  matrix products: 403 us -> 430 us
  other arithmetic: 98.4 us -> 115 us
    all_gather x7 -> x3, waiting for transfers between devices: 288 us -> 0.02 us  [the longest x1 0.02 us: on_device(): expert_up_full = lax.all_gather(expert_up[0], 'dp', axis=0, tiled=True)]
    reduce_scatter x7 -> x2, waiting for transfers between devices: 334 us -> 68.6 us  [the longest x1 68.6 us: on_device(): lax.psum_scatter(grad_expert_up.astype(NARROW_TYPE), 'dp', scatter_dimens...]
    unnamed x26 -> x9, waiting for transfers between devices: 195 us -> 1.49 us
    ppermute x0 -> x16, waiting for transfers between devices: none -> 91.2 us  [flip(): lax.ppermute(value, PLANE, [(index, index ^ mask) for index in range(coun...]
    all_to_all x4 -> x10, waiting for transfers between devices: 0.01 us -> 41.9 us  [the longest x6 27.7 us: exchange(): lax.all_to_all(rows.reshape((experts, capacity) + rows.shape[1:]), PLANE,...]
    gather x4 -> x0, local copies, waits for them, and re-layouts: 41.3 us -> none  [the longest x1 12.7 us: on_device(): came_back.reshape(experts * capacity, feature_rows)[destinations]]
    all_gather x1 -> x3, blocking collectives: 13.8 us -> 54.5 us  [the longest x1 21.1 us: on_device(): first_group = lax.all_gather(own(qkv_weight), 'dp', axis=0)]
    dot_general x8 -> x13, matrix products: 87.4 us -> 123 us  [product_plain_operands(): return jnp.dot(left_side, right_side, preferred_element_type=WIDE_TYPE)]
  transfers between devices with their start and end apart: 24 -> 33, of which waited for: 16 -> 10; matrix products, arithmetic and copies ran while one was open for 37% -> 46% of each run, Pallas kernels for 0% -> 0%
where the time goes in v1:
time: 1040 us
  matrix products  430 us (41%)
  waiting for transfers between devices  203 us (20%)
  local copies, waits for them, and re-layouts  150 us (14%)
  other arithmetic  115 us (11%)
  starting transfers between devices  58.6 us (6%)
  blocking collectives  54.5 us (5%)
  between operations  16.4 us (2%)
    dot_general x13, matrix products, product_plain_operands(): return jnp.dot(left_side, right_side, preferred_element_type=WIDE_TYPE)  123 us
    dot_general x8, matrix products, product_right_operand(): lax.dot_general(left_side, right_side, (((1,), (1,)), ((), ())), preferre...  100 us
    ppermute x16, waiting for transfers between devices, flip(): lax.ppermute(value, PLANE, [(index, index ^ mask) for index in range(coun...  91.2 us
    reduce_scatter x1, waiting for transfers between devices, on_device(): lax.psum_scatter(grad_expert_up.astype(NARROW_TYPE), 'dp', scatter_dimens...  68.6 us
    dot_general x8, matrix products, product_left_operand(): lax.dot_general(left_side, right_side, (((0,), (0,)), ((), ())), preferre...  68.5 us
    dot_general x12, matrix products, masked_scores(): jnp.einsum('qhd,khd->hqk', queries, keys, preferred_element_type=WIDE_TYPE)  31.6 us
    all_to_all x6, waiting for transfers between devices, exchange(): lax.all_to_all(rows.reshape((experts, capacity) + rows.shape[1:]), PLANE,...  27.7 us
    dot_general x6, matrix products, attend_forward(): jnp.einsum('hqk,khd->qhd', probabilities, values, preferred_element_type=...  26.4 us
  transfers between devices with their start and end apart: 33, of which 10 were waited for; matrix products, arithmetic and copies ran while one was open for 46% of the time, Pallas kernels for 0%

profile of v1, /device:TPU:0, one launch (start us, length us, event | category | flops | bytes accessed | tf_op | source)
XLA Modules:
  0.0 1036.6 jit_solution(2793461382315278830)
XLA Ops:
  14.9 21.1 %all-gather = bf16[96,2304]{1,0:T(8,128)(2,1)} all-gather(bf16[24,2304]{1,0:T(8,128)(2,1)S(1)} %constant_dynamic-slice_fusion.3), channel_id=2, replica_groups=mesh['dp'=4,'expert'=4,'stream'=2] {'dp'}, dimensions={0}, use_global_device_ids=true | all-gather | bytes 552960 | tf_op jit(solution)/shard_map/all_gather | solution.py:198
  60.3 5.6 all-to-all-start.1
  69.7 10.6 %all-to-all-done.1 = f32[4,4,4608]{2,1,0:T(4,128)} async-done(((f32[4,4,4608]{2,1,0:T(4,128)}), f32[4,4,4608]{2,1,0:T(4,128)}, u32[]{:S(2)}, u32[]{:S(2)}) %all-to-all-start.1) | async-done | bytes 294944 | tf_op jit(solution)/shard_map/all_to_all | solution.py:229
  85.1 6.8 fusion.99
  95.4 4.9 broadcast_in_dim.243
  114.2 6.0 convolution_convert_fusion
  130.4 13.4 %collective-permute-done.5 = bf16[4,24,7040]{2,1,0:T(8,128)(2,1)} collective-permute-done((bf16[4,24,7040]{2,1,0:T(8,128)(2,1)}, bf16[4,24,7040]{2,1,0:T(8,128)(2,1)}, u32[]{:S(2)}, u32[]{:S(2)}) %collective-permute-start.5) | collective-permute-done | bytes 1351712 | tf_op jit(solution)/shard_map/ppermute | solution.py:65
  143.8 6.0 pad_maximum_fusion
  149.8 71.3 %while.30 = (s32[]{:T(128)}, bf16[6,1024,2,64]{1,3,2,0:T(8,128)(2,1)}, f32[6,2,1024]{2,1,0:T(2,128)}, bf16[6,1024,2,64]{1,3,2,0:T(8,128)(2,1)}, s32[6]{0:T(128)S...) while((s32[]{:T(128)}, ...), condition=%wide.region_6.7_spmd, body=%wide.region_3.6_spmd.sunk | while | flops 563223552 | bytes 30485108 | solution.py:275
  238.7 5.2 fusion.168
  246.1 6.8 fusion.96
  252.9 8.1 fusion.113
  269.1 9.8 reshape.997
  282.2 15.2 %fusion.75 = bf16[1024,3072]{1,0:T(8,128)(2,1)S(1)} fusion(f32[1024,3072]{1,0:T(8,128)} %fusion.113, bf16[1024,768]{1,0:T(8,128)(2,1)S(1)} %copy-done.22, bf16[3072,768]{1,0:T(8,128)(2,1)S(1)} %bitcast.485), kind=kOutput, calls=%fused_computation.95 | convolution fusion | flops 4894752768 | bytes 25165824 | tf_op jit(solution)/shard_map/dot_general | solution.py:31
  297.4 12.3 %convolution_convert_fusion.3 = bf16[768,3072]{1,0:T(8,128)(2,1)} fusion(bf16[1024,768]{1,0:T(8,128)(2,1)S(1)} %copy-done.22, f32[1024,3072]{1,0:T(8,128)} %fusion.113), kind=kOutput, calls=%fused_computation.132 | convolution fusion | flops 4862509056 | bytes 18874368 | tf_op jit(solution)/shard_map/dot_general | solution.py:25
  309.7 6.9 convolution_convert_fusion.4
  316.6 5.0 all-to-all-start.4
  321.6 27.1 %multiply_convert_fusion.1 = (bf16[2560,3072]{1,0:T(8,128)(2,1)}, f32[2560,3072]{1,0:T(8,128)}) fusion(bf16[2560,768]{1,0:T(8,128)(2,1)} %bitcast.81, bf16[1,768,3072]{2,1,0:T(8,128)(2,1)} %all-gather.11.cloned.1.call-done), kind=kOutput, calls=%fused_computation.86 | convolution fusion | flops 12150374400 | bytes 55836672 | tf_op jit(solution)/shard_map/dot_general | solution.py:21
  348.7 18.3 %all-to-all-done.4 = bf16[8,320,768]{2,1,0:T(8,128)(2,1)} async-done(((bf16[8,320,768]{2,1,0:T(8,128)(2,1)}), bf16[8,320,768]{2,1,0:T(8,128)(2,1)}, u32[]{:S(2)}, u32[]{:S(2)}) %all-to-all-start.4) | async-done | bytes 3932192 | tf_op jit(solution)/shard_map/all_to_all | solution.py:250
  367.0 19.2 %fusion.86 = (f32[2560]{0:T(1024)S(1)}, bf16[2560,768]{1,0:T(8,128)(2,1)}) fusion(bf16[8,320,768]{2,1,0:T(8,128)(2,1)} %all-to-all-done.4, bf16[2560,3072]{1,0:T(8,128)(2,1)} %get-tuple-element.379, bf16[1,3072,768]{2,1,0:T(8,128)(2,1)} %all-gather.13.cloned.1.call-done), kind=kOutput, calls=%fused_computation.118 | convolution fusion | flops 12089423872 | bytes 28321792 | tf_op jit(solution)/shard_map/dot_general | solution.py:21
  390.5 9.8 reshape.1029
  400.2 5.4 copy.204
  405.7 7.1 select_reduce_fusion.1
  417.7 4.9 fusion.103
  427.8 4.7 fusion.87
  432.4 38.4 %fusion.68 = bf16[2560,3072]{1,0:T(8,128)(2,1)} fusion(f32[2560,3072]{1,0:T(8,128)} %get-tuple-element.380, bf16[2560,768]{1,0:T(8,128)(2,1)} %fusion.87, bf16[1,3072,768]{2,1,0:T(8,128)(2,1)} %all-gather.13.cloned.1.call-done), kind=kOutput, calls=%fused_computation.85 | convolution fusion | flops 12236881920 | bytes 55836672 | tf_op jit(solution)/shard_map/dot_general | solution.py:31
  470.8 18.0 %convolution_convert_fusion.6 = bf16[2560,768]{1,0:T(8,128)(2,1)} fusion(bf16[2560,3072]{1,0:T(8,128)(2,1)} %fusion.68, bf16[1,768,3072]{2,1,0:T(8,128)(2,1)} %all-gather.11.cloned.1.call-done), kind=kOutput, calls=%fused_computation.137 | convolution fusion | flops 12081561600 | bytes 24379392 | tf_op jit(solution)/shard_map/dot_general | solution.py:31
  488.8 4.5 all-to-all-start.7
  493.5 13.3 %fusion.167 = f32[1024,768]{1,0:T(8,128)} fusion(bf16[3072,768]{1,0:T(8,128)(2,1)} %bitcast.486, f32[1024,3072]{1,0:T(8,128)} %fusion.113), kind=kOutput, calls=%fused_computation.320 | convolution fusion | flops 4860149760 | bytes 20447232 | tf_op jit(solution)/shard_map/dot_general | solution.py:21
  511.2 4.8 convert_add_fusion
  521.0 8.4 fusion.77
  529.4 9.4 all-to-all-done.7
  538.8 9.5 fusion.79
  548.4 10.1 fusion.125
  558.6 11.6 %fusion.116 = (bf16[1024,768]{1,0:T(8,128)(2,1)S(1)}, f32[1024,768]{1,0:T(8,128)}, bf16[1024,768]{1,0:T(8,128)(2,1)}, f32[1024,768]{1,0:T(8,128)}) fusion(f32[4,768]{1,0:T(4,128)S(1)} %copy-done.31, f32[1024]{0:T(1024)S(1)} %get-tuple-element.386, f32[1024,768]{1,0:T(8,128)S(1)} %copy-done.2, f32[1024]{0:T(1024)S(1)} %copy-done.34, ...), kind=kOutput, calls=%fused_computation.164 | convolution fusion | flops 4043309056 | bytes 27590656 | tf_op jit(solution)/shard_map/dot_general | solution.py:21
  578.0 133.2 %while.31 = (s32[]{:T(128)}, bf16[6,1024,2,64]{1,3,2,0:T(8,128)(2,1)}, bf16[6,1024,2,64]{1,3,2,0:T(8,128)(2,1)}, bf16[6,1024,2,64]{1,3,2,0:T(8,128)(2,1)}, bf16[...) while((s32[]{:T(128)}, ...), condition=%wide.region_25.26_spmd, body=%wide.region_23.25_spmd.sunk | while | flops 1374952448 | bytes 83170504 | solution.py:399
  711.3 6.3 convolution_convert_fusion.5
  729.1 25.5 %collective-permute-done.13 = bf16[768,768]{1,0:T(8,128)(2,1)S(1)} collective-permute-done((bf16[768,768]{1,0:T(8,128)(2,1)}, bf16[768,768]{1,0:T(8,128)(2,1)S(1)}, u32[]{:S(2)}, u32[]{:S(2)}) %collective-permute-start.13) | collective-permute-done | bytes 1179680 | tf_op jit(solution)/shard_map/ppermute | solution.py:65
  754.6 26.1 %collective-permute-done.14 = bf16[768,768]{1,0:T(8,128)(2,1)} collective-permute-done((bf16[768,768]{1,0:T(8,128)(2,1)}, bf16[768,768]{1,0:T(8,128)(2,1)}, u32[]{:S(2)}, u32[]{:S(2)}) %collective-permute-start.14) | collective-permute-done | bytes 1179680 | tf_op jit(solution)/shard_map/ppermute | solution.py:65
  797.0 25.1 %collective-permute-done.10 = bf16[400,768]{1,0:T(8,128)(2,1)S(1)} collective-permute-done((bf16[400,768]{1,0:T(8,128)(2,1)S(1)}, bf16[400,768]{1,0:T(8,128)(2,1)S(1)}, u32[]{:S(2)}, u32[]{:S(2)}) %collective-permute-start.10) | collective-permute-done | bytes 614432 | tf_op jit(solution)/shard_map/ppermute | solution.py:65
  824.8 19.0 %convolution_convert_fusion.1 = bf16[3072,768]{1,0:T(8,128)(2,1)} fusion(bf16[2560,3072]{1,0:T(8,128)(2,1)} %get-tuple-element.379, bf16[2560,768]{1,0:T(8,128)(2,1)} %fusion.87), kind=kOutput, calls=%fused_computation.130 | convolution fusion | flops 12081954816 | bytes 24379392 | tf_op jit(solution)/shard_map/dot_general | solution.py:25
  843.9 18.7 %convolution_convert_fusion.2 = bf16[768,3072]{1,0:T(8,128)(2,1)} fusion(bf16[2560,768]{1,0:T(8,128)(2,1)} %bitcast.81, bf16[2560,3072]{1,0:T(8,128)(2,1)} %fusion.68), kind=kOutput, calls=%fused_computation.131 | convolution fusion | flops 12081954816 | bytes 24379392 | tf_op jit(solution)/shard_map/dot_general | solution.py:25
  863.3 16.0 %all_gather.31 = bf16[128,192]{1,0:T(8,128)(2,1)S(1)} all-gather(bf16[16,192]{1,0:T(8,128)(2,1)S(1)} %reshape.1025), channel_id=1, replica_groups=mesh['dp'=4,'expert'=4,'stream'=2] {'expert','stream'}, dimensions={0}, use_global_device_ids=true | all-gather | bytes 55296 | tf_op jit(solution)/shard_map/all_gather | solution.py:461
  879.4 9.4 fusion.124
  891.7 5.8 multiply_reduce_fusion.2
  901.8 17.4 %all-gather.4 = bf16[4,4,4608]{2,1,0:T(4,128)(2,1)S(1)} all-gather(bf16[1,4,4608]{2,1,0:T(4,128)(2,1)S(1)} %fusion.152), channel_id=1, replica_groups=mesh['dp'=4,'expert'=4,'stream'=2] {'dp'}, dimensions={0}, use_global_device_ids=true | all-gather | bytes 184320 | tf_op jit(solution)/shard_map/all_gather | solution.py:451
  932.7 4.6 multiply_add_fusion
  958.0 68.6 %reduce-scatter.9.cloned.1.call-done = bf16[192,3072]{1,0:T(8,128)(2,1)} async-done(((bf16[768,3072]{1,0:T(8,128)(2,1)}), bf16[192,3072]{1,0:T(8,128)(2,1)}) %reduce-scatter.9.cloned.1.call-update) | async-done | bytes 1179664 | tf_op jit(solution)/shard_map/reduce_scatter | solution.py:320
  (473 shorter events, 400.8 us)
Async XLA Ops:
  7.2 52.0 %copy-start = (bf16[192,4608]{1,0:T(8,128)(2,1)S(1)}, bf16[192,4608]{1,0:T(8,128)(2,1)}, u32[]{:S(2)}) copy-start(bf16[192,4608]{1,0:T(8,128)(2,1)} %param.21) | copy-start | bytes 5308420
  7.2 32.4 %copy-start.60 = (bf16[4,768]{1,0:T(4,128)(2,1)S(1)}, bf16[4,768]{1,0:T(4,128)(2,1)}, u32[]{:S(2)}) copy-start(bf16[4,768]{1,0:T(4,128)(2,1)} %param.18) | copy-start | bytes 18436
  7.2 38.1 %copy-start.36 = (s32[1024,2]{0,1:T(2,128)S(1)}, s32[1024,2]{0,1:T(2,128)}, u32[]{:S(2)}) copy-start(s32[1024,2]{0,1:T(2,128)} %param.20) | copy-start | bytes 24580
  7.2 41.8 %copy-start.3 = (bf16[1024,768]{1,0:T(8,128)(2,1)S(1)}, bf16[1024,768]{1,0:T(8,128)(2,1)}, u32[]{:S(2)}) copy-start(bf16[1024,768]{1,0:T(8,128)(2,1)} %param.17) | copy-start | bytes 4718596
  7.2 84.7 %all-gather.9.cloned.1.call-start = ((), (), s32[]{:S(2)}) async-start(), calls=%async_computation.16 | async-start | bytes 1689600 | tf_op jit(solution)/shard_map/all_gather | solution.py:199
  13.3 308.3 %all-gather.11.cloned.1.call-start = ((), (), s32[]{:S(2)}) async-start(), calls=%async_computation.17 | async-start | bytes 5898240 | tf_op jit(solution)/shard_map/all_gather | solution.py:303
  36.1 30.7 %collective-permute-start = (bf16[4,24,2304]{2,1,0:T(8,128)(2,1)}, bf16[4,24,2304]{2,1,0:T(8,128)(2,1)}, u32[]{:S(2)}, u32[]{:S(2)}) collective-permute-start(bf16[4,24,2304]{2,1,0:T(8,128)(2,1)} %bitcast.31), channel_id=1, source_target_pairs={{0,4},{1,5},{2,6},{3,7},{4,0},{5,1},{6,2},{7,3},{8,12},{9,13},{10,... | collective-permute-start | bytes 1327112 | tf_op jit(solution)/shard_map/ppermute | solution.py:65
  37.6 29.2 %collective-permute-start.1 = (bf16[4,24,2304]{2,1,0:T(8,128)(2,1)}, bf16[4,24,2304]{2,1,0:T(8,128)(2,1)}, u32[]{:S(2)}, u32[]{:S(2)}) collective-permute-start(bf16[4,24,2304]{2,1,0:T(8,128)(2,1)} %bitcast.31), channel_id=1, source_target_pairs={{0,1},{1,0},{2,3},{3,2},{4,5},{5,4},{6,7},{7,6},{8,9},{9,8},{10,11... | collective-permute-start | bytes 1327112 | tf_op jit(solution)/shard_map/ppermute | solution.py:65
  39.1 27.7 %collective-permute-start.2 = (bf16[4,24,2304]{2,1,0:T(8,128)(2,1)}, bf16[4,24,2304]{2,1,0:T(8,128)(2,1)}, u32[]{:S(2)}, u32[]{:S(2)}) collective-permute-start(bf16[4,24,2304]{2,1,0:T(8,128)(2,1)} %bitcast.31), channel_id=1, source_target_pairs={{0,5},{1,4},{2,7},{3,6},{4,1},{5,0},{6,3},{7,2},{8,13},{9,12},{10,... | collective-permute-start | bytes 1327112 | tf_op jit(solution)/shard_map/ppermute | solution.py:65
  40.3 18.9 %all-to-all-start = ((bf16[4,4,192]{2,1,0:T(4,128)(2,1)}), bf16[4,4,192]{2,1,0:T(4,128)(2,1)S(1)}, u32[]{:S(2)}, u32[]{:S(2)}) async-start(bf16[4,4,192]{2,1,0:T(4,128)(2,1)} %bitcast.414), calls=%async_computation | async-start | bytes 16384 | tf_op jit(solution)/shard_map/all_to_all | solution.py:220
  44.6 322.5 %all-gather.13.cloned.1.call-start = ((), (), s32[]{:S(2)}) async-start(), calls=%async_computation.18 | async-start | bytes 5898240 | tf_op jit(solution)/shard_map/all_gather | solution.py:304
  49.3 34.0 %copy-start.43 = (f32[1024]{0:T(1024)}, f32[1024]{0:T(1024)S(1)}, u32[]{:S(2)}) copy-start(f32[1024]{0:T(1024)S(1)} %broadcast_multiply_fusion.5) | copy-start | bytes 12292
  59.2 24.0 %copy-start.50 = (bf16[4,4,192]{2,1,0:T(4,128)(2,1)}, bf16[4,4,192]{2,1,0:T(4,128)(2,1)S(1)}, u32[]{:S(2)}) copy-start(bf16[4,4,192]{2,1,0:T(4,128)(2,1)S(1)} %all-to-all-done) | copy-start | bytes 18436
  60.3 20.0 %all-to-all-start.1 = ((f32[4,4,4608]{2,1,0:T(4,128)}), f32[4,4,4608]{2,1,0:T(4,128)}, u32[]{:S(2)}, u32[]{:S(2)}) async-start(f32[4,4,4608]{2,1,0:T(4,128)} %fusion.130), calls=%async_computation.1 | async-start | bytes 589824 | tf_op jit(solution)/shard_map/all_to_all | solution.py:229
  65.9 19.2 %copy-start.52 = (f32[1024]{0:T(1024)}, f32[1024]{0:T(1024)S(1)}, u32[]{:S(2)}) copy-start(f32[1024]{0:T(1024)S(1)} %add_rsqrt_fusion.1) | copy-start | bytes 12292
  69.6 31.7 %collective-permute-start.3 = (bf16[4,4,24,2304]{3,2,0,1:T(8,128)(2,1)}, bf16[4,4,24,2304]{3,2,0,1:T(8,128)(2,1)}, u32[]{:S(2)}, u32[]{:S(2)}) collective-permute-start(bf16[4,4,24,2304]{3,2,0,1:T(8,128)(2,1)} %pad_maximum_fusion.5), channel_id=1, source_target_pairs={{0,2},{1,3},{2,0},{3,1},{4,6},{5,7},{6,4},{7,5},{8,10},{9,11},{10,... | collective-permute-start | bytes 5308424 | tf_op jit(solution)/shard_map/ppermute | solution.py:65
  81.4 157.2 %copy-start.30 = (f32[4,768]{1,0:T(4,128)}, f32[4,768]{1,0:T(4,128)S(1)}, u32[]{:S(2)}) copy-start(f32[4,768]{1,0:T(4,128)S(1)} %get-tuple-element.373) | copy-start | bytes 36868
  81.4 163.0 %copy-start.25 = (f32[4,768]{1,0:T(4,128)}, f32[4,768]{1,0:T(4,128)S(1)}, u32[]{:S(2)}) copy-start(f32[4,768]{1,0:T(4,128)S(1)} %get-tuple-element.370) | copy-start | bytes 36868
  91.9 38.5 %collective-permute-start.4 = (bf16[4,24,7040]{2,1,0:T(8,128)(2,1)}, bf16[4,24,7040]{2,1,0:T(8,128)(2,1)}, u32[]{:S(2)}, u32[]{:S(2)}) collective-permute-start(bf16[4,24,7040]{2,1,0:T(8,128)(2,1)} %bitcast.479), channel_id=1, source_target_pairs={{0,4},{1,5},{2,6},{3,7},{4,0},{5,1},{6,2},{7,3},{8,12},{9,13},{10,... | collective-permute-start | bytes 4055048 | tf_op jit(solution)/shard_map/ppermute | solution.py:65
  93.2 50.5 %collective-permute-start.5 = (bf16[4,24,7040]{2,1,0:T(8,128)(2,1)}, bf16[4,24,7040]{2,1,0:T(8,128)(2,1)}, u32[]{:S(2)}, u32[]{:S(2)}) collective-permute-start(bf16[4,24,7040]{2,1,0:T(8,128)(2,1)} %bitcast.480), channel_id=1, source_target_pairs={{0,1},{1,0},{2,3},{3,2},{4,5},{5,4},{6,7},{7,6},{8,9},{9,8},{10,11... | collective-permute-start | bytes 4055048 | tf_op jit(solution)/shard_map/ppermute | solution.py:65
  94.8 49.0 %collective-permute-start.6 = (bf16[4,24,7040]{2,1,0:T(8,128)(2,1)}, bf16[4,24,7040]{2,1,0:T(8,128)(2,1)}, u32[]{:S(2)}, u32[]{:S(2)}) collective-permute-start(bf16[4,24,7040]{2,1,0:T(8,128)(2,1)} %bitcast.481), channel_id=1, source_target_pairs={{0,5},{1,4},{2,7},{3,6},{4,1},{5,0},{6,3},{7,2},{8,13},{9,12},{10,... | collective-permute-start | bytes 4055048 | tf_op jit(solution)/shard_map/ppermute | solution.py:65
  149.8 71.3 %collective-permute-start.7 = (bf16[4,4,24,7040]{3,2,0,1:T(8,128)(2,1)}, bf16[4,4,24,7040]{3,2,0,1:T(8,128)(2,1)}, u32[]{:S(2)}, u32[]{:S(2)}) collective-permute-start(bf16[4,4,24,7040]{3,2,0,1:T(8,128)(2,1)} %pad_maximum_fusion), channel_id=1, source_target_pairs={{0,2},{1,3},{2,0},{3,1},{4,6},{5,7},{6,4},{7,5},{8,10},{9,11},{10,... | collective-permute-start | bytes 16220168 | tf_op jit(solution)/shard_map/ppermute | solution.py:65
  245.6 64.1 %copy-start.10 = (bf16[1024,768]{1,0:T(8,128)(2,1)}, bf16[1024,768]{1,0:T(8,128)(2,1)S(1)}, u32[]{:S(2)}) copy-start(bf16[1024,768]{1,0:T(8,128)(2,1)S(1)} %fusion.123) | copy-start | bytes 4718596
  264.6 52.0 %all-to-all-start.2 = ((bf16[8,320,768]{2,1,0:T(8,128)(2,1)}), bf16[8,320,768]{2,1,0:T(8,128)(2,1)}, u32[]{:S(2)}, u32[]{:S(2)}) async-start(bf16[8,320,768]{2,1,0:T(8,128)(2,1)} %bitcast.490), calls=%async_computation.2 | async-start | bytes 7864320 | tf_op jit(solution)/shard_map/all_to_all | solution.py:250
  316.6 50.4 %all-to-all-start.4 = ((bf16[8,320,768]{2,1,0:T(8,128)(2,1)}), bf16[8,320,768]{2,1,0:T(8,128)(2,1)}, u32[]{:S(2)}, u32[]{:S(2)}) async-start(bf16[8,320,768]{2,1,0:T(8,128)(2,1)} %bitcast.487), calls=%async_computation.4 | async-start | bytes 7864320 | tf_op jit(solution)/shard_map/all_to_all | solution.py:250
  386.9 18.7 %all-to-all-start.5 = ((f32[8,1,320]{2,1,0:T(1,128)}), f32[8,1,320]{2,1,0:T(1,128)S(1)}, u32[]{:S(2)}, u32[]{:S(2)}) async-start(f32[8,1,320]{2,1,0:T(1,128)} %all_to_all.41), calls=%async_computation.5 | async-start | bytes 24576 | tf_op jit(solution)/shard_map/all_to_all | solution.py:250
  413.6 9.6 all-to-all-start.6
  422.6 88.5 %collective-permute-start.12 = (bf16[2,2,768,768]{3,2,1,0:T(8,128)(2,1)}, bf16[2,2,768,768]{3,2,1,0:T(8,128)(2,1)}, u32[]{:S(2)}, u32[]{:S(2)}) collective-permute-start(bf16[2,2,768,768]{3,2,1,0:T(8,128)(2,1)} %fusion.103), channel_id=1, source_target_pairs={{0,2},{1,3},{2,0},{3,1},{4,6},{5,7},{6,4},{7,5},{8,10},{9,11},{10,... | collective-permute-start | bytes 14155784 | tf_op jit(solution)/shard_map/ppermute | solution.py:65
  423.1 65.7 %all-to-all-start.3 = ((bf16[8,320,768]{2,1,0:T(8,128)(2,1)}), bf16[8,320,768]{2,1,0:T(8,128)(2,1)}, u32[]{:S(2)}, u32[]{:S(2)}) async-start(bf16[8,320,768]{2,1,0:T(8,128)(2,1)} %bitcast.488), calls=%async_computation.3 | async-start | bytes 7864320 | tf_op jit(solution)/shard_map/all_to_all | solution.py:250
  488.8 50.0 %all-to-all-start.7 = ((bf16[8,320,768]{2,1,0:T(8,128)(2,1)}), bf16[8,320,768]{2,1,0:T(8,128)(2,1)}, u32[]{:S(2)}, u32[]{:S(2)}) async-start(bf16[8,320,768]{2,1,0:T(8,128)(2,1)} %bitcast.489), calls=%async_computation.7 | async-start | bytes 7864320 | tf_op jit(solution)/shard_map/all_to_all | solution.py:250
  493.4 453.2 %reduce-scatter.15.cloned.1.call-start = ((), (), s32[]{:S(2)}) async-start(), calls=%async_computation.20 | async-start | bytes 1474560
  578.0 133.2 %copy-start.20 = (bf16[1024,768]{1,0:T(8,128)(2,1)S(1)}, bf16[1024,768]{1,0:T(8,128)(2,1)}, u32[]{:S(2)}) copy-start(bf16[1024,768]{1,0:T(8,128)(2,1)} %fusion.118) | copy-start | bytes 4718596
  721.7 68.3 %collective-permute-start.8 = (bf16[2,2,400,768]{3,2,1,0:T(8,128)(2,1)}, bf16[2,2,400,768]{3,2,1,0:T(8,128)(2,1)}, u32[]{:S(2)}, u32[]{:S(2)}) collective-permute-start(bf16[2,2,400,768]{3,2,1,0:T(8,128)(2,1)} %dynamic-slice_bitcast_fusion.1), channel_id=1, source_target_pairs={{0,2},{1,3},{2,0},{3,1},{4,6},{5,7},{6,4},{7,5},{8,10},{9,11},{10,... | collective-permute-start | bytes 7372808 | tf_op jit(solution)/shard_map/ppermute | solution.py:65
  725.6 29.0 %collective-permute-start.13 = (bf16[768,768]{1,0:T(8,128)(2,1)}, bf16[768,768]{1,0:T(8,128)(2,1)S(1)}, u32[]{:S(2)}, u32[]{:S(2)}) collective-permute-start(bf16[768,768]{1,0:T(8,128)(2,1)} %get-tuple-element.354), channel_id=1, source_target_pairs={{0,4},{1,5},{2,6},{3,7},{4,0},{5,1},{6,2},{7,3},{8,12},{9,13},{10,... | collective-permute-start | bytes 3538952 | tf_op jit(solution)/shard_map/ppermute | solution.py:65
  727.0 53.6 %collective-permute-start.14 = (bf16[768,768]{1,0:T(8,128)(2,1)}, bf16[768,768]{1,0:T(8,128)(2,1)}, u32[]{:S(2)}, u32[]{:S(2)}) collective-permute-start(bf16[768,768]{1,0:T(8,128)(2,1)} %get-tuple-element.356), channel_id=1, source_target_pairs={{0,1},{1,0},{2,3},{3,2},{4,5},{5,4},{6,7},{7,6},{8,9},{9,8},{10,11... | collective-permute-start | bytes 3538952 | tf_op jit(solution)/shard_map/ppermute | solution.py:65
  727.6 53.0 %collective-permute-start.15 = (bf16[768,768]{1,0:T(8,128)(2,1)}, bf16[768,768]{1,0:T(8,128)(2,1)}, u32[]{:S(2)}, u32[]{:S(2)}) collective-permute-start(bf16[768,768]{1,0:T(8,128)(2,1)} %get-tuple-element.355), channel_id=1, source_target_pairs={{0,5},{1,4},{2,7},{3,6},{4,1},{5,0},{6,3},{7,2},{8,13},{9,12},{10,... | collective-permute-start | bytes 3538952 | tf_op jit(solution)/shard_map/ppermute | solution.py:65
  790.0 160.0 %reduce-scatter.13.cloned.1.call-start = ((), (), s32[]{:S(2)}) async-start(), calls=%async_computation.19 | async-start | bytes 983040
  793.4 28.6 %collective-permute-start.10 = (bf16[400,768]{1,0:T(8,128)(2,1)S(1)}, bf16[400,768]{1,0:T(8,128)(2,1)S(1)}, u32[]{:S(2)}, u32[]{:S(2)}) collective-permute-start(bf16[400,768]{1,0:T(8,128)(2,1)S(1)} %get-tuple-element.363), channel_id=1, source_target_pairs={{0,1},{1,0},{2,3},{3,2},{4,5},{5,4},{6,7},{7,6},{8,9},{9,8},{10,11... | collective-permute-start | bytes 1843208 | tf_op jit(solution)/shard_map/ppermute | solution.py:65
  794.1 27.9 %collective-permute-start.11 = (bf16[400,768]{1,0:T(8,128)(2,1)S(1)}, bf16[400,768]{1,0:T(8,128)(2,1)S(1)}, u32[]{:S(2)}, u32[]{:S(2)}) collective-permute-start(bf16[400,768]{1,0:T(8,128)(2,1)S(1)} %get-tuple-element.362), channel_id=1, source_target_pairs={{0,5},{1,4},{2,7},{3,6},{4,1},{5,0},{6,3},{7,2},{8,13},{9,12},{10,... | collective-permute-start | bytes 1843208 | tf_op jit(solution)/shard_map/ppermute | solution.py:65
  795.6 27.6 %collective-permute-start.9 = (bf16[400,768]{1,0:T(8,128)(2,1)S(1)}, bf16[400,768]{1,0:T(8,128)(2,1)S(1)}, u32[]{:S(2)}, u32[]{:S(2)}) collective-permute-start(bf16[400,768]{1,0:T(8,128)(2,1)S(1)} %get-tuple-element.361), channel_id=1, source_target_pairs={{0,4},{1,5},{2,6},{3,7},{4,0},{5,1},{6,2},{7,3},{8,12},{9,13},{10,... | collective-permute-start | bytes 1843208 | tf_op jit(solution)/shard_map/ppermute | solution.py:65
  824.8 130.4 %reduce-scatter.11.cloned.1.call-start = ((), (), s32[]{:S(2)}) async-start(), calls=%async_computation.15 | async-start | bytes 5898240 | tf_op jit(solution)/shard_map/reduce_scatter | solution.py:323
  843.8 182.8 %reduce-scatter.9.cloned.1.call-start = ((), (), s32[]{:S(2)}) async-start(), calls=%async_computation.14 | async-start | bytes 5898240 | tf_op jit(solution)/shard_map/reduce_scatter | solution.py:320
  862.6 16.7 %copy-start.49 = (f32[1024]{0:T(1024)S(1)}, f32[1024]{0:T(1024)}, u32[]{:S(2)}) copy-start(f32[1024]{0:T(1024)} %copy-done.47) | copy-start | bytes 12292
  862.6 16.7 %copy-start.35 = (f32[1024]{0:T(1024)S(1)}, f32[1024]{0:T(1024)}, u32[]{:S(2)}) copy-start(f32[1024]{0:T(1024)} %copy-done.33) | copy-start | bytes 12292
  862.6 16.7 %copy-start.4 = (bf16[1024,768]{1,0:T(8,128)(2,1)S(1)}, bf16[1024,768]{1,0:T(8,128)(2,1)}, u32[]{:S(2)}) copy-start(bf16[1024,768]{1,0:T(8,128)(2,1)} %param.17) | copy-start | bytes 4718596
  862.6 16.7 %copy-start.40 = (f32[4,768]{1,0:T(4,128)S(1)}, f32[4,768]{1,0:T(4,128)}, u32[]{:S(2)}) copy-start(f32[4,768]{1,0:T(4,128)} %copy-done.39) | copy-start | bytes 36868
  923.4 13.9 %all-to-all-start.8 = ((f32[4,4,192]{2,1,0:T(4,128)}), f32[4,4,192]{2,1,0:T(4,128)}, u32[]{:S(2)}, u32[]{:S(2)}) async-start(f32[4,4,192]{2,1,0:T(4,128)} %reshape.1023), calls=%async_computation.8 | async-start | bytes 32768 | tf_op jit(solution)/shard_map/all_to_all | solution.py:452
  937.3 8.4 all-to-all-start.9
  (61 other events, 389.0 us)
Sparse Core Ops, SparseCore 0:
  13.4 39.1 all-gather.8
  54.2 92.9 all-gather.10
  148.8 88.0 all-gather.12
  790.1 30.5 reduce-scatter.14
  824.9 24.3 reduce-scatter.12
  851.4 87.1 reduce-scatter.10
  940.9 85.7 reduce-scatter.8

commit v2 on v1

v2 whole, which is shorter than its diff:
```python
import functools
import math

import jax
import jax.numpy as jnp
from jax import lax
from jax.experimental import pallas as pl
from jax.experimental.pallas import tpu as pltpu
from jax.sharding import PartitionSpec as P

HEAD = 64
TOP = 2
CAP = 320
SPARE = 16


EPSILON = 1e-06
ROOT = math.sqrt(2.0 / math.pi)
CUBE = 0.044715 * ROOT
MEBI = 1 << 20
WIDE_TYPE = jnp.float32
NARROW_TYPE = jnp.bfloat16


def product_plain_operands(left_side, right_side):
    return jnp.dot(left_side, right_side, preferred_element_type=WIDE_TYPE)


def product_left_operand(left_side, right_side):
    return lax.dot_general(
        left_side, right_side, (((0,), (0,)), ((), ())), preferred_element_type=WIDE_TYPE
    )


def product_right_operand(left_side, right_side):
    return lax.dot_general(
        left_side, right_side, (((1,), (1,)), ((), ())), preferred_element_type=WIDE_TYPE
    )


def contract(left_side, right_side, left_dim, right_dim):
    return lax.dot_general(
        left_side, right_side, (((left_dim,), (right_dim,)), ((), ())), preferred_element_type=WIDE_TYPE
    )

def attend_rows(joined_ref, attended_ref, total_ref, head, rows, columns):
    lanes = slice(head * HEAD, (head + 1) * HEAD)
    queries = joined_ref[0, rows, lanes] * (1.0 / 8.0)
    keys = joined_ref[1, columns, lanes]
    values = joined_ref[2, columns, lanes]
    scores = contract(queries.astype(NARROW_TYPE), keys, 1, 1)
    summit = jnp.max(scores, axis=1, keepdims=True)
    weights = jnp.exp(scores - summit)
    row_total = jnp.sum(weights, axis=1, keepdims=True)
    probabilities = (weights * (1.0 / row_total)).astype(NARROW_TYPE)
    attended_ref[rows, lanes] = contract(probabilities, values, 1, 0).astype(NARROW_TYPE)
    total_ref[rows, lanes] = jnp.broadcast_to(summit + jnp.log(row_total), (scores.shape[0], HEAD))

def attend_kernel(long_ref, joined_ref, attended_ref, total_ref):
    length = joined_ref.shape[1]
    quarter = length // 4
    for whole in (True, False):
        @pl.when((long_ref[0] == 1) == whole)
        def _():
            for head in range(2):
                for part in range(4):
                    rows = slice(part * quarter, (part + 1) * quarter)
                    attend_rows(joined_ref, attended_ref, total_ref, head, rows, slice(None) if whole else rows)

def attend(long_pack, joined):
    three, length, width = joined.shape
    return pl.pallas_call(
        attend_kernel,
        grid=(width // 128,),
        in_specs=[pl.BlockSpec(memory_space=pltpu.SMEM), pl.BlockSpec((3, length, 128), lambda pair: (0, 0, pair))],
        out_specs=[pl.BlockSpec((length, 128), lambda pair: (0, pair))] * 2,
        out_shape=[jax.ShapeDtypeStruct((length, width), NARROW_TYPE), jax.ShapeDtypeStruct((length, width), WIDE_TYPE)],
        compiler_params=pltpu.CompilerParams(vmem_limit_bytes=56 * MEBI),
        name="attend",
    )(long_pack, joined)

def attend_back_rows(joined_ref, total_ref, grad_ref, out_ref, keys_acc, values_acc, head, rows, columns):
    lanes = slice(head * HEAD, (head + 1) * HEAD)
    queries = joined_ref[0, rows, lanes]
    scaled = (queries * (1.0 / 8.0)).astype(NARROW_TYPE)
    keys = joined_ref[1, columns, lanes]
    values = joined_ref[2, columns, lanes]
    grads = grad_ref[rows, lanes]
    scores = contract(scaled, keys, 1, 1)
    probabilities = jnp.exp(scores - total_ref[rows, head * HEAD : head * HEAD + 1])
    grad_probs = contract(grads, values, 1, 1)
    product = probabilities * grad_probs
    centre = jnp.sum(product, axis=1, keepdims=True)
    grad_scores = (product - probabilities * centre).astype(NARROW_TYPE)
    out_ref[0, rows, lanes] = (contract(grad_scores, keys, 1, 0) * (1.0 / 8.0)).astype(NARROW_TYPE)
    keys_acc[lanes, columns] += contract(scaled.T, grad_scores, 1, 0)
    values_acc[lanes, columns] += contract(grads.T, probabilities.astype(NARROW_TYPE), 1, 0)

def attend_back_kernel(long_ref, joined_ref, total_ref, grad_ref, *refs):
    out_ref, keys_acc, values_acc = refs[-3:]
    length = joined_ref.shape[1]
    quarter = length // 4
    keys_acc[...] = jnp.zeros_like(keys_acc)
    values_acc[...] = jnp.zeros_like(values_acc)
    for whole in (True, False):
        @pl.when((long_ref[0] == 1) == whole)
        def _():
            for head in range(2):
                for part in range(4):
                    rows = slice(part * quarter, (part + 1) * quarter)
                    attend_back_rows(joined_ref, total_ref, grad_ref, out_ref, keys_acc, values_acc, head, rows, slice(None) if whole else rows)
    out_ref[1] = keys_acc[...].T.astype(NARROW_TYPE)
    out_ref[2] = values_acc[...].T.astype(NARROW_TYPE)

def attend_back(long_pack, joined, total, grad, after):
    three, length, width = joined.shape
    wide = pl.BlockSpec((3, length, 128), lambda pair: (0, 0, pair))
    flat = pl.BlockSpec((length, 128), lambda pair: (0, pair))
    return pl.pallas_call(
        attend_back_kernel,
        grid=(width // 128,),
        in_specs=[pl.BlockSpec(memory_space=pltpu.SMEM), wide, flat, flat]
        + [pl.BlockSpec(memory_space=pl.ANY)] * len(after),
        out_specs=wide,
        out_shape=jax.ShapeDtypeStruct((3, length, width), NARROW_TYPE),
        scratch_shapes=[pltpu.VMEM((128, length), WIDE_TYPE)] * 2,
        compiler_params=pltpu.CompilerParams(vmem_limit_bytes=56 * MEBI),
        name="attend_back",
    )(long_pack, joined, total, grad, *after)


def gelu_pair(values):
    square = values * values
    half = 0.5 * jnp.tanh(values * (CUBE * square + ROOT)) + 0.5
    result = values * half
    slope = half + result * (1.0 - half) * (6.0 * CUBE * square + 2.0 * ROOT)
    return result, slope


def expert_block(rows, grads, up, down):
    hidden, slope = gelu_pair(contract(rows, up, 1, 0))
    grad_pre = slope * contract(grads, down, 1, 1)
    return hidden.astype(NARROW_TYPE), grad_pre.astype(NARROW_TYPE)


def routed_kernel(
    rows_ref, grad_ref, gate_ref, weight_ref, out_ref, back_ref, dots_ref, hidden_ref, grad_pre_ref
):
    width = rows_ref.shape[1]
    count = weight_ref.shape[1] // (2 * width)
    rows = rows_ref[...]
    cotangent = grad_ref[...].astype(WIDE_TYPE)
    grads = (gate_ref[...] * cotangent).astype(NARROW_TYPE)
    out = jnp.zeros(rows.shape, WIDE_TYPE)
    back = jnp.zeros(rows.shape, WIDE_TYPE)
    for block in range(count):
        units = slice(block * width, (block + 1) * width)
        up = weight_ref[:, units]
        down = weight_ref[:, (count + block) * width : (count + block + 1) * width]
        hidden, grad_pre = expert_block(rows, grads, up, down)
        hidden_ref[:, units] = hidden
        grad_pre_ref[:, units] = grad_pre
        out += contract(hidden, down, 1, 0)
        back += contract(grad_pre, up, 1, 1)
    out = out.astype(NARROW_TYPE).astype(WIDE_TYPE)
    out_ref[...] = (gate_ref[...] * out).astype(NARROW_TYPE)
    back_ref[...] = back.astype(NARROW_TYPE)
    dots_ref[...] = jnp.sum(out * cotangent, axis=1, keepdims=True)


def routed_expert(rows, grads, gates, weights, after, block=512):
    count, width = rows.shape
    hidden = weights.shape[1] // 2
    narrow = jax.ShapeDtypeStruct((count, width), NARROW_TYPE)
    units = jax.ShapeDtypeStruct((count, hidden), NARROW_TYPE)
    return stepped(
        routed_kernel,
        count // block,
        (rows, grads, gates, weights),
        [row_block(block, width), row_block(block, width), row_block(block, 1), whole_block(weights)],
        [row_block(block, width), row_block(block, width), row_block(block, 1)]
        + [row_block(block, hidden)] * 2,
        [narrow, narrow, jax.ShapeDtypeStruct((count, 1), WIDE_TYPE), units, units],
        after,
        "routed_expert",
    )


def sums_kernel(
    steps, rows_ref, grad_ref, gate_ref, hidden_ref, grad_pre_ref, sums_ref, totals
):
    step = pl.program_id(0)
    width = rows_ref.shape[1]
    count = totals.shape[0] // 2

    @pl.when(step == 0)
    def _():
        totals[...] = jnp.zeros_like(totals)

    @pl.when(step < steps)
    def _():
        turned = rows_ref[...].T
        grads = (gate_ref[...] * grad_ref[...].astype(WIDE_TYPE)).astype(NARROW_TYPE)
        for block in range(count):
            units = slice(block * width, (block + 1) * width)
            totals[block] += contract(turned, grad_pre_ref[:, units], 1, 0)
            totals[count + block] += contract(hidden_ref[:, units], grads, 0, 0)

    @pl.when(step >= steps)
    def _():
        sums_ref[...] = totals[jnp.maximum(step - steps, 0)].astype(NARROW_TYPE)


def routed_sums(rows, grads, gates, hidden, grad_pre, side, after, block=512):
    total_rows, width = rows.shape
    half = hidden.shape[1] // 2
    count = half // width
    steps = total_rows // block

    def spec(columns, place):
        return pl.BlockSpec((block, columns), lambda step: (jnp.minimum(step, steps - 1), place))

    square = (width, width)
    return stepped(
        functools.partial(sums_kernel, steps),
        steps + 2 * count,
        (rows, grads, gates, hidden, grad_pre),
        [spec(width, 0), spec(width, 0), spec(1, 0), spec(half, side), spec(half, side)],
        pl.BlockSpec(square, lambda step: (0, jnp.maximum(step - steps, 0))),
        jax.ShapeDtypeStruct((width, 2 * half), NARROW_TYPE),
        after,
        "routed_sums",
        scratch_shapes=[pltpu.VMEM((2 * count,) + square, WIDE_TYPE)],
    )


def part_of_step(core, place):
    chip = lax.rem(place, 4)
    owner = jnp.where(place < 4, core, 1 - core)
    return 4 * (chip // 2) + 2 * owner + lax.rem(chip, 2)


def shared_kernel(
    local, steps, core_ref, rows_ref, grad_ref, up_ref, down_ref, out_ref, back_ref, kept_ref, sent_ref, totals
):
    step = pl.program_id(0)
    width = rows_ref.shape[1]
    count = totals.shape[0] // 2

    @pl.when(step == 0)
    def _():
        totals[...] = jnp.zeros_like(totals)

    @pl.when(step < steps)
    def _():
        rows, grads = rows_ref[...], grad_ref[...]
        turned = grads.T
        out = jnp.zeros(rows.shape, WIDE_TYPE)
        back = jnp.zeros(rows.shape, WIDE_TYPE)
        for block in range(count):
            units = slice(block * width, (block + 1) * width)
            up, down = up_ref[:, units], down_ref[:, units]
            hidden, grad_pre = expert_block(rows, grads, up, down)
            out += contract(hidden, down, 1, 0)
            back += contract(grad_pre, up, 1, 1)
            totals[block] += contract(grad_pre, rows, 0, 0)
            totals[count + block] += contract(turned, hidden, 1, 0)
        out_ref[...] = out
        back_ref[...] = back

    units = count * width // 8
    features = width // 8
    part = part_of_step(core_ref[0], jnp.maximum(step - steps, 0))

    def write(part_ref):
        for piece in range(units // local):
            number = part * (units // local) + piece
            start = pl.multiple_of((number // count) * local, 8)
            part_ref[0, piece * local : (piece + 1) * local] = totals[
                lax.rem(number, count), pl.ds(start, local)
            ].astype(NARROW_TYPE)
        for block in range(count):
            start = units + block * features
            part_ref[0, start : start + features] = totals[
                count + block, pl.ds(pl.multiple_of(part * features, 8), features)
            ].astype(NARROW_TYPE)

    @pl.when(jnp.logical_and(step >= steps, step < steps + 4))
    def _():
        write(kept_ref)

    @pl.when(step >= steps + 4)
    def _():
        write(sent_ref)


def part_specs(steps, rows, width):
    return [
        pl.BlockSpec((1, rows, width), lambda step, *_: (jnp.clip(step - steps, 0, 3), 0, 0)),
        pl.BlockSpec((1, rows, width), lambda step, *_: (jnp.clip(step - steps - 4, 0, 3), 0, 0)),
    ]


def own_core():
    return ((lax.axis_index(PLANE) // 2) % 2).reshape(1).astype(jnp.int32)


def shared_expert(rows, grads, weights, local, after, row_block=512):
    total_rows, width = rows.shape
    steps = total_rows // row_block
    count = 4
    row_spec = pl.BlockSpec((row_block, width), lambda step, core: (jnp.minimum(step, steps - 1), 0))

    def held(place):
        return pl.BlockSpec(
            (width, count * width), lambda step, core: (0, place), pipeline_mode=pl.Buffered(1)
        )

    def kernel(*refs):
        shared_kernel(local, steps, *refs[:5], *refs[5 + len(after) :])

    wide = jax.ShapeDtypeStruct((total_rows, width), WIDE_TYPE)
    return pl.pallas_call(
        kernel,
        grid_spec=pltpu.PrefetchScalarGridSpec(
            num_scalar_prefetch=1,
            grid=(steps + 8,),
            in_specs=[row_spec, row_spec, held(0), held(1)] + [ANYWHERE] * len(after),
            out_specs=[row_spec, row_spec] + part_specs(steps, width, width),
            scratch_shapes=[pltpu.VMEM((2 * count, width, width), WIDE_TYPE)],
        ),
        out_shape=[wide, wide] + [jax.ShapeDtypeStruct((4, width, width), NARROW_TYPE)] * 2,
        compiler_params=pltpu.CompilerParams(vmem_limit_bytes=60 * MEBI),
        name="shared_expert",
    )(own_core(), rows, grads, weights, weights, *after)


PLANE = ("expert", "stream")
CORE, SIDES = 2, (4, 1, 5)


def flip(value, mask):
    count = lax.axis_size(PLANE)
    return lax.ppermute(value, PLANE, [(index, index ^ mask) for index in range(count)])


def together(*values):
    return lax.optimization_barrier(values)


ANYWHERE = pl.BlockSpec(memory_space=pl.ANY)


def whole_block(operand):
    rank = len(operand.shape)
    return pl.BlockSpec(operand.shape, lambda *_: (0,) * rank, pipeline_mode=pl.Buffered(1))


def row_block(rows, columns):
    return pl.BlockSpec((rows, columns), lambda step, *_: (step, 0))


def column_block(operand, columns, place):
    return pl.BlockSpec(
        (operand.shape[0], columns), lambda step, *_: (0, place), pipeline_mode=pl.Buffered(1)
    )


def stepped(kernel, steps, operands, in_specs, out_specs, out_shape, after, name, **extra):
    given = len(operands)

    def body(*refs):
        kernel(*refs[:given], *refs[given + len(after) :])

    return pl.pallas_call(
        body,
        grid=(steps,),
        in_specs=list(in_specs) + [ANYWHERE] * len(after),
        out_specs=out_specs,
        out_shape=out_shape,
        compiler_params=pltpu.CompilerParams(vmem_limit_bytes=58 * MEBI),
        name=name,
        **extra,
    )(*operands, *after)


def depth_stack(piece):
    parts = jnp.broadcast_to(piece[None], (lax.axis_size("dp"),) + piece.shape)
    return lax.all_to_all(parts, "dp", split_axis=0, concat_axis=0, tiled=True)


def stack_kernel(*refs):
    for place, ref in enumerate(refs[:-1]):
        refs[-1][place] = ref[...]


def place_kernel(order_ref, near_ref, far_ref, out_ref):
    for place in range(4):
        chip = order_ref[place]
        first = 4 * (chip // 2) + lax.rem(chip, 2)
        out_ref[0, first + 2 * order_ref[4]] = near_ref[place, 0]
        out_ref[0, first + 2 * (1 - order_ref[4])] = far_ref[place, 0]


def side_gather(stacked):
    return [stacked] + [flip(stacked, mask) for mask in SIDES]


def near_slices(sides, after=()):
    depth, rows, columns = sides[0].shape
    slice_shape = (1, rows, columns)
    return stepped(
        stack_kernel,
        depth,
        sides,
        [pl.BlockSpec(slice_shape, lambda part: (part, 0, 0))] * 4,
        pl.BlockSpec((4,) + slice_shape, lambda part: (0, part, 0, 0)),
        jax.ShapeDtypeStruct((4, depth, rows, columns), sides[0].dtype),
        after,
        "stack_sides",
    )


def plane_gather(near):
    depth, rows, columns = near.shape[1:]
    slice_shape = (1, rows, columns)
    me = lax.axis_index(PLANE)
    chip = 2 * (me // 4) + me % 2
    far = flip(near, CORE)
    order = jnp.stack([chip, chip ^ 2, chip ^ 1, chip ^ 3, (me // 2) % 2]).astype(jnp.int32)
    source = pl.BlockSpec((4,) + slice_shape, lambda part, order: (0, part, 0, 0))
    placed = pl.pallas_call(
        place_kernel,
        grid_spec=pltpu.PrefetchScalarGridSpec(
            num_scalar_prefetch=1,
            grid=(depth,),
            in_specs=[source] * 2,
            out_specs=pl.BlockSpec((1, 8, rows, columns), lambda part, order: (part, 0, 0, 0)),
        ),
        out_shape=jax.ShapeDtypeStruct((depth, 8, rows, columns), near.dtype),
        compiler_params=pltpu.CompilerParams(vmem_limit_bytes=40 * MEBI),
        name="place_slices",
    )(order, near, far)
    return placed.reshape(depth * 8 * rows, columns)


def pair_kernel(place_ref, kept_ref, other_ref, *refs):
    own_ref, *side_refs = refs[-4:]
    place = place_ref[0]
    own_ref[...] = kept_ref[place].astype(WIDE_TYPE) + other_ref[place].astype(WIDE_TYPE)
    for side_ref, other in zip(side_refs, (2, 1, 3)):
        chip = place ^ other
        total = kept_ref[chip].astype(WIDE_TYPE) + other_ref[chip].astype(WIDE_TYPE)
        side_ref[...] = total.astype(NARROW_TYPE)


def finish_kernel(own_ref, *refs):
    total = own_ref[...]
    for ref in refs[:3]:
        total += ref[...].astype(WIDE_TYPE)
    refs[-1][...] = total.T.astype(NARROW_TYPE)


def pair_sum(kept, other, after=(), columns=256):
    me = lax.axis_index(PLANE)
    place = (2 * (me // 4) + me % 2).reshape(1).astype(jnp.int32)
    rows, width = kept.shape[1:]
    stack = pl.BlockSpec((4, rows, columns), lambda step, place: (0, 0, step))
    flat = pl.BlockSpec((rows, columns), lambda step, *_: (0, step))
    narrow = jax.ShapeDtypeStruct((rows, width), NARROW_TYPE)
    return pl.pallas_call(
        pair_kernel,
        grid_spec=pltpu.PrefetchScalarGridSpec(
            num_scalar_prefetch=1,
            grid=(width // columns,),
            in_specs=[stack, stack] + [ANYWHERE] * len(after),
            out_specs=[flat] * 4,
        ),
        out_shape=[jax.ShapeDtypeStruct((rows, width), WIDE_TYPE)] + [narrow] * 3,
        compiler_params=pltpu.CompilerParams(vmem_limit_bytes=40 * MEBI),
        name="pair_sum",
    )(place, kept, other, *after)


def side_sum(own, *sides, after=(), columns=256):
    rows, width = own.shape
    flat = pl.BlockSpec((rows, columns), lambda step, *_: (0, step))
    sides = [flip(side, mask) for side, mask in zip(sides, SIDES)]
    return pl.pallas_call(
        finish_kernel,
        grid=(width // columns,),
        in_specs=[flat] * 4 + [ANYWHERE] * len(after),
        out_specs=pl.BlockSpec((columns, rows), lambda step: (step, 0)),
        out_shape=jax.ShapeDtypeStruct((width, rows), NARROW_TYPE),
        compiler_params=pltpu.CompilerParams(vmem_limit_bytes=40 * MEBI),
        name="side_sum",
    )(own, *sides, *after)


def last_kernel(
    core_ref, joined_ref, first_ref, grad_ref, attended_ref, logits_ref, second_ref, kept_ref, sent_ref, totals, router
):
    step = pl.program_id(0)
    width = first_ref.shape[1]

    @pl.when(step < 3)
    def _():
        start = pl.multiple_of(step * width, 8)
        totals[pl.ds(start, width)] = contract(joined_ref[0], first_ref[...], 0, 0)

    @pl.when(step == 3)
    def _():
        totals[3 * width :] = contract(grad_ref[...], attended_ref[...], 0, 0)
        router[...] = contract(logits_ref[...], second_ref[...], 0, 0)

    part = part_of_step(core_ref[0], jnp.maximum(step - 4, 0))

    def write(part_ref):
        place = 0
        for start, rows in ((0, 3 * width // 8), (3 * width, width // 8)):
            first = pl.multiple_of(start + part * rows, 8)
            part_ref[0, place : place + rows] = totals[pl.ds(first, rows)].astype(NARROW_TYPE)
            place += rows
        number = lax.broadcasted_iota(jnp.int32, router.shape, 0)
        column = jnp.sum(jnp.where(number == part, router[...], 0.0), axis=0, keepdims=True)
        tail = part_ref.shape[1] - place
        row = lax.broadcasted_iota(jnp.int32, (tail, width), 0)
        part_ref[0, place:] = jnp.where(row == 0, column, 0.0).astype(NARROW_TYPE)

    @pl.when(jnp.logical_and(step >= 4, step < 8))
    def _():
        write(kept_ref)

    @pl.when(step >= 8)
    def _():
        write(sent_ref)


def last_gradients(grad_joined, first_in, grad_attention, attended, grad_logits, second_in):
    count, width = first_in.shape
    rows = width // 2 + 16
    flat = pl.BlockSpec((count, width), lambda step, core: (0, 0))
    thin = pl.BlockSpec((count, grad_logits.shape[1]), lambda step, core: (0, 0))
    return pl.pallas_call(
        last_kernel,
        grid_spec=pltpu.PrefetchScalarGridSpec(
            num_scalar_prefetch=1,
            grid=(12,),
            in_specs=[
                pl.BlockSpec((1, count, width), lambda step, core: (jnp.minimum(step, 2), 0, 0)),
                flat,
                flat,
                flat,
                thin,
                flat,
            ],
            out_specs=part_specs(4, rows, width),
            scratch_shapes=[
                pltpu.VMEM((4 * width, width), WIDE_TYPE),
                pltpu.VMEM((grad_logits.shape[1], width), WIDE_TYPE),
            ],
        ),
        out_shape=[jax.ShapeDtypeStruct((4, rows, width), NARROW_TYPE)] * 2,
        compiler_params=pltpu.CompilerParams(vmem_limit_bytes=56 * MEBI),
        name="last_gradients",
    )(own_core(), grad_joined, first_in, grad_attention, attended, grad_logits, second_in)


def depth_shift(value, shift):
    depth = lax.axis_size("dp")
    return lax.ppermute(value, "dp", [(index, (index + shift) % depth) for index in range(depth)])


def depth_scatter(parts):
    depth = lax.axis_size("dp")
    blocks = parts.reshape(depth, parts.shape[0] // depth, parts.shape[1])
    if depth > 8:
        blocks = lax.all_to_all(blocks, "dp", split_axis=0, concat_axis=0, tiled=True)
        return jnp.sum(blocks.astype(WIDE_TYPE), axis=0)
    me = lax.axis_index("dp")
    total = lax.dynamic_index_in_dim(blocks, me, 0, keepdims=False).astype(WIDE_TYPE)
    for shift in range(1, depth):
        part = lax.dynamic_index_in_dim(blocks, (me + shift) % depth, 0, keepdims=False)
        total = total + depth_shift(part, shift).astype(WIDE_TYPE)
    return total


def first_payload_kernel(place_ref, qkv_ref, out_ref, router_ref, cond_ref, payload_ref):
    del place_ref
    depth, rows, columns = payload_ref.shape
    slots = cond_ref.shape[0]
    local = cond_ref.shape[1] // depth
    qkv_end = qkv_ref.shape[1]
    out_end = qkv_end + out_ref.shape[1]
    router_end = out_end + 128
    silu = cond_ref[...].astype(WIDE_TYPE)
    silu = silu * jax.nn.sigmoid(silu)
    router = jnp.concatenate(
        [router_ref[...].astype(WIDE_TYPE), jnp.zeros((rows, 128 - router_ref.shape[1]), WIDE_TYPE)],
        axis=1,
    ).astype(NARROW_TYPE)
    payload_ref[...] = jnp.zeros_like(payload_ref)
    for part in range(depth):
        payload_ref[part, :, :qkv_end] = qkv_ref[...]
        payload_ref[part, :, qkv_end:out_end] = out_ref[...]
        payload_ref[part, :, out_end:router_end] = router
        tail = jnp.concatenate(
            [silu[:, part * local : (part + 1) * local], jnp.zeros((slots, columns - router_end - local), WIDE_TYPE)],
            axis=1,
        )
        tail = jnp.concatenate([tail, jnp.zeros((rows - slots, columns - router_end), WIDE_TYPE)], axis=0)
        payload_ref[part, :, router_end:] = tail.astype(NARROW_TYPE)


def first_payload(qkv, out, router, cond, depth, rows):
    place = lax.axis_index(PLANE).reshape(1).astype(jnp.int32)
    local = cond.shape[1] // depth
    columns = qkv.shape[1] + out.shape[1] + 128 + local + -local % 128

    def slice_of(operand):
        return pl.BlockSpec((rows, operand.shape[1]), lambda step, place: (place[0], 0))

    return pl.pallas_call(
        first_payload_kernel,
        grid_spec=pltpu.PrefetchScalarGridSpec(
            num_scalar_prefetch=1,
            grid=(1,),
            in_specs=[slice_of(qkv), slice_of(out), slice_of(router), whole_block(cond)],
            out_specs=pl.BlockSpec((depth, rows, columns), lambda step, place: (0, 0, 0)),
        ),
        out_shape=jax.ShapeDtypeStruct((depth, rows, columns), NARROW_TYPE),
        name="first_payload",
    )(place, qkv, out, router, cond)


def rest_payload_kernel(local, place_ref, up_ref, down_ref, *refs):
    del place_ref
    payload_ref = refs[-1]
    hidden = up_ref.shape[1]
    width = down_ref.shape[2]
    depth = hidden // (4 * local)
    for block in range(4):
        for part in range(depth):
            target = (block * depth + part) * local
            source = (part * 4 + block) * local
            payload_ref[:, target : target + local] = up_ref[:, source : source + local]
        start = hidden + block * width
        payload_ref[:, start : start + width] = down_ref[block]


def rest_payload(up, down, rows, after):
    place = lax.axis_index(PLANE).reshape(1).astype(jnp.int32)
    local, hidden = up.shape
    width = down.shape[1]
    shape = (rows, hidden + 4 * width)
    return pl.pallas_call(
        functools.partial(rest_payload_kernel, local),
        grid_spec=pltpu.PrefetchScalarGridSpec(
            num_scalar_prefetch=1,
            grid=(1,),
            in_specs=[
                pl.BlockSpec((rows, hidden), lambda step, place: (place[0], 0)),
                pl.BlockSpec((4, rows, width), lambda step, place: (0, place[0], 0)),
            ]
            + [ANYWHERE] * len(after),
            out_specs=pl.BlockSpec(shape, lambda step, place: (0, 0)),
        ),
        out_shape=jax.ShapeDtypeStruct(shape, NARROW_TYPE),
        name="rest_payload",
    )(place, up, down.reshape(4, local, width), *after)


def expert_payload_kernel(up_ref, down_ref, *refs):
    payload_ref = refs[-1]
    local, hidden = up_ref.shape
    width = down_ref.shape[1]
    depth = hidden // (4 * local)
    for block in range(4):
        for part in range(depth):
            target = (block * depth + part) * local
            source = (part * 4 + block) * local
            payload_ref[:, target : target + local] = up_ref[:, source : source + local]
        start = hidden + block * width
        payload_ref[:, start : start + width] = down_ref[block * local : (block + 1) * local, :]


def expert_payload(up, down, after):
    local, hidden = up.shape
    whole = pl.BlockSpec(memory_space=pltpu.VMEM)
    return pl.pallas_call(
        expert_payload_kernel,
        in_specs=[whole, whole] + [ANYWHERE] * len(after),
        out_specs=whole,
        out_shape=jax.ShapeDtypeStruct((local, hidden + 4 * down.shape[1]), up.dtype),
        name="expert_payload",
    )(up, down, *after)


def normalize_rows(values):
    centre = values - jnp.mean(values, axis=-1, keepdims=True)
    spread = jnp.mean(centre * centre, axis=-1, keepdims=True)
    reciprocal = lax.rsqrt(spread + EPSILON)
    return centre * reciprocal, reciprocal


def normalize_rows_back(gradient, normed, reciprocal):
    mean = jnp.mean(gradient, axis=-1, keepdims=True)
    along = jnp.mean(gradient * normed, axis=-1, keepdims=True)
    return reciprocal * (gradient - mean - normed * along)


def pick_slots(first, count, places_ref):
    patches = places_ref.shape[1]
    slot = first + lax.broadcasted_iota(jnp.int32, (count, patches), 0)
    return jnp.logical_or(slot == places_ref[0:1, :], slot == places_ref[1:2, :])


def one(mask):
    return jnp.where(mask, 1.0, 0.0).astype(NARROW_TYPE)


def mixture_kernel(grad_ref, mods_ref, places_ref, silu_ref, shared_ref, out_ref):
    step = pl.program_id(0)
    quarter = grad_ref.shape[0] // 4

    @pl.when(step == 0)
    def _():
        for part in range(4):
            rows = slice(part * quarter, (part + 1) * quarter)
            gradient = grad_ref[rows, :].astype(WIDE_TYPE) * mods_ref[part, 5:6, :]
            shared_ref[rows, :] = gradient.astype(NARROW_TYPE)

    taken = one(pick_slots(step * CAP, CAP, places_ref))
    out_ref[0, :CAP] = contract(taken, shared_ref[...], 1, 0).astype(NARROW_TYPE)
    out_ref[0, CAP:] = jnp.zeros((SPARE, out_ref.shape[2]), NARROW_TYPE)
    out_ref[0, CAP:, : silu_ref.shape[1]] = silu_ref[...]


def slot_block(width):
    return pl.BlockSpec((1, CAP + SPARE, width), lambda step: (step, 0, 0))


def spread_mixture(out_grad, mods, places, silu, after):
    count, width = out_grad.shape
    return stepped(
        mixture_kernel,
        8,
        (out_grad, mods, places, silu),
        [whole_block(operand) for operand in (out_grad, mods, places, silu)],
        [pl.BlockSpec((count, width), lambda step: (0, 0)), slot_block(width)],
        [
            jax.ShapeDtypeStruct((count, width), NARROW_TYPE),
            jax.ShapeDtypeStruct((8, CAP + SPARE, width), NARROW_TYPE),
        ],
        after,
        "spread_mixture",
    )


def first_kernel(patch_ref, mods_ref, weight_ref, first_ref, joined_ref):
    normed, _ = normalize_rows(patch_ref[...].astype(WIDE_TYPE))
    first = (normed * (1.0 + mods_ref[0, 1:2, :]) + mods_ref[0, 0:1, :]).astype(NARROW_TYPE)
    first_ref[...] = first
    width = first.shape[1]
    for part in range(3):
        columns = slice(part * width, (part + 1) * width)
        joined_ref[part] = contract(first, weight_ref[:, columns], 1, 0).astype(NARROW_TYPE)


def mods_block(mods):
    return pl.BlockSpec((1,) + mods.shape[1:], lambda step, *_: (step, 0, 0))


def first_half(patches, mods, weights, after):
    count, width = patches.shape
    quarter = count // 4
    rows = row_block(quarter, width)
    return stepped(
        first_kernel,
        4,
        (patches, mods, weights),
        [rows, mods_block(mods), column_block(weights, 3 * width, 0)],
        [rows, pl.BlockSpec((3, quarter, width), lambda step: (0, step, 0))],
        [
            jax.ShapeDtypeStruct((count, width), NARROW_TYPE),
            jax.ShapeDtypeStruct((3, count, width), NARROW_TYPE),
        ],
        after,
        "first_half",
    )


def second_kernel(
    attended_ref, patch_ref, mods_ref, routes_ref, out_ref, router_ref, attention_ref, middle_ref, second_ref, gates_ref, gate_rows_ref
):
    attention = contract(attended_ref[...], out_ref[...], 1, 0)
    attention_ref[...] = attention
    middle = patch_ref[...].astype(WIDE_TYPE) + mods_ref[0, 2:3, :] * attention
    middle_ref[...] = middle
    normed, _ = normalize_rows(middle)
    second = (normed * (1.0 + mods_ref[0, 4:5, :]) + mods_ref[0, 3:4, :]).astype(NARROW_TYPE)
    second_ref[...] = second
    logits = contract(second, router_ref[...], 1, 0)
    lane = lax.broadcasted_iota(jnp.int32, logits.shape, 1)
    picked = [
        jnp.sum(jnp.where(lane == routes_ref[:, k : k + 1], logits, 0.0), axis=1, keepdims=True)
        for k in range(TOP)
    ]
    summit = jnp.maximum(picked[0], picked[1])
    weights = [jnp.exp(value - summit) for value in picked]
    total = weights[0] + weights[1]
    gates = [weight / total for weight in weights]
    gates_ref[...] = jnp.concatenate(gates, axis=1)
    wide = jnp.where(lane == 0, gates[0], jnp.where(lane == 1, gates[1], 0.0))
    gate_rows_ref[...] = wide.T[0:TOP, :]


def second_half(attended, patches, mods, routes, weights, after):
    count, width = patches.shape
    quarter = count // 4
    rows = row_block(quarter, width)
    pair = row_block(quarter, TOP)
    wide = jax.ShapeDtypeStruct((count, width), WIDE_TYPE)
    return stepped(
        second_kernel,
        4,
        (attended, patches, mods, routes, weights, weights),
        [
            rows,
            rows,
            mods_block(mods),
            pair,
            column_block(weights, width, 3),
            column_block(weights, 128, 4 * width // 128),
        ],
        [rows, rows, rows, pair, pl.BlockSpec((TOP, quarter), lambda step: (0, step))],
        [
            wide,
            wide,
            jax.ShapeDtypeStruct((count, width), NARROW_TYPE),
            jax.ShapeDtypeStruct((count, TOP), WIDE_TYPE),
            jax.ShapeDtypeStruct((TOP, count), WIDE_TYPE),
        ],
        after,
        "second_half",
    )


def spread_kernel(second_ref, places_ref, gates_ref, rows_ref):
    slots = pick_slots(pl.program_id(0) * CAP, CAP, places_ref)
    rows_ref[0, :CAP] = contract(one(slots), second_ref[...], 1, 0).astype(NARROW_TYPE)
    slot = pl.program_id(0) * CAP + lax.broadcasted_iota(jnp.int32, slots.shape, 0)
    total = jnp.where(slot == places_ref[0:1, :], gates_ref[0:1, :], 0.0)
    total += jnp.where(slot == places_ref[1:2, :], gates_ref[1:2, :], 0.0)
    column = jnp.sum(total, axis=1, keepdims=True)
    gates = jnp.broadcast_to(column, (CAP, 128)).T[0:SPARE, :]
    row = lax.broadcasted_iota(jnp.int32, gates.shape, 0)
    terms = jnp.zeros(gates.shape, WIDE_TYPE)
    for number in range(3):
        term = gates.astype(NARROW_TYPE).astype(WIDE_TYPE)
        terms = jnp.where(row == number, term, terms)
        gates = gates - term
    rows_ref[0, CAP:] = jnp.zeros((SPARE, rows_ref.shape[2]), NARROW_TYPE)
    rows_ref[0, CAP:, :CAP] = terms.astype(NARROW_TYPE)


def spread_second(second_in, places, gates, after):
    width = second_in.shape[1]
    operands = (second_in, places, gates)
    return stepped(
        spread_kernel,
        8,
        operands,
        [whole_block(operand) for operand in operands],
        slot_block(width),
        jax.ShapeDtypeStruct((8, CAP + SPARE, width), NARROW_TYPE),
        after,
        "spread_second",
    )


def middle_kernel(
    back_ref,
    dots_ref,
    columns_ref,
    routes_ref,
    gates_ref,
    shared_ref,
    middle_ref,
    attention_ref,
    mods_ref,
    grad_ref,
    out_ref,
    router_ref,
    grad_middle_ref,
    grad_attention_ref,
    grad_attended_ref,
    grad_logits_ref,
    sums_ref,
):
    quarter, width = middle_ref.shape
    slot = lax.broadcasted_iota(jnp.int32, (quarter, back_ref.shape[0]), 1)
    takes = [slot == columns_ref[:, k : k + 1] for k in range(TOP)]
    collected = contract(one(jnp.logical_or(*takes)), back_ref[...], 1, 0)
    gates = [gates_ref[:, k : k + 1] for k in range(TOP)]
    grad_gate = [
        jnp.sum(jnp.where(take, dots_ref[...], 0.0), axis=1, keepdims=True) for take in takes
    ]
    centre = gates[0] * grad_gate[0] + gates[1] * grad_gate[1]
    lane = lax.broadcasted_iota(jnp.int32, grad_logits_ref.shape, 1)
    grad_logits = jnp.zeros(grad_logits_ref.shape, WIDE_TYPE)
    for k in range(TOP):
        picked = gates[k] * (grad_gate[k] - centre)
        grad_logits += jnp.where(lane == routes_ref[:, k : k + 1], picked, 0.0)
    grad_logits = grad_logits.astype(NARROW_TYPE)
    grad_logits_ref[...] = grad_logits
    grad_second = shared_ref[...] + contract(grad_logits, router_ref[...], 1, 1) + collected
    normed, reciprocal = normalize_rows(middle_ref[...])
    grad_middle = grad_ref[...].astype(WIDE_TYPE) + normalize_rows_back(
        grad_second * (1.0 + mods_ref[0, 4:5, :]), normed, reciprocal
    )
    grad_middle_ref[...] = grad_middle
    grad_attention = (grad_middle * mods_ref[0, 2:3, :]).astype(NARROW_TYPE)
    grad_attention_ref[...] = grad_attention
    grad_attended_ref[...] = contract(grad_attention, out_ref[...], 1, 1).astype(NARROW_TYPE)
    sums_ref[0] = jnp.concatenate(
        [
            jnp.sum(grad_middle * attention_ref[...], axis=0, keepdims=True),
            jnp.sum(grad_second, axis=0, keepdims=True),
            jnp.sum(grad_second * normed, axis=0, keepdims=True),
        ],
        axis=0,
    )


def sums_block(count, width):
    return pl.BlockSpec((1, count, width), lambda step: (step, 0, 0))


def middle_back(
    back, dots, columns, routes, gates, grad_shared, middle, attention, mods, out_grad, weights, after
):
    count, width = middle.shape
    quarter = count // 4
    rows, pair, lanes = row_block(quarter, width), row_block(quarter, TOP), row_block(quarter, 128)
    narrow = jax.ShapeDtypeStruct((count, width), NARROW_TYPE)
    return stepped(
        middle_kernel,
        4,
        (back, dots, columns, routes, gates, grad_shared, middle, attention, mods, out_grad, weights, weights),
        [whole_block(back), whole_block(dots), pair, pair, pair, rows, rows, rows]
        + [mods_block(mods), rows]
        + [column_block(weights, width, 3), column_block(weights, 128, 4 * width // 128)],
        [rows, rows, rows, lanes, sums_block(3, width)],
        [
            jax.ShapeDtypeStruct((count, width), WIDE_TYPE),
            narrow,
            narrow,
            jax.ShapeDtypeStruct((count, 128), NARROW_TYPE),
            jax.ShapeDtypeStruct((4, 3, width), WIDE_TYPE),
        ],
        after,
        "middle_back",
    )


def output_kernel(
    result_ref, columns_ref, shared_ref, middle_ref, mods_ref, grad_ref, out_ref, sums_ref
):
    quarter = middle_ref.shape[0]
    slot = lax.broadcasted_iota(jnp.int32, (quarter, result_ref.shape[0]), 1)
    takes = [slot == columns_ref[:, k : k + 1] for k in range(TOP)]
    mixture = shared_ref[...] + contract(one(jnp.logical_or(*takes)), result_ref[...], 1, 0)
    out_ref[...] = (middle_ref[...] + mods_ref[0, 5:6, :] * mixture).astype(NARROW_TYPE)
    sums_ref[0] = jnp.sum(grad_ref[...].astype(WIDE_TYPE) * mixture, axis=0, keepdims=True)


def block_output(result, columns, shared, middle, mods, out_grad, after):
    count, width = middle.shape
    quarter = count // 4
    rows, pair = row_block(quarter, width), row_block(quarter, TOP)
    return stepped(
        output_kernel,
        4,
        (result, columns, shared, middle, mods, out_grad),
        [whole_block(result), pair, rows, rows, mods_block(mods), rows],
        [rows, sums_block(1, width)],
        [
            jax.ShapeDtypeStruct((count, width), NARROW_TYPE),
            jax.ShapeDtypeStruct((4, 1, width), WIDE_TYPE),
        ],
        after,
        "block_output",
    )


def start_kernel(joined_ref, weight_ref, patch_ref, mods_ref, middle_ref, out_ref, sums_ref):
    width = patch_ref.shape[1]
    grad_first = jnp.zeros(patch_ref.shape, WIDE_TYPE)
    for part in range(3):
        columns = slice(part * width, (part + 1) * width)
        grad_first += contract(joined_ref[part], weight_ref[:, columns], 1, 1)
    normed, reciprocal = normalize_rows(patch_ref[...].astype(WIDE_TYPE))
    out_ref[...] = middle_ref[...] + normalize_rows_back(
        grad_first * (1.0 + mods_ref[0, 1:2, :]), normed, reciprocal
    )
    sums_ref[0] = jnp.concatenate(
        [
            jnp.sum(grad_first, axis=0, keepdims=True),
            jnp.sum(grad_first * normed, axis=0, keepdims=True),
        ],
        axis=0,
    )


def start_back(grad_joined, weights, patches, mods, grad_middle, after):
    count, width = patches.shape
    quarter = count // 4
    rows = row_block(quarter, width)
    return stepped(
        start_kernel,
        4,
        (grad_joined, weights, patches, mods, grad_middle),
        [
            pl.BlockSpec((3, quarter, width), lambda step: (0, step, 0)),
            column_block(weights, 3 * width, 0),
            rows,
            mods_block(mods),
            rows,
        ],
        [rows, sums_block(2, width)],
        [
            jax.ShapeDtypeStruct((count, width), WIDE_TYPE),
            jax.ShapeDtypeStruct((4, 2, width), WIDE_TYPE),
        ],
        after,
        "start_back",
    )


def expert_sums_kernel(early_ref, late_ref, up_ref, down_ref):
    local, hidden = up_ref.shape
    width = down_ref.shape[1]
    depth = hidden // (4 * local)
    for block in range(4):
        ref = (early_ref, late_ref)[block // 2]
        for part in range(depth):
            source = (block % 2) * width + part * local
            target = (part * 4 + block) * local
            up_ref[:, target : target + local] = ref[:, source : source + local].astype(WIDE_TYPE)
        source = (2 + block % 2) * width
        down_ref[block * local : (block + 1) * local] = ref[:, source : source + width].astype(WIDE_TYPE)


def expert_sums(early, late):
    local, hidden = early.shape
    width = hidden // 4
    return stepped(
        expert_sums_kernel,
        1,
        (early, late),
        [whole_block(early), whole_block(late)],
        [
            pl.BlockSpec((local, hidden), lambda step: (0, 0)),
            pl.BlockSpec((4 * local, width), lambda step: (0, 0)),
        ],
        [
            jax.ShapeDtypeStruct((local, hidden), WIDE_TYPE),
            jax.ShapeDtypeStruct((4 * local, width), WIDE_TYPE),
        ],
        (),
        "expert_sums",
    )


def slot_of_routes(route_rows, expert_count, capacity):
    pair_ids = route_rows.reshape(-1)
    onehot = (pair_ids[:, None] == jnp.arange(expert_count, dtype=jnp.int32)[None, :]).astype(
        jnp.int32
    )
    rank_values = jnp.cumsum(onehot, axis=0) - onehot
    slot_index = jnp.sum(rank_values * onehot, axis=1)
    return (pair_ids * capacity + slot_index).reshape(route_rows.shape)


def on_device(
    patches,
    cond,
    long_pack,
    routes,
    ada_weight,
    qkv_weight,
    out_weight,
    router_weight,
    shared_up,
    shared_down,
    expert_up,
    expert_down,
    out_grad,
):
    width = patches.shape[1]
    hidden = shared_up.shape[1]
    depth = lax.axis_size("dp")
    experts = lax.axis_size(PLANE)
    capacity = CAP
    slots = experts * capacity
    local = qkv_weight.shape[0]
    slice_rows = local // experts
    plane_index = lax.axis_index(PLANE)

    def blocked(columns):
        split = columns.reshape(columns.shape[0], depth, 4, local)
        return jnp.transpose(split, (0, 2, 1, 3)).reshape(columns.shape)

    def own(rows):
        return lax.dynamic_slice_in_dim(rows, plane_index * slice_rows, slice_rows, 0)

    places = slot_of_routes(routes, experts, capacity)
    columns, places = places, places.T
    expert_piece = expert_payload(expert_up[0], expert_down[0], ())

    cond_wide = cond.astype(WIDE_TYPE)
    cond_rows = cond.shape[0]
    if slice_rows % 8 == 0:
        first_stack = lax.all_to_all(
            first_payload(qkv_weight, out_weight, router_weight, cond, depth, slice_rows),
            "dp",
            split_axis=0,
            concat_axis=0,
            tiled=True,
        )
        first_end = 4 * width + 128
        silu_parts = first_stack[:, :cond_rows, first_end : first_end + local]
        rest_piece = rest_payload(
            shared_up, shared_down, slice_rows, (first_stack, places, expert_piece)
        )
    else:
        silu_cond = jax.nn.silu(cond_wide).astype(NARROW_TYPE)
        silu_parts = lax.all_to_all(
            jnp.transpose(silu_cond.reshape(cond_rows, depth, local), (1, 0, 2)),
            "dp",
            split_axis=0,
            concat_axis=0,
            tiled=True,
        )
        router_slice = jnp.pad(own(router_weight), ((0, 0), (0, 128 - router_weight.shape[1])))
        first_stack = depth_stack(
            jnp.concatenate([own(qkv_weight), own(out_weight), router_slice], axis=1)
        )
        down_slice = lax.dynamic_slice_in_dim(
            shared_down.reshape(4, local, width), plane_index * slice_rows, slice_rows, 1
        )
        rest_piece = jnp.concatenate(
            [
                blocked(own(shared_up)),
                jnp.transpose(down_slice, (1, 0, 2)).reshape(slice_rows, 4 * width),
            ],
            axis=1,
        )
    silu_parts = silu_parts.reshape(depth * cond_rows, local)
    partial = product_plain_operands(silu_parts, ada_weight)
    first_sides = side_gather(first_stack)
    rest_stack = lax.all_gather(rest_piece, "dp", axis=0)
    modulation = jnp.sum(
        lax.all_to_all(
            partial.reshape(depth, cond_rows, 6 * width), "dp", split_axis=0, concat_axis=0, tiled=True
        ),
        axis=0,
    )
    blocks = modulation.reshape(4, 6, width)
    is_long = long_pack[0] == 1
    mods = jnp.where(is_long, blocks[:1], blocks)

    def exchange(rows):
        return lax.all_to_all(rows, PLANE, split_axis=0, concat_axis=0, tiled=True)

    grad_shared, mixture_slots = spread_mixture(
        out_grad, mods, places, silu_parts.reshape(SPARE, -1), ()
    )
    first_near = near_slices(first_sides, (mixture_slots,))
    expert_piece, first_near = together(expert_piece, first_near)
    expert_weights = lax.all_gather(expert_piece, "dp", axis=0, tiled=True)
    mixture_slots = exchange(mixture_slots)
    first_full = plane_gather(first_near)
    rest_sides = side_gather(rest_stack)
    first_in, joined = first_half(patches, mods, first_full, ())
    attended, log_total = attend(long_pack, joined)
    attended, mixture_slots = together(attended, mixture_slots)
    attention, middle, second_in, gate_values, gate_rows = second_half(
        attended, patches, mods, routes, first_full, ()
    )
    slot_rows = spread_second(second_in, places, gate_rows, ())
    rest = plane_gather(near_slices(rest_sides, (attended, slot_rows)))
    slots_there = exchange(slot_rows)

    shared, grad_from_shared, kept, sent = shared_expert(
        second_in, grad_shared, rest, local, (slot_rows,)
    )
    sent, slots_there = together(sent, slots_there)
    gates_there = jnp.sum(slots_there[:, capacity : capacity + 3, :capacity].astype(WIDE_TYPE), axis=1)
    routed = (
        slots_there[:, :capacity].reshape(slots, width),
        mixture_slots[:, :capacity].reshape(slots, width),
        gates_there.reshape(slots, 1),
    )
    silu_all = mixture_slots[:, capacity:, : silu_parts.size // SPARE]
    silu_all = silu_all.reshape(experts, depth, cond_rows, local)
    silu_all = jnp.transpose(silu_all, (1, 0, 2, 3)).reshape(depth * experts * cond_rows, local)
    result_rows, grad_rows, gate_dots, units, grad_units = routed_expert(
        *routed, expert_weights, ()
    )
    grad_rows_back = exchange(grad_rows.reshape(experts, capacity, width)).reshape(slots, width)
    gate_dots_back = exchange(gate_dots.reshape(experts, 1, capacity)).reshape(1, slots)
    early_sums = routed_sums(*routed, units, grad_units, 0, ())
    early_sums, gate_dots_back = together(early_sums, gate_dots_back)
    early_final = lax.psum_scatter(early_sums, "dp", scatter_dimension=0, tiled=True)
    late_sums = routed_sums(*routed, units, grad_units, 1, (early_sums,))
    middle_own, *middle_sides = pair_sum(kept, flip(sent, CORE), (late_sums,))

    grad_middle, grad_attention, grad_attended, grad_logits, middle_sums = middle_back(
        grad_rows_back,
        gate_dots_back,
        columns,
        routes,
        gate_values,
        grad_from_shared,
        middle,
        attention,
        mods,
        out_grad,
        first_full,
        (silu_all,),
    )
    late_sums, *middle_sides, grad_attended = together(late_sums, *middle_sides, grad_attended)
    late_final = lax.psum_scatter(late_sums, "dp", scatter_dimension=0, tiled=True)
    result_back = exchange(result_rows.reshape(experts, capacity, width)).reshape(slots, width)
    grad_joined = attend_back(long_pack, joined, log_total, grad_attended, ())
    last_parts = last_gradients(
        grad_joined, first_in, grad_attention, attended, grad_logits, second_in
    )
    middle_sum = side_sum(middle_own, *middle_sides, after=(grad_joined,))
    block_out, output_sums = block_output(
        result_back,
        columns,
        shared,
        middle,
        mods,
        out_grad,
        (*last_parts, middle_sum, early_final),
    )
    middle_final = lax.psum_scatter(middle_sum, "dp", scatter_dimension=0, tiled=True)
    middle_final = middle_final.astype(WIDE_TYPE)
    shared_up_grad = middle_final[:, : hidden // experts]
    shared_down_grad = jnp.transpose(
        middle_final[:, hidden // experts :].reshape(local, 4, width // experts), (1, 0, 2)
    ).reshape(4 * local, width // experts)

    last_pair = pair_sum(last_parts[0], flip(last_parts[1], CORE))
    patches_grad, start_sums = start_back(
        grad_joined, first_full, patches, mods, grad_middle, tuple(last_pair)
    )
    last_sum = side_sum(*last_pair)
    grad_chosen = jnp.concatenate([start_sums, middle_sums, output_sums], axis=1)
    grad_chosen = grad_chosen.reshape(1, 4, 6 * width)
    long_total = jnp.sum(grad_chosen, axis=1, keepdims=True)
    first_slot = (jnp.arange(4, dtype=jnp.int32) == 0)[None, :, None]
    grad_blocks = jnp.where(is_long, jnp.where(first_slot, long_total, 0.0), grad_chosen)
    grad_modulation = grad_blocks.reshape(cond_rows, 6 * width).astype(NARROW_TYPE)
    everyone = ("dp",) + PLANE
    columns = 6 * width // experts
    grad_columns = jnp.transpose(grad_modulation.reshape(cond_rows, experts, columns), (1, 0, 2))
    grad_columns = jnp.broadcast_to(grad_columns[None], (depth, experts, cond_rows, columns))
    grad_columns = lax.all_to_all(
        grad_columns.reshape(depth * experts, cond_rows, columns),
        everyone,
        split_axis=0,
        concat_axis=0,
        tiled=True,
    ).reshape(depth * experts * cond_rows, columns)
    ada_weight_grad = product_left_operand(silu_all, grad_columns)
    own_ada = lax.dynamic_slice_in_dim(ada_weight, plane_index * columns, columns, 1)
    silu_back, last_sum = together(product_right_operand(grad_columns, own_ada), last_sum)
    silu_back = lax.all_to_all(
        silu_back.reshape(depth * experts, cond_rows, local),
        everyone,
        split_axis=0,
        concat_axis=0,
        tiled=True,
    )
    silu_back = jnp.sum(silu_back.reshape(depth, experts, cond_rows, local), axis=1)
    grad_silu = jnp.transpose(silu_back, (1, 0, 2)).reshape(cond_rows, width)
    cond_grad = jax.vjp(jax.nn.silu, cond_wide)[1](grad_silu)[0]
    last_final = depth_scatter(last_sum)
    edge_one, edge_two = 3 * width // experts, 4 * width // experts
    qkv_weight_grad = last_final[:, :edge_one]
    out_weight_grad = last_final[:, edge_one:edge_two]
    router_weight_grad = last_final[:, edge_two : edge_two + 1]

    expert_up_grad, expert_down_grad = expert_sums(early_final, late_final)
    return (
        block_out,
        patches_grad,
        cond_grad,
        ada_weight_grad,
        qkv_weight_grad,
        out_weight_grad,
        router_weight_grad,
        shared_up_grad,
        shared_down_grad,
        expert_up_grad[None],
        expert_down_grad[None],
    )


def solution(mesh):
    in_specs = (
        P(("dp", "expert", "stream"), None),
        P(("dp", "expert", "stream"), None),
        P(("dp", "expert", "stream")),
        P(("dp", "expert", "stream"), None),
        P("dp", None),
        P("dp", None),
        P("dp", None),
        P("dp", None),
        P("dp", None),
        P("dp", None),
        P(("expert", "stream"), "dp", None),
        P(("expert", "stream"), "dp", None),
        P(("dp", "expert", "stream"), None),
    )
    out_specs = (
        P(("dp", "expert", "stream"), None),
        P(("dp", "expert", "stream"), None),
        P(("dp", "expert", "stream"), None),
        P("dp", ("expert", "stream")),
        P("dp", ("expert", "stream")),
        P("dp", ("expert", "stream")),
        P("dp", ("expert", "stream")),
        P("dp", ("expert", "stream")),
        P("dp", ("expert", "stream")),
        P(("expert", "stream"), "dp", None),
        P(("expert", "stream"), "dp", None),
    )
    return jax.shard_map(
        on_device, mesh=mesh, in_specs=in_specs, out_specs=out_specs, check_vma=False
    )
```

time: 1040 us -> 625 us (0.60)
  matrix products: 430 us -> 4.64 us
  Pallas kernels: 0 us -> 355 us
  other arithmetic: 115 us -> 9.48 us
  local copies, waits for them, and re-layouts: 150 us -> 44.7 us
  waiting for transfers between devices: 203 us -> 123 us
  blocking collectives: 54.5 us -> 0 us
    pallas_call x0 -> x26, Pallas kernels: none -> 355 us  [the longest x13 187 us: stepped(): pl.pallas_call(body, grid=(steps,), in_specs=list(in_specs) + [ANYWHERE]...]
    dot_general x42 -> x0, matrix products: 138 us -> none  [the longest x12 31.6 us: masked_scores(): jnp.einsum('qhd,khd->hqk', queries, keys, preferred_element_type=WIDE_TYPE)]
    dot_general x13 -> x1, matrix products: 123 us -> 1.84 us  [product_plain_operands(): return jnp.dot(left_side, right_side, preferred_element_type=WIDE_TYPE)]
    dot_general x8 -> x1, matrix products: 100 us -> 0.93 us  [product_right_operand(): lax.dot_general(left_side, right_side, (((1,), (1,)), ((), ())), preferre...]
    dot_general x8 -> x1, matrix products: 68.5 us -> 1.87 us  [product_left_operand(): lax.dot_general(left_side, right_side, (((0,), (0,)), ((), ())), preferre...]
    reduce_scatter x2 -> x3, waiting for transfers between devices: 68.6 us -> 4.59 us  [the longest x1 4.59 us: on_device(): lax.psum_scatter(late_sums, 'dp', scatter_dimension=0, tiled=True)]
    all_gather x3 -> x0, blocking collectives: 54.5 us -> none  [the longest x1 21.1 us: on_device(): first_group = lax.all_gather(own(qkv_weight), 'dp', axis=0)]
    ppermute x16, waiting for transfers between devices: 91.2 us -> 55.3 us  [flip(): lax.ppermute(value, PLANE, [(index, index ^ mask) for index in range(coun...]
  transfers between devices with their start and end apart: 33 -> 33, of which waited for: 10 -> 16; matrix products, arithmetic and copies ran while one was open for 46% -> 6% of each run, Pallas kernels for 0% -> 46%
where the time goes in v2:
time: 625 us; the launch traced here: 614 us
  Pallas kernels  355 us (57%)
  waiting for transfers between devices  123 us (20%)
  starting transfers between devices  62.6 us (10%)
  local copies, waits for them, and re-layouts  44.7 us (7%)
  between operations  15.1 us (2%)
  other arithmetic  9.48 us (2%)
    pallas_call x13, Pallas kernels, stepped(): pl.pallas_call(body, grid=(steps,), in_specs=list(in_specs) + [ANYWHERE]...  187 us
    ppermute x16, waiting for transfers between devices, flip(): lax.ppermute(value, PLANE, [(index, index ^ mask) for index in range(coun...  55.3 us
    pallas_call x1, Pallas kernels, attend_back(): pl.pallas_call(attend_back_kernel, grid=(width // 128,), in_specs=[pl.Blo...  45.5 us
    pallas_call x1, Pallas kernels, shared_expert(): pl.pallas_call(kernel, grid_spec=pltpu.PrefetchScalarGridSpec(num_scalar_...  44 us
    pallas_call x1, Pallas kernels, attend(): pl.pallas_call(attend_kernel, grid=(width // 128,), in_specs=[pl.BlockSpe...  33.5 us
    ppermute x3, waiting for transfers between devices, depth_shift(): lax.ppermute(value, 'dp', [(index, (index + shift) % depth) for index in...  23.7 us
    all_to_all x5, starting transfers between devices, exchange(): return lax.all_to_all(rows, PLANE, split_axis=0, concat_axis=0, tiled=True)  22.6 us
    all_to_all x5, waiting for transfers between devices, exchange(): return lax.all_to_all(rows, PLANE, split_axis=0, concat_axis=0, tiled=True)  22.4 us
  transfers between devices with their start and end apart: 33, of which 16 were waited for; matrix products, arithmetic and copies ran while one was open for 6% of the time, Pallas kernels for 46%

profile of v2, /device:TPU:0, one launch (start us, length us, event | category | flops | bytes accessed | tf_op | source)
XLA Modules:
  0.0 614.3 jit_solution(6688110592343095049)
XLA Ops:
  10.6 6.3 %all-to-all-start = ((bf16[4,24,3456]{2,1,0:T(8,128)(2,1)}), bf16[4,24,3456]{2,1,0:T(8,128)(2,1)S(1)}, u32[]{:S(2)}, u32[]{:S(2)}) async-start(bf16[4,24,3456]{2,1,0:T(8,128)(2,1)} %first_payload.1), calls=%async_computation | async-start | bytes 1327104 | tf_op jit(solution)/shard_map/all_to_all | solution.py:1125
  25.0 3.4 expert_payload.1.refs_2_
  28.3 6.1 all-to-all-done.refs_0_
  38.9 3.5 all-to-all-start.1
  42.4 2.5 collective-permute-start.2
  47.3 10.0 %all-to-all-done.1 = f32[4,4,4608]{2,1,0:T(4,128)S(1)} async-done(((f32[4,4,4608]{2,1,0:T(4,128)}), f32[4,4,4608]{2,1,0:T(4,128)S(1)}, u32[]{:S(2)}, u32[]{:S(2)}) %all-to-all-start.1) | async-done | bytes 294944 | tf_op jit(solution)/shard_map/all_to_all | solution.py:1165
  58.1 8.7 %spread_mixture.1 = (bf16[1024,768]{1,0:T(8,128)(2,1)}, bf16[8,336,768]{2,1,0:T(8,128)(2,1)}) custom-call(bf16[1024,768]{1,0:T(8,128)(2,1)} %refs_5_.1, f32[4,6,768]{2,1,0:T(8,128)} %broadcast_select_fusion.refs_1_.refs_2_.refs_8_.refs_4_.refs_3_, s32[2,1024]{1,0:T(2,128)} %copy.117.refs_2_.refs_1_, bf16[16,192]{1,0:T(8,128)(2,1)} %reshape.181.refs_3_), custom_call_target="tpu_custom_call" | custom-call | tf_op jit(solution)/shard_map/spread_mixture/pallas_call | solution.py:375
  66.8 6.8 %collective-permute-done.1.refs_2_ = bf16[4,24,3456]{2,1,0:T(8,128)(2,1)} collective-permute-done((bf16[4,24,3456]{2,1,0:T(8,128)(2,1)S(1)}, bf16[4,24,3456]{2,1,0:T(8,128)(2,1)}, u32[]{:S(2)}, u32[]{:S(2)}) %collective-permute-start.1) | collective-permute-done | bytes 663584 | tf_op jit(solution)/shard_map/ppermute | solution.py:344
  73.7 4.0 stack_sides.2.near_ref
  77.8 4.7 all-to-all-start.2
  83.0 2.6 collective-permute-start.6
  90.3 3.4 place_slices.2
  96.2 8.5 %first_half.1 = (bf16[1024,768]{1,0:T(8,128)(2,1)}, bf16[3,1024,768]{2,1,0:T(8,128)(2,1)}) custom-call(bf16[1024,768]{1,0:T(8,128)(2,1)} %refs_2_.1, f32[4,6,768]{2,1,0:T(8,128)} %broadcast_select_fusion.refs_1_.refs_2_.refs_8_.refs_4_.refs_3_, bf16[768,3456]{1,0:T(8,128)(2,1)} %bitcast.66), custom_call_target="tpu_custom_call" | custom-call | tf_op jit(solution)/shard_map/first_half/pallas_call | solution.py:375
  104.7 33.5 %attend.1 = (bf16[1024,768]{1,0:T(8,128)(2,1)}, f32[1024,768]{1,0:T(8,128)}) custom-call(s32[1]{0:T(128)S(6)} %copy.142.long_ref, bf16[3,1024,768]{2,1,0:T(8,128)(2,1)} %get-tuple-element.69.joined_ref), custom_call_target="tpu_custom_call" | custom-call | tf_op jit(solution)/shard_map/attend/pallas_call | solution.py:72
  138.1 7.3 %second_half.1 = (f32[1024,768]{1,0:T(8,128)}, f32[1024,768]{1,0:T(8,128)}, bf16[1024,768]{1,0:T(8,128)(2,1)}, f32[1024,2]{1,0:T(8,128)}, f32[2,1024]{1,0:T(2,128)}) custom-call(bf16[1024,768]{1,0:T(8,128)(2,1)} %get-tuple-element.71.refs_0_.refs_4_.attended_ref, bf16[1024,768]{1,0:T(8,128)(2,1)} %refs_2_.1, ...), custom_call_target="tpu_custom_call" | custom-call | tf_op jit(solution)/shard_map/second_half/pallas_call | solution.py:375
  145.4 9.2 %spread_second.1.refs_5_ = bf16[8,336,768]{2,1,0:T(8,128)(2,1)} custom-call(bf16[1024,768]{1,0:T(8,128)(2,1)} %get-tuple-element.72.refs_0_.refs_1_.second_ref, s32[2,1024]{1,0:T(2,128)} %copy.117.refs_2_.refs_1_, f32[2,1024]{1,0:T(2,128)} %get-tuple-element.74.refs_2_), custom_call_target="tpu_custom_call" | custom-call | tf_op jit(solution)/shard_map/spread_second/pallas_call | solution.py:375
  156.7 23.8 %collective-permute-done.5.refs_2_ = bf16[4,24,6144]{2,1,0:T(8,128)(2,1)} collective-permute-done((bf16[4,24,6144]{2,1,0:T(8,128)(2,1)}, bf16[4,24,6144]{2,1,0:T(8,128)(2,1)}, u32[]{:S(2)}, u32[]{:S(2)}) %collective-permute-start.5) | collective-permute-done | bytes 1179680 | tf_op jit(solution)/shard_map/ppermute | solution.py:344
  180.7 5.0 stack_sides.3.near_ref
  185.6 4.6 all-to-all-start.3
  190.2 4.4 slice.45
  194.7 7.1 %place_slices.3 = bf16[4,8,24,6144]{3,2,1,0:T(8,128)(2,1)} custom-call(s32[5]{0:T(128)S(1)} %stack.26.order_ref, bf16[4,4,24,6144]{3,2,1,0:T(8,128)(2,1)S(1)} %copy-done.3, bf16[4,4,24,6144]{3,2,1,0:T(8,128)(2,1)} %collective-permute-done.7.far_ref), custom_call_target="tpu_custom_call" | custom-call | tf_op jit(solution)/shard_map/place_slices/pallas_call | solution.py:432
  201.7 44.0 %shared_expert.1 = (f32[1024,768]{1,0:T(8,128)}, f32[1024,768]{1,0:T(8,128)}, bf16[4,768,768]{2,1,0:T(8,128)(2,1)}, bf16[4,768,768]{2,1,0:T(8,128)(2,1)}) custom-call(s32[1]{0:T(128)} %bitcast.refs_0_.core_ref, bf16[1024,768]{1,0:T(8,128)(2,1)} %get-tuple-element.72.refs_0_.refs_1_.second_ref, bf16[1024,768]{1,0:T(8,128)(2,1)} %get-tuple-element.73.refs_2_, ...), custom_call_target="tpu_custom_call" | custom-call | tf_op jit(solution)/shard_map/shared_expert/pallas_call | solution.py:323
  245.7 4.3 slice.44
  253.1 62.2 %routed_expert.1 = (bf16[2560,768]{1,0:T(8,128)(2,1)}, bf16[2560,768]{1,0:T(8,128)(2,1)}, f32[2560,1]{1,0:T(8,128)}, bf16[2560,3072]{1,0:T(8,128)(2,1)}, bf16[2560,3072]{1,0:T(8,128)(2,1)}) custom-call(bf16[2560,768]{1,0:T(8,128)(2,1)} %bitcast.78, bf16[2560,768]{1,0:T(8,128)(2,1)} %bitcast.75, f32[2560,1]{1,0:T(8,128)} %reshape.209.refs_2_, ...), custom_call_target="tpu_custom_call" | custom-call | tf_op jit(solution)/shard_map/routed_expert/pallas_call | solution.py:375
  317.7 4.1 all-to-all-start.5
  321.8 19.7 %routed_sums.2.refs_5_ = bf16[768,3072]{1,0:T(8,128)(2,1)} custom-call(bf16[2560,768]{1,0:T(8,128)(2,1)} %bitcast.79, bf16[2560,768]{1,0:T(8,128)(2,1)} %bitcast.76, f32[2560,1]{1,0:T(8,128)} %reshape.209.refs_2_, bf16[2560,3072]{1,0:T(8,128)(2,1)} %get-tuple-element.83.refs_3_, bf16[2560,3072]{1,0:T(8,128)(2,1)} %get-tuple-element.84.refs_4_), custom_call_target="tpu_custom_call" | custom-call | tf_op jit(solution)/shard_map/routed_sums/pallas_call | solution.py:375
  342.8 4.5 all-to-all-start.6
  348.9 20.5 %routed_sums.3.refs_0_ = bf16[768,3072]{1,0:T(8,128)(2,1)} custom-call(bf16[2560,768]{1,0:T(8,128)(2,1)} %bitcast.80, bf16[2560,768]{1,0:T(8,128)(2,1)} %bitcast.77, f32[2560,1]{1,0:T(8,128)} %reshape.209.refs_2_, bf16[2560,3072]{1,0:T(8,128)(2,1)} %get-tuple-element.83.refs_3_, bf16[2560,3072]{1,0:T(8,128)(2,1)} %get-tuple-element.84.refs_4_, ...), custom_call_target="tpu_custom_call" | custom-call | tf_op jit(solution)/shard_map/routed_sums/pallas_call | solution.py:375
  371.7 5.8 pair_sum.2
  378.9 13.8 %all-to-all-done.6 = bf16[8,320,768]{2,1,0:T(8,128)(2,1)} async-done(((bf16[8,320,768]{2,1,0:T(8,128)(2,1)}), bf16[8,320,768]{2,1,0:T(8,128)(2,1)}, u32[]{:S(2)}, u32[]{:S(2)}) %all-to-all-start.6) | async-done | bytes 3932192 | tf_op jit(solution)/shard_map/all_to_all | solution.py:1175
  392.7 18.2 %middle_back.1 = (f32[1024,768]{1,0:T(8,128)}, bf16[1024,768]{1,0:T(8,128)(2,1)}, bf16[1024,768]{1,0:T(8,128)(2,1)}, bf16[1024,128]{1,0:T(8,128)(2,1)}, f32[4,3,768]{2,1,0:T(4,128)}) custom-call(bf16[2560,768]{1,0:T(8,128)(2,1)} %bitcast.21.refs_0_, f32[1,2560]{1,0:T(1,128)} %reshape.191.refs_1_, s32[1024,2]{1,0:T(8,128)} %copy-done.14, ...), custom_call_target="tpu_custom_call" | custom-call | tf_op jit(solution)/shard_map/middle_back/pallas_call | solution.py:375
  414.5 45.5 %attend_back.1.joined_ref.refs_3_.refs_0_ = bf16[3,1024,768]{2,1,0:T(8,128)(2,1)} custom-call(s32[1]{0:T(128)S(6)} %copy.142.long_ref, bf16[3,1024,768]{2,1,0:T(8,128)(2,1)} %get-tuple-element.69.joined_ref, f32[1024,768]{1,0:T(8,128)} %get-tuple-element.82.total_ref, bf16[1024,768]{1,0:T(8,128)(2,1)} %get-tuple-element.98.grad_ref), custom_call_target="tpu_custom_call" | custom-call | tf_op jit(solution)/shard_map/attend_back/pallas_call | solution.py:119
  460.0 5.5 collective-permute-done.10.refs_1_
  470.8 4.7 all-to-all-start.4
  475.5 14.0 %last_gradients.1 = (bf16[4,400,768]{2,1,0:T(8,128)(2,1)}, bf16[4,400,768]{2,1,0:T(8,128)(2,1)}) custom-call(s32[1]{0:T(128)} %bitcast.refs_0_.core_ref, bf16[3,1024,768]{2,1,0:T(8,128)(2,1)} %attend_back.1.joined_ref.refs_3_.refs_0_, bf16[1024,768]{1,0:T(8,128)(2,1)} %get-tuple-element.99.first_ref, bf16[1024,768]{1,0:T(8,128)(2,1)} %get-tuple-element.100.grad_ref, ...), custom_call_target="tpu_custom_call" | custom-call | tf_op jit(solution)/shard_map/last_gradients/pallas_call | solution.py:544
  489.9 4.5 collective-permute-done.12.other_ref
  503.0 9.8 %start_back.1 = (f32[1024,768]{1,0:T(8,128)}, f32[4,2,768]{2,1,0:T(2,128)}) custom-call(bf16[3,1024,768]{2,1,0:T(8,128)(2,1)} %attend_back.1.joined_ref.refs_3_.refs_0_, bf16[768,3456]{1,0:T(8,128)(2,1)} %bitcast.71, bf16[1024,768]{1,0:T(8,128)(2,1)} %refs_2_.1, f32[4,6,768]{2,1,0:T(8,128)} %broadcast_select_fusion.refs_1_.refs_2_.refs_8_.refs_4_.refs_3_, ...), custom_call_target="tpu_custom_call" | custom-call | tf_op jit(solution)/shard_map/start_back/pallas_call | solution.py:375
  512.9 8.5 %all-to-all-done.4 = bf16[8,320,768]{2,1,0:T(8,128)(2,1)} async-done(((bf16[8,320,768]{2,1,0:T(8,128)(2,1)}), bf16[8,320,768]{2,1,0:T(8,128)(2,1)}, u32[]{:S(2)}, u32[]{:S(2)}) %all-to-all-start.4) | async-done | bytes 3932192 | tf_op jit(solution)/shard_map/all_to_all | solution.py:1175
  521.4 10.2 %block_output.1 = (bf16[1024,768]{1,0:T(8,128)(2,1)}, f32[4,1,768]{2,1,0:T(1,128)}) custom-call(bf16[2560,768]{1,0:T(8,128)(2,1)} %bitcast.19.refs_0_, s32[1024,2]{1,0:T(8,128)} %copy-done.14, f32[1024,768]{1,0:T(8,128)} %get-tuple-element.80.refs_2_, f32[1024,768]{1,0:T(8,128)} %get-tuple-element.81.refs_6_.refs_3_, ...), custom_call_target="tpu_custom_call" | custom-call | tf_op jit(solution)/shard_map/block_output/pallas_call | solution.py:375
  534.2 4.6 all-to-all-start.7
  538.9 10.4 %collective-permute-done.15.refs_2_ = bf16[400,768]{1,0:T(8,128)(2,1)} collective-permute-done((bf16[400,768]{1,0:T(8,128)(2,1)}, bf16[400,768]{1,0:T(8,128)(2,1)}, u32[]{:S(2)}, u32[]{:S(2)}) %collective-permute-start.15) | collective-permute-done | bytes 614432 | tf_op jit(solution)/shard_map/ppermute | solution.py:344
  549.3 2.7 side_sum.3
  559.1 4.2 all-to-all-start.8
  566.3 2.4 collective-permute-start.17
  572.0 9.6 %collective-permute-done.16 = bf16[192,400]{0,1:T(8,128)(2,1)S(1)} collective-permute-done((bf16[192,400]{0,1:T(8,128)(2,1)S(1)}, bf16[192,400]{0,1:T(8,128)(2,1)S(1)}, u32[]{:S(2)}, u32[]{:S(2)}) %collective-permute-start.16) | collective-permute-done | bytes 153632 | tf_op jit(solution)/shard_map/ppermute | solution.py:571
  581.6 14.1 %collective-permute-done.17 = bf16[192,400]{0,1:T(8,128)(2,1)S(1)} collective-permute-done((bf16[192,400]{0,1:T(8,128)(2,1)}, bf16[192,400]{0,1:T(8,128)(2,1)S(1)}, u32[]{:S(2)}, u32[]{:S(2)}) %collective-permute-start.17) | collective-permute-done | bytes 153632 | tf_op jit(solution)/shard_map/ppermute | solution.py:571
  598.8 4.6 reduce-scatter.8.cloned.1.call-done.refs_1_
  603.4 4.2 expert_sums.1
  (163 shorter events, 77.1 us)
Async XLA Ops:
  7.2 29.9 %copy-start = (bf16[192,4608]{1,0:T(8,128)(2,1)S(1)}, bf16[192,4608]{1,0:T(8,128)(2,1)}, u32[]{:S(2)}) copy-start(bf16[192,4608]{1,0:T(8,128)(2,1)} %param.17) | copy-start | bytes 5308420
  7.2 9.7 %copy-start.21 = (s32[1024,2]{0,1:T(2,128)S(1)}, s32[1024,2]{0,1:T(2,128)}, u32[]{:S(2)}) copy-start(s32[1024,2]{0,1:T(2,128)} %param.16) | copy-start | bytes 24580
  10.6 23.8 %all-to-all-start = ((bf16[4,24,3456]{2,1,0:T(8,128)(2,1)}), bf16[4,24,3456]{2,1,0:T(8,128)(2,1)S(1)}, u32[]{:S(2)}, u32[]{:S(2)}) async-start(bf16[4,24,3456]{2,1,0:T(8,128)(2,1)} %first_payload.1), calls=%async_computation | async-start | bytes 1327104 | tf_op jit(solution)/shard_map/all_to_all | solution.py:1125
  16.9 66.1 %all-gather.6.cloned.1.call-start = ((), (), s32[]{:S(2)}) async-start(), calls=%async_computation.16 | async-start | bytes 1474560 | tf_op jit(solution)/shard_map/all_gather | solution.py:1163
  17.2 7.8 %copy-start.13 = (s32[1024,2]{1,0:T(8,128)}, s32[1024,2]{1,0:T(8,128)S(1)}, u32[]{:S(2)}) copy-start(s32[1024,2]{1,0:T(8,128)S(1)} %copy.114.refs_3_) | copy-start | bytes 24580
  24.2 4.2 copy-start.14
  37.0 5.4 copy-start.16
  38.9 18.3 %all-to-all-start.1 = ((f32[4,4,4608]{2,1,0:T(4,128)}), f32[4,4,4608]{2,1,0:T(4,128)S(1)}, u32[]{:S(2)}, u32[]{:S(2)}) async-start(f32[4,4,4608]{2,1,0:T(4,128)} %fusion), calls=%async_computation.1 | async-start | bytes 589824 | tf_op jit(solution)/shard_map/all_to_all | solution.py:1165
  42.4 210.7 %all-gather.4.cloned.1.call-start = ((), (), s32[]{:S(2)}) async-start(), calls=%async_computation.12 | async-start | bytes 11796480 | tf_op jit(solution)/shard_map/all_gather | solution.py:1182
  42.4 24.4 %collective-permute-start.2 = (bf16[4,24,3456]{2,1,0:T(8,128)(2,1)S(1)}, bf16[4,24,3456]{2,1,0:T(8,128)(2,1)S(1)}, u32[]{:S(2)}, u32[]{:S(2)}) collective-permute-start(bf16[4,24,3456]{2,1,0:T(8,128)(2,1)S(1)} %copy-done.16), channel_id=1, source_target_pairs={{0,5},{1,4},{2,7},{3,6},{4,1},{5,0},{6,3},{7,2},{8,13},{9,12},{10,... | collective-permute-start | bytes 1990664 | tf_op jit(solution)/shard_map/ppermute | solution.py:344
  44.9 28.7 %collective-permute-start.1 = (bf16[4,24,3456]{2,1,0:T(8,128)(2,1)S(1)}, bf16[4,24,3456]{2,1,0:T(8,128)(2,1)}, u32[]{:S(2)}, u32[]{:S(2)}) collective-permute-start(bf16[4,24,3456]{2,1,0:T(8,128)(2,1)S(1)} %copy-done.16), channel_id=1, source_target_pairs={{0,1},{1,0},{2,3},{3,2},{4,5},{5,4},{6,7},{7,6},{8,9},{9,8},{10,11... | collective-permute-start | bytes 1990664 | tf_op jit(solution)/shard_map/ppermute | solution.py:344
  45.4 28.2 %collective-permute-start = (bf16[4,24,3456]{2,1,0:T(8,128)(2,1)S(1)}, bf16[4,24,3456]{2,1,0:T(8,128)(2,1)}, u32[]{:S(2)}, u32[]{:S(2)}) collective-permute-start(bf16[4,24,3456]{2,1,0:T(8,128)(2,1)S(1)} %copy-done.16), channel_id=1, source_target_pairs={{0,4},{1,5},{2,6},{3,7},{4,0},{5,1},{6,2},{7,3},{8,12},{9,13},{10,... | collective-permute-start | bytes 1990664 | tf_op jit(solution)/shard_map/ppermute | solution.py:344
  66.8 6.9 %copy-start.18 = (bf16[4,24,3456]{2,1,0:T(8,128)(2,1)}, bf16[4,24,3456]{2,1,0:T(8,128)(2,1)S(1)}, u32[]{:S(2)}) copy-start(bf16[4,24,3456]{2,1,0:T(8,128)(2,1)S(1)} %collective-permute-done.2.refs_3_) | copy-start | bytes 1990660
  77.8 60.4 %all-to-all-start.2 = ((bf16[8,336,768]{2,1,0:T(8,128)(2,1)}), bf16[8,336,768]{2,1,0:T(8,128)(2,1)}, u32[]{:S(2)}, u32[]{:S(2)}) async-start(bf16[8,336,768]{2,1,0:T(8,128)(2,1)} %get-tuple-element.67.refs_4_), calls=%async_computation.2 | async-start | bytes 8257536 | tf_op jit(solution)/shard_map/all_to_all | solution.py:1175
  82.5 5.9 collective-permute-start.3
  83.0 73.6 %collective-permute-start.6 = (bf16[4,24,6144]{2,1,0:T(8,128)(2,1)}, bf16[4,24,6144]{2,1,0:T(8,128)(2,1)S(1)}, u32[]{:S(2)}, u32[]{:S(2)}) collective-permute-start(bf16[4,24,6144]{2,1,0:T(8,128)(2,1)} %bitcast.88), channel_id=1, source_target_pairs={{0,5},{1,4},{2,7},{3,6},{4,1},{5,0},{6,3},{7,2},{8,13},{9,12},{10,... | collective-permute-start | bytes 3538952 | tf_op jit(solution)/shard_map/ppermute | solution.py:344
  85.6 94.9 %collective-permute-start.5 = (bf16[4,24,6144]{2,1,0:T(8,128)(2,1)}, bf16[4,24,6144]{2,1,0:T(8,128)(2,1)}, u32[]{:S(2)}, u32[]{:S(2)}) collective-permute-start(bf16[4,24,6144]{2,1,0:T(8,128)(2,1)} %bitcast.89), channel_id=1, source_target_pairs={{0,1},{1,0},{2,3},{3,2},{4,5},{5,4},{6,7},{7,6},{8,9},{9,8},{10,11... | collective-permute-start | bytes 3538952 | tf_op jit(solution)/shard_map/ppermute | solution.py:344
  86.2 94.5 %collective-permute-start.4 = (bf16[4,24,6144]{2,1,0:T(8,128)(2,1)}, bf16[4,24,6144]{2,1,0:T(8,128)(2,1)}, u32[]{:S(2)}, u32[]{:S(2)}) collective-permute-start(bf16[4,24,6144]{2,1,0:T(8,128)(2,1)} %bitcast.90), channel_id=1, source_target_pairs={{0,4},{1,5},{2,6},{3,7},{4,0},{5,1},{6,2},{7,3},{8,12},{9,13},{10,... | collective-permute-start | bytes 3538952 | tf_op jit(solution)/shard_map/ppermute | solution.py:344
  93.8 2.4 copy-start.1
  156.7 24.0 %copy-start.17 = (bf16[4,24,6144]{2,1,0:T(8,128)(2,1)}, bf16[4,24,6144]{2,1,0:T(8,128)(2,1)S(1)}, u32[]{:S(2)}) copy-start(bf16[4,24,6144]{2,1,0:T(8,128)(2,1)S(1)} %collective-permute-done.6.refs_3_) | copy-start | bytes 3538948
  185.6 9.0 %collective-permute-start.7 = (bf16[4,4,24,6144]{3,2,1,0:T(8,128)(2,1)}, bf16[4,4,24,6144]{3,2,1,0:T(8,128)(2,1)}, u32[]{:S(2)}, u32[]{:S(2)}) collective-permute-start(bf16[4,4,24,6144]{3,2,1,0:T(8,128)(2,1)} %stack_sides.3.near_ref), channel_id=1, source_target_pairs={{0,2},{1,3},{2,0},{3,1},{4,6},{5,7},{6,4},{7,5},{8,10},{9,11},{10,... | collective-permute-start | bytes 14155784 | tf_op jit(solution)/shard_map/ppermute | solution.py:344
  185.6 60.1 %all-to-all-start.3 = ((bf16[8,336,768]{2,1,0:T(8,128)(2,1)}), bf16[8,336,768]{2,1,0:T(8,128)(2,1)}, u32[]{:S(2)}, u32[]{:S(2)}) async-start(bf16[8,336,768]{2,1,0:T(8,128)(2,1)} %spread_second.1.refs_5_), calls=%async_computation.3 | async-start | bytes 8257536 | tf_op jit(solution)/shard_map/all_to_all | solution.py:1175
  190.2 4.4 copy-start.3
  317.7 23.8 %all-to-all-start.5 = ((f32[8,1,320]{2,1,0:T(1,128)}), f32[8,1,320]{2,1,0:T(1,128)S(1)}, u32[]{:S(2)}, u32[]{:S(2)}) async-start(f32[8,1,320]{2,1,0:T(1,128)} %reshape.208), calls=%async_computation.5 | async-start | bytes 24576 | tf_op jit(solution)/shard_map/all_to_all | solution.py:1175
  321.7 199.7 %reduce-scatter.4.cloned.1.call-start = ((), (), s32[]{:S(2)}) async-start(), calls=%async_computation.13 | async-start | bytes 5898240 | tf_op jit(solution)/shard_map/reduce_scatter | solution.py:1216
  342.2 27.1 %collective-permute-start.8 = (bf16[4,768,768]{2,1,0:T(8,128)(2,1)}, bf16[4,768,768]{2,1,0:T(8,128)(2,1)}, u32[]{:S(2)}, u32[]{:S(2)}) collective-permute-start(bf16[4,768,768]{2,1,0:T(8,128)(2,1)} %get-tuple-element.88), channel_id=1, source_target_pairs={{0,2},{1,3},{2,0},{3,1},{4,6},{5,7},{6,4},{7,5},{8,10},{9,11},{10,... | collective-permute-start | bytes 14155784 | tf_op jit(solution)/shard_map/ppermute | solution.py:344
  342.8 50.0 %all-to-all-start.6 = ((bf16[8,320,768]{2,1,0:T(8,128)(2,1)}), bf16[8,320,768]{2,1,0:T(8,128)(2,1)}, u32[]{:S(2)}, u32[]{:S(2)}) async-start(bf16[8,320,768]{2,1,0:T(8,128)(2,1)} %bitcast.83), calls=%async_computation.6 | async-start | bytes 7864320 | tf_op jit(solution)/shard_map/all_to_all | solution.py:1175
  347.3 205.6 %reduce-scatter.6.cloned.1.call-start = ((), (), s32[]{:S(2)}) async-start(), calls=%async_computation.14 | async-start | bytes 1474560 | tf_op jit(solution)/shard_map/reduce_scatter | solution.py:1251
  410.9 49.1 %collective-permute-start.9 = (bf16[768,768]{1,0:T(8,128)(2,1)}, bf16[768,768]{1,0:T(8,128)(2,1)S(1)}, u32[]{:S(2)}, u32[]{:S(2)}) collective-permute-start(bf16[768,768]{1,0:T(8,128)(2,1)} %get-tuple-element.105), channel_id=1, source_target_pairs={{0,4},{1,5},{2,6},{3,7},{4,0},{5,1},{6,2},{7,3},{8,12},{9,13},{10,... | collective-permute-start | bytes 3538952 | tf_op jit(solution)/shard_map/ppermute | solution.py:344
  412.3 53.2 %collective-permute-start.10 = (bf16[768,768]{1,0:T(8,128)(2,1)}, bf16[768,768]{1,0:T(8,128)(2,1)S(1)}, u32[]{:S(2)}, u32[]{:S(2)}) collective-permute-start(bf16[768,768]{1,0:T(8,128)(2,1)} %get-tuple-element.106), channel_id=1, source_target_pairs={{0,1},{1,0},{2,3},{3,2},{4,5},{5,4},{6,7},{7,6},{8,9},{9,8},{10,11... | collective-permute-start | bytes 3538952 | tf_op jit(solution)/shard_map/ppermute | solution.py:344
  412.9 52.6 %collective-permute-start.11 = (bf16[768,768]{1,0:T(8,128)(2,1)}, bf16[768,768]{1,0:T(8,128)(2,1)S(1)}, u32[]{:S(2)}, u32[]{:S(2)}) collective-permute-start(bf16[768,768]{1,0:T(8,128)(2,1)} %get-tuple-element.107), channel_id=1, source_target_pairs={{0,5},{1,4},{2,7},{3,6},{4,1},{5,0},{6,3},{7,2},{8,13},{9,12},{10,... | collective-permute-start | bytes 3538952 | tf_op jit(solution)/shard_map/ppermute | solution.py:344
  414.5 51.1 %copy-start.12 = (f32[768,768]{1,0:T(8,128)S(1)}, f32[768,768]{1,0:T(8,128)}, u32[]{:S(2)}) copy-start(f32[768,768]{1,0:T(8,128)} %copy-done.11) | copy-start | bytes 7077892
  470.2 133.2 %reduce-scatter.8.cloned.1.call-start = ((), (), s32[]{:S(2)}) async-start(), calls=%async_computation.15 | async-start | bytes 5898240 | tf_op jit(solution)/shard_map/reduce_scatter | solution.py:1235
  470.8 50.6 %all-to-all-start.4 = ((bf16[8,320,768]{2,1,0:T(8,128)(2,1)}), bf16[8,320,768]{2,1,0:T(8,128)(2,1)}, u32[]{:S(2)}, u32[]{:S(2)}) async-start(bf16[8,320,768]{2,1,0:T(8,128)(2,1)} %bitcast.82), calls=%async_computation.4 | async-start | bytes 7864320 | tf_op jit(solution)/shard_map/all_to_all | solution.py:1175
  489.5 4.9 collective-permute-start.12
  499.5 39.4 %collective-permute-start.13 = (bf16[400,768]{1,0:T(8,128)(2,1)}, bf16[400,768]{1,0:T(8,128)(2,1)}, u32[]{:S(2)}, u32[]{:S(2)}) collective-permute-start(bf16[400,768]{1,0:T(8,128)(2,1)} %get-tuple-element.111.refs_6_), channel_id=1, source_target_pairs={{0,4},{1,5},{2,6},{3,7},{4,0},{5,1},{6,2},{7,3},{8,12},{9,13},{10,... | collective-permute-start | bytes 1843208 | tf_op jit(solution)/shard_map/ppermute | solution.py:344
  501.5 37.5 %collective-permute-start.14 = (bf16[400,768]{1,0:T(8,128)(2,1)}, bf16[400,768]{1,0:T(8,128)(2,1)}, u32[]{:S(2)}, u32[]{:S(2)}) collective-permute-start(bf16[400,768]{1,0:T(8,128)(2,1)} %get-tuple-element.112.refs_7_), channel_id=1, source_target_pairs={{0,1},{1,0},{2,3},{3,2},{4,5},{5,4},{6,7},{7,6},{8,9},{9,8},{10,11... | collective-permute-start | bytes 1843208 | tf_op jit(solution)/shard_map/ppermute | solution.py:344
  502.9 46.4 %collective-permute-start.15 = (bf16[400,768]{1,0:T(8,128)(2,1)}, bf16[400,768]{1,0:T(8,128)(2,1)}, u32[]{:S(2)}, u32[]{:S(2)}) collective-permute-start(bf16[400,768]{1,0:T(8,128)(2,1)} %get-tuple-element.113.refs_8_), channel_id=1, source_target_pairs={{0,5},{1,4},{2,7},{3,6},{4,1},{5,0},{6,3},{7,2},{8,13},{9,12},{10,... | collective-permute-start | bytes 1843208 | tf_op jit(solution)/shard_map/ppermute | solution.py:344
  521.4 10.2 %copy-start.19 = (f32[4,3,768]{2,1,0:T(4,128)S(1)}, f32[4,3,768]{2,1,0:T(4,128)}, u32[]{:S(2)}) copy-start(f32[4,3,768]{2,1,0:T(4,128)} %get-tuple-element.116) | copy-start | bytes 110596
  521.4 10.2 %copy-start.20 = (f32[4,2,768]{2,1,0:T(2,128)S(1)}, f32[4,2,768]{2,1,0:T(2,128)}, u32[]{:S(2)}) copy-start(f32[4,2,768]{2,1,0:T(2,128)} %get-tuple-element.115) | copy-start | bytes 73732
  521.4 27.9 %copy-start.7 = (f32[400,768]{1,0:T(8,128)S(1)}, f32[400,768]{1,0:T(8,128)}, u32[]{:S(2)}) copy-start(f32[400,768]{1,0:T(8,128)} %copy-done.6) | copy-start | bytes 3686404
  534.2 22.0 %all-to-all-start.7 = ((bf16[32,4,576]{2,1,0:T(4,128)(2,1)}), bf16[32,4,576]{2,1,0:T(4,128)(2,1)S(1)}, u32[]{:S(2)}, u32[]{:S(2)}) async-start(bf16[32,4,576]{2,1,0:T(4,128)(2,1)} %bitcast.24), calls=%async_computation.8 | async-start | bytes 327680 | tf_op jit(solution)/shard_map/all_to_all | solution.py:1273
  552.9 4.3 copy-start.10
  559.1 38.9 %all-to-all-start.8 = ((f32[32,4,192]{2,1,0:T(4,128)}), f32[32,4,192]{2,1,0:T(4,128)S(1)}, u32[]{:S(2)}, u32[]{:S(2)}) async-start(f32[32,4,192]{2,1,0:T(4,128)} %reshape.199), calls=%async_computation.9 | async-start | bytes 262144 | tf_op jit(solution)/shard_map/all_to_all | solution.py:1283
  563.5 34.7 %copy-start.22 = (bf16[4,768]{1,0:T(4,128)(2,1)S(1)}, bf16[4,768]{1,0:T(4,128)(2,1)}, u32[]{:S(2)}) copy-start(bf16[4,768]{1,0:T(4,128)(2,1)} %cond_ref.1) | copy-start | bytes 18436
  564.4 17.1 %collective-permute-start.16 = (bf16[192,400]{0,1:T(8,128)(2,1)S(1)}, bf16[192,400]{0,1:T(8,128)(2,1)S(1)}, u32[]{:S(2)}, u32[]{:S(2)}) collective-permute-start(bf16[192,400]{0,1:T(8,128)(2,1)S(1)} %bitcast.95), channel_id=1, source_target_pairs={{0,8},{8,16},{16,24},{24,0},{1,9},{9,17},{17,25},{25,1},{2,10},{10... | collective-permute-start | bytes 460808 | tf_op jit(solution)/shard_map/ppermute | solution.py:571
  566.3 29.4 %collective-permute-start.17 = (bf16[192,400]{0,1:T(8,128)(2,1)}, bf16[192,400]{0,1:T(8,128)(2,1)S(1)}, u32[]{:S(2)}, u32[]{:S(2)}) collective-permute-start(bf16[192,400]{0,1:T(8,128)(2,1)} %bitcast.94), channel_id=1, source_target_pairs={{0,16},{8,24},{16,0},{24,8},{1,17},{9,25},{17,1},{25,9},{2,18},{10... | collective-permute-start | bytes 460808 | tf_op jit(solution)/shard_map/ppermute | solution.py:571
  568.7 27.0 %collective-permute-start.18 = (bf16[192,400]{0,1:T(8,128)(2,1)S(1)}, bf16[192,400]{0,1:T(8,128)(2,1)S(1)}, u32[]{:S(2)}, u32[]{:S(2)}) collective-permute-start(bf16[192,400]{0,1:T(8,128)(2,1)S(1)} %bitcast.93), channel_id=1, source_target_pairs={{0,24},{8,0},{16,8},{24,16},{1,25},{9,1},{17,9},{25,17},{2,26},{10... | collective-permute-start | bytes 460808 | tf_op jit(solution)/shard_map/ppermute | solution.py:571
  (8 other events, 12.4 us)
Sparse Core Ops, SparseCore 0:
  37.2 33.5 all-gather.5
  77.9 167.0 all-gather.3
  342.4 86.7 reduce-scatter.3
  470.3 28.9 reduce-scatter.5
  501.5 101.8 reduce-scatter.7

commit v3 on v2

--- a/solution.py
+++ b/solution.py
@@ -62,9 +62,10 @@
     for whole in (True, False):
         @pl.when((long_ref[0] == 1) == whole)
         def _():
+            block = 2 * quarter if whole else quarter
             for head in range(2):
-                for part in range(4):
-                    rows = slice(part * quarter, (part + 1) * quarter)
+                for start in range(0, length, block):
+                    rows = slice(start, start + block)
                     attend_rows(joined_ref, attended_ref, total_ref, head, rows, slice(None) if whole else rows)
 
 def attend(long_pack, joined):
@@ -75,7 +76,7 @@
         in_specs=[pl.BlockSpec(memory_space=pltpu.SMEM), pl.BlockSpec((3, length, 128), lambda pair: (0, 0, pair))],
         out_specs=[pl.BlockSpec((length, 128), lambda pair: (0, pair))] * 2,
         out_shape=[jax.ShapeDtypeStruct((length, width), NARROW_TYPE), jax.ShapeDtypeStruct((length, width), WIDE_TYPE)],
-        compiler_params=pltpu.CompilerParams(vmem_limit_bytes=56 * MEBI),
+        compiler_params=pltpu.CompilerParams(vmem_limit_bytes=61 * MEBI),
         name="attend",
     )(long_pack, joined)
 
@@ -105,9 +106,10 @@
     for whole in (True, False):
         @pl.when((long_ref[0] == 1) == whole)
         def _():
+            block = 2 * quarter if whole else quarter
             for head in range(2):
-                for part in range(4):
-                    rows = slice(part * quarter, (part + 1) * quarter)
+                for start in range(0, length, block):
+                    rows = slice(start, start + block)
                     attend_back_rows(joined_ref, total_ref, grad_ref, out_ref, keys_acc, values_acc, head, rows, slice(None) if whole else rows)
     out_ref[1] = keys_acc[...].T.astype(NARROW_TYPE)
     out_ref[2] = values_acc[...].T.astype(NARROW_TYPE)
@@ -124,7 +126,7 @@
         out_specs=wide,
         out_shape=jax.ShapeDtypeStruct((3, length, width), NARROW_TYPE),
         scratch_shapes=[pltpu.VMEM((128, length), WIDE_TYPE)] * 2,
-        compiler_params=pltpu.CompilerParams(vmem_limit_bytes=56 * MEBI),
+        compiler_params=pltpu.CompilerParams(vmem_limit_bytes=61 * MEBI),
         name="attend_back",
     )(long_pack, joined, total, grad, *after)
 
@@ -143,14 +145,29 @@
     return hidden.astype(NARROW_TYPE), grad_pre.astype(NARROW_TYPE)
 
 
+def slot_rows_of(ref):
+    parts = [ref[part, :CAP] for part in range(ref.shape[0])]
+    return jnp.concatenate(parts, axis=0)
+
+
+def slot_gates_of(ref):
+    columns = []
+    for part in range(ref.shape[0]):
+        terms = ref[part, CAP:, :].astype(WIDE_TYPE)
+        gates = terms[0:1] + terms[1:2] + terms[2:3]
+        columns.append(jnp.broadcast_to(gates, (128, gates.shape[1])).T[:CAP, 0:1])
+    return jnp.concatenate(columns, axis=0)
+
+
 def routed_kernel(
-    rows_ref, grad_ref, gate_ref, weight_ref, out_ref, back_ref, dots_ref, hidden_ref, grad_pre_ref
+    rows_ref, grad_ref, weight_ref, out_ref, left_ref, right_ref, dots_ref, hidden_ref, grad_pre_ref
 ):
-    width = rows_ref.shape[1]
+    width = rows_ref.shape[2]
     count = weight_ref.shape[1] // (2 * width)
-    rows = rows_ref[...]
-    cotangent = grad_ref[...].astype(WIDE_TYPE)
-    grads = (gate_ref[...] * cotangent).astype(NARROW_TYPE)
+    rows = slot_rows_of(rows_ref)
+    gates = slot_gates_of(rows_ref)
+    cotangent = slot_rows_of(grad_ref).astype(WIDE_TYPE)
+    grads = (gates * cotangent).astype(NARROW_TYPE)
     out = jnp.zeros(rows.shape, WIDE_TYPE)
     back = jnp.zeros(rows.shape, WIDE_TYPE)
     for block in range(count):
@@ -163,34 +180,41 @@
         out += contract(hidden, down, 1, 0)
         back += contract(grad_pre, up, 1, 1)
     out = out.astype(NARROW_TYPE).astype(WIDE_TYPE)
-    out_ref[...] = (gate_ref[...] * out).astype(NARROW_TYPE)
-    back_ref[...] = back.astype(NARROW_TYPE)
+    out_ref[...] = (gates * out).astype(NARROW_TYPE)
+    left_ref[...] = back[:, : width // 2].astype(NARROW_TYPE)
+    right_ref[...] = back[:, width // 2 :].astype(NARROW_TYPE)
     dots_ref[...] = jnp.sum(out * cotangent, axis=1, keepdims=True)
 
 
-def routed_expert(rows, grads, gates, weights, after, block=512):
-    count, width = rows.shape
+def routed_expert(rows, grads, weights, after, parts=2):
+    sources, _, width = rows.shape
+    count, block = sources * CAP, parts * CAP
     hidden = weights.shape[1] // 2
     narrow = jax.ShapeDtypeStruct((count, width), NARROW_TYPE)
+    side = jax.ShapeDtypeStruct((count, width // 2), NARROW_TYPE)
     units = jax.ShapeDtypeStruct((count, hidden), NARROW_TYPE)
+    slots = pl.BlockSpec((parts,) + rows.shape[1:], lambda step: (step, 0, 0))
     return stepped(
         routed_kernel,
-        count // block,
-        (rows, grads, gates, weights),
-        [row_block(block, width), row_block(block, width), row_block(block, 1), whole_block(weights)],
-        [row_block(block, width), row_block(block, width), row_block(block, 1)]
+        sources // parts,
+        (rows, grads, weights),
+        [slots, slots, whole_block(weights)],
+        [row_block(block, width)]
+        + [row_block(block, width // 2)] * 2
+        + [row_block(block, 1)]
         + [row_block(block, hidden)] * 2,
-        [narrow, narrow, jax.ShapeDtypeStruct((count, 1), WIDE_TYPE), units, units],
+        [narrow, side, side, jax.ShapeDtypeStruct((count, 1), WIDE_TYPE), units, units],
         after,
         "routed_expert",
     )
 
 
 def sums_kernel(
-    steps, rows_ref, grad_ref, gate_ref, hidden_ref, grad_pre_ref, sums_ref, totals
+    steps, rows_ref, grad_ref, hidden_ref, grad_pre_ref, *refs
 ):
+    sums_ref, totals = refs[-2:]
     step = pl.program_id(0)
-    width = rows_ref.shape[1]
+    width = rows_ref.shape[2]
     count = totals.shape[0] // 2
 
     @pl.when(step == 0)
@@ -199,35 +223,42 @@
 
     @pl.when(step < steps)
     def _():
-        turned = rows_ref[...].T
-        grads = (gate_ref[...] * grad_ref[...].astype(WIDE_TYPE)).astype(NARROW_TYPE)
+        turned = slot_rows_of(rows_ref).T
+        cotangent = slot_rows_of(grad_ref).astype(WIDE_TYPE)
+        grads = (slot_gates_of(rows_ref) * cotangent).astype(NARROW_TYPE)
         for block in range(count):
             units = slice(block * width, (block + 1) * width)
             totals[block] += contract(turned, grad_pre_ref[:, units], 1, 0)
             totals[count + block] += contract(hidden_ref[:, units], grads, 0, 0)
 
-    @pl.when(step >= steps)
+    @pl.when(jnp.logical_and(step >= steps, step < steps + 2 * count))
     def _():
-        sums_ref[...] = totals[jnp.maximum(step - steps, 0)].astype(NARROW_TYPE)
-
-
-def routed_sums(rows, grads, gates, hidden, grad_pre, side, after, block=512):
-    total_rows, width = rows.shape
+        sums_ref[...] = totals[jnp.clip(step - steps, 0, 2 * count - 1)].astype(NARROW_TYPE)
+
+    if len(refs) == 3:
+
+        @pl.when(step == steps + 2 * count)
+        def _():
+            sums_ref[...] = refs[0][...]
+
+
+def routed_sums(rows, grads, hidden, grad_pre, side, after, extra=(), parts=4):
+    sources, _, width = rows.shape
     half = hidden.shape[1] // 2
     count = half // width
-    steps = total_rows // block
-
-    def spec(columns, place):
-        return pl.BlockSpec((block, columns), lambda step: (jnp.minimum(step, steps - 1), place))
-
+    steps = sources // parts
+    slots = pl.BlockSpec(
+        (parts,) + rows.shape[1:], lambda step: (jnp.minimum(step, steps - 1), 0, 0)
+    )
+    units = pl.BlockSpec((parts * CAP, half), lambda step: (jnp.minimum(step, steps - 1), side))
     square = (width, width)
     return stepped(
         functools.partial(sums_kernel, steps),
-        steps + 2 * count,
-        (rows, grads, gates, hidden, grad_pre),
-        [spec(width, 0), spec(width, 0), spec(1, 0), spec(half, side), spec(half, side)],
+        steps + 2 * count + len(extra),
+        (rows, grads, hidden, grad_pre, *extra),
+        [slots, slots, units, units] + [whole_block(block) for block in extra],
         pl.BlockSpec(square, lambda step: (0, jnp.maximum(step - steps, 0))),
-        jax.ShapeDtypeStruct((width, 2 * half), NARROW_TYPE),
+        jax.ShapeDtypeStruct((width, 2 * half + len(extra) * width), NARROW_TYPE),
         after,
         "routed_sums",
         scratch_shapes=[pltpu.VMEM((2 * count,) + square, WIDE_TYPE)],
@@ -330,7 +361,7 @@
             scratch_shapes=[pltpu.VMEM((2 * count, width, width), WIDE_TYPE)],
         ),
         out_shape=[wide, wide] + [jax.ShapeDtypeStruct((4, width, width), NARROW_TYPE)] * 2,
-        compiler_params=pltpu.CompilerParams(vmem_limit_bytes=60 * MEBI),
+        compiler_params=pltpu.CompilerParams(vmem_limit_bytes=61 * MEBI),
         name="shared_expert",
     )(own_core(), rows, grads, weights, weights, *after)
 
@@ -378,7 +409,7 @@
         in_specs=list(in_specs) + [ANYWHERE] * len(after),
         out_specs=out_specs,
         out_shape=out_shape,
-        compiler_params=pltpu.CompilerParams(vmem_limit_bytes=58 * MEBI),
+        compiler_params=pltpu.CompilerParams(vmem_limit_bytes=61 * MEBI),
         name=name,
         **extra,
     )(*operands, *after)
@@ -438,7 +469,7 @@
             out_specs=pl.BlockSpec((1, 8, rows, columns), lambda part, order: (part, 0, 0, 0)),
         ),
         out_shape=jax.ShapeDtypeStruct((depth, 8, rows, columns), near.dtype),
-        compiler_params=pltpu.CompilerParams(vmem_limit_bytes=40 * MEBI),
+        compiler_params=pltpu.CompilerParams(vmem_limit_bytes=61 * MEBI),
         name="place_slices",
     )(order, near, far)
     return placed.reshape(depth * 8 * rows, columns)
@@ -477,22 +508,25 @@
             out_specs=[flat] * 4,
         ),
         out_shape=[jax.ShapeDtypeStruct((rows, width), WIDE_TYPE)] + [narrow] * 3,
-        compiler_params=pltpu.CompilerParams(vmem_limit_bytes=40 * MEBI),
+        compiler_params=pltpu.CompilerParams(vmem_limit_bytes=61 * MEBI),
         name="pair_sum",
     )(place, kept, other, *after)
+
+
+def side_flips(sides):
+    return [flip(side, mask) for side, mask in zip(sides, SIDES)]
 
 
 def side_sum(own, *sides, after=(), columns=256):
     rows, width = own.shape
     flat = pl.BlockSpec((rows, columns), lambda step, *_: (0, step))
-    sides = [flip(side, mask) for side, mask in zip(sides, SIDES)]
     return pl.pallas_call(
         finish_kernel,
         grid=(width // columns,),
         in_specs=[flat] * 4 + [ANYWHERE] * len(after),
         out_specs=pl.BlockSpec((columns, rows), lambda step: (step, 0)),
         out_shape=jax.ShapeDtypeStruct((width, rows), NARROW_TYPE),
-        compiler_params=pltpu.CompilerParams(vmem_limit_bytes=40 * MEBI),
+        compiler_params=pltpu.CompilerParams(vmem_limit_bytes=61 * MEBI),
         name="side_sum",
     )(own, *sides, *after)
 
@@ -536,13 +570,16 @@
         write(sent_ref)
 
 
-def last_gradients(grad_joined, first_in, grad_attention, attended, grad_logits, second_in):
+def last_gradients(grad_joined, first_in, grad_attention, attended, grad_logits, second_in, after):
     count, width = first_in.shape
     rows = width // 2 + 16
     flat = pl.BlockSpec((count, width), lambda step, core: (0, 0))
     thin = pl.BlockSpec((count, grad_logits.shape[1]), lambda step, core: (0, 0))
+    def kernel(*refs):
+        last_kernel(*refs[:7], *refs[7 + len(after) :])
+
     return pl.pallas_call(
-        last_kernel,
+        kernel,
         grid_spec=pltpu.PrefetchScalarGridSpec(
             num_scalar_prefetch=1,
             grid=(12,),
@@ -553,7 +590,8 @@
                 flat,
                 thin,
                 flat,
-            ],
+            ]
+            + [ANYWHERE] * len(after),
             out_specs=part_specs(4, rows, width),
             scratch_shapes=[
                 pltpu.VMEM((4 * width, width), WIDE_TYPE),
@@ -561,9 +599,9 @@
             ],
         ),
         out_shape=[jax.ShapeDtypeStruct((4, rows, width), NARROW_TYPE)] * 2,
-        compiler_params=pltpu.CompilerParams(vmem_limit_bytes=56 * MEBI),
+        compiler_params=pltpu.CompilerParams(vmem_limit_bytes=61 * MEBI),
         name="last_gradients",
-    )(own_core(), grad_joined, first_in, grad_attention, attended, grad_logits, second_in)
+    )(own_core(), grad_joined, first_in, grad_attention, attended, grad_logits, second_in, *after)
 
 
 def depth_shift(value, shift):
@@ -629,6 +667,7 @@
             out_specs=pl.BlockSpec((depth, rows, columns), lambda step, place: (0, 0, 0)),
         ),
         out_shape=jax.ShapeDtypeStruct((depth, rows, columns), NARROW_TYPE),
+        compiler_params=pltpu.CompilerParams(vmem_limit_bytes=61 * MEBI),
         name="first_payload",
     )(place, qkv, out, router, cond)
 
@@ -666,6 +705,7 @@
             out_specs=pl.BlockSpec(shape, lambda step, place: (0, 0)),
         ),
         out_shape=jax.ShapeDtypeStruct(shape, NARROW_TYPE),
+        compiler_params=pltpu.CompilerParams(vmem_limit_bytes=61 * MEBI),
         name="rest_payload",
     )(place, up, down.reshape(4, local, width), *after)
 
@@ -692,6 +732,7 @@
         in_specs=[whole, whole] + [ANYWHERE] * len(after),
         out_specs=whole,
         out_shape=jax.ShapeDtypeStruct((local, hidden + 4 * down.shape[1]), up.dtype),
+        compiler_params=pltpu.CompilerParams(vmem_limit_bytes=61 * MEBI),
         name="expert_payload",
     )(up, down, *after)
 
@@ -730,21 +771,24 @@
             gradient = grad_ref[rows, :].astype(WIDE_TYPE) * mods_ref[part, 5:6, :]
             shared_ref[rows, :] = gradient.astype(NARROW_TYPE)
 
-    taken = one(pick_slots(step * CAP, CAP, places_ref))
-    out_ref[0, :CAP] = contract(taken, shared_ref[...], 1, 0).astype(NARROW_TYPE)
-    out_ref[0, CAP:] = jnp.zeros((SPARE, out_ref.shape[2]), NARROW_TYPE)
-    out_ref[0, CAP:, : silu_ref.shape[1]] = silu_ref[...]
+    parts = out_ref.shape[0]
+    taken = one(pick_slots(step * parts * CAP, parts * CAP, places_ref))
+    rows = contract(taken, shared_ref[...], 1, 0).astype(NARROW_TYPE)
+    for part in range(parts):
+        out_ref[part, :CAP] = rows[part * CAP : (part + 1) * CAP]
+        out_ref[part, CAP:] = jnp.zeros((SPARE, out_ref.shape[2]), NARROW_TYPE)
+        out_ref[part, CAP:, : silu_ref.shape[1]] = silu_ref[...]
 
 
 def slot_block(width):
-    return pl.BlockSpec((1, CAP + SPARE, width), lambda step: (step, 0, 0))
+    return pl.BlockSpec((2, CAP + SPARE, width), lambda step: (step, 0, 0))
 
 
 def spread_mixture(out_grad, mods, places, silu, after):
     count, width = out_grad.shape
     return stepped(
         mixture_kernel,
-        8,
+        4,
         (out_grad, mods, places, silu),
         [whole_block(operand) for operand in (out_grad, mods, places, silu)],
         [pl.BlockSpec((count, width), lambda step: (0, 0)), slot_block(width)],
@@ -767,8 +811,8 @@
         joined_ref[part] = contract(first, weight_ref[:, columns], 1, 0).astype(NARROW_TYPE)
 
 
-def mods_block(mods):
-    return pl.BlockSpec((1,) + mods.shape[1:], lambda step, *_: (step, 0, 0))
+def mods_block(mods, quarters=1):
+    return pl.BlockSpec((quarters,) + mods.shape[1:], lambda step, *_: (step, 0, 0))
 
 
 def first_half(patches, mods, weights, after):
@@ -847,21 +891,26 @@
 
 
 def spread_kernel(second_ref, places_ref, gates_ref, rows_ref):
-    slots = pick_slots(pl.program_id(0) * CAP, CAP, places_ref)
-    rows_ref[0, :CAP] = contract(one(slots), second_ref[...], 1, 0).astype(NARROW_TYPE)
-    slot = pl.program_id(0) * CAP + lax.broadcasted_iota(jnp.int32, slots.shape, 0)
+    parts = rows_ref.shape[0]
+    first = pl.program_id(0) * parts * CAP
+    slots = pick_slots(first, parts * CAP, places_ref)
+    rows = contract(one(slots), second_ref[...], 1, 0).astype(NARROW_TYPE)
+    slot = first + lax.broadcasted_iota(jnp.int32, slots.shape, 0)
     total = jnp.where(slot == places_ref[0:1, :], gates_ref[0:1, :], 0.0)
     total += jnp.where(slot == places_ref[1:2, :], gates_ref[1:2, :], 0.0)
     column = jnp.sum(total, axis=1, keepdims=True)
-    gates = jnp.broadcast_to(column, (CAP, 128)).T[0:SPARE, :]
+    gates = jnp.broadcast_to(column, (parts * CAP, 128)).T[0:SPARE, :]
     row = lax.broadcasted_iota(jnp.int32, gates.shape, 0)
     terms = jnp.zeros(gates.shape, WIDE_TYPE)
     for number in range(3):
         term = gates.astype(NARROW_TYPE).astype(WIDE_TYPE)
         terms = jnp.where(row == number, term, terms)
         gates = gates - term
-    rows_ref[0, CAP:] = jnp.zeros((SPARE, rows_ref.shape[2]), NARROW_TYPE)
-    rows_ref[0, CAP:, :CAP] = terms.astype(NARROW_TYPE)
+    for part in range(parts):
+        own = slice(part * CAP, (part + 1) * CAP)
+        rows_ref[part, :CAP] = rows[own]
+        rows_ref[part, CAP:] = jnp.zeros((SPARE, rows_ref.shape[2]), NARROW_TYPE)
+        rows_ref[part, CAP:, :CAP] = terms[:, own].astype(NARROW_TYPE)
 
 
 def spread_second(second_in, places, gates, after):
@@ -869,7 +918,7 @@
     operands = (second_in, places, gates)
     return stepped(
         spread_kernel,
-        8,
+        4,
         operands,
         [whole_block(operand) for operand in operands],
         slot_block(width),
@@ -880,7 +929,8 @@
 
 
 def middle_kernel(
-    back_ref,
+    left_ref,
+    right_ref,
     dots_ref,
     columns_ref,
     routes_ref,
@@ -898,10 +948,14 @@
     grad_logits_ref,
     sums_ref,
 ):
-    quarter, width = middle_ref.shape
-    slot = lax.broadcasted_iota(jnp.int32, (quarter, back_ref.shape[0]), 1)
+    count, width = middle_ref.shape
+    quarters = mods_ref.shape[0]
+    quarter = count // quarters
+    slot = lax.broadcasted_iota(jnp.int32, (count, left_ref.shape[0]), 1)
     takes = [slot == columns_ref[:, k : k + 1] for k in range(TOP)]
-    collected = contract(one(jnp.logical_or(*takes)), back_ref[...], 1, 0)
+    taken = one(jnp.logical_or(*takes))
+    collected = [contract(taken, ref[...], 1, 0) for ref in (left_ref, right_ref)]
+    collected = jnp.concatenate(collected, axis=1)
     gates = [gates_ref[:, k : k + 1] for k in range(TOP)]
     grad_gate = [
         jnp.sum(jnp.where(take, dots_ref[...], 0.0), axis=1, keepdims=True) for take in takes
@@ -917,41 +971,53 @@
     grad_second = shared_ref[...] + contract(grad_logits, router_ref[...], 1, 1) + collected
     normed, reciprocal = normalize_rows(middle_ref[...])
     grad_middle = grad_ref[...].astype(WIDE_TYPE) + normalize_rows_back(
-        grad_second * (1.0 + mods_ref[0, 4:5, :]), normed, reciprocal
+        grad_second * (1.0 + mods_rows(mods_ref, 4, quarter)), normed, reciprocal
     )
     grad_middle_ref[...] = grad_middle
-    grad_attention = (grad_middle * mods_ref[0, 2:3, :]).astype(NARROW_TYPE)
+    grad_attention = (grad_middle * mods_rows(mods_ref, 2, quarter)).astype(NARROW_TYPE)
     grad_attention_ref[...] = grad_attention
     grad_attended_ref[...] = contract(grad_attention, out_ref[...], 1, 1).astype(NARROW_TYPE)
-    sums_ref[0] = jnp.concatenate(
-        [
-            jnp.sum(grad_middle * attention_ref[...], axis=0, keepdims=True),
-            jnp.sum(grad_second, axis=0, keepdims=True),
-            jnp.sum(grad_second * normed, axis=0, keepdims=True),
-        ],
-        axis=0,
-    )
-
-
-def sums_block(count, width):
-    return pl.BlockSpec((1, count, width), lambda step: (step, 0, 0))
+    totals = [grad_middle * attention_ref[...], grad_second, grad_second * normed]
+    totals = [quarter_sums(total, quarters) for total in totals]
+    for part in range(quarters):
+        sums_ref[part] = jnp.concatenate([total[part] for total in totals], axis=0)
+
+
+def sums_block(count, width, quarters=1):
+    return pl.BlockSpec((quarters, count, width), lambda step: (step, 0, 0))
+
+
+def mods_rows(mods_ref, piece, quarter):
+    parts = [
+        jnp.broadcast_to(mods_ref[part, piece : piece + 1, :], (quarter, mods_ref.shape[2]))
+        for part in range(mods_ref.shape[0])
+    ]
+    return jnp.concatenate(parts, axis=0)
+
+
+def quarter_sums(values, quarters):
+    rows = values.shape[0] // quarters
+    return [
+        jnp.sum(values[part * rows : (part + 1) * rows], axis=0, keepdims=True)
+        for part in range(quarters)
+    ]
 
 
 def middle_back(
-    back, dots, columns, routes, gates, grad_shared, middle, attention, mods, out_grad, weights, after
+    left, right, dots, columns, routes, gates, grad_shared, middle, attention, mods, out_grad, weights, after
 ):
     count, width = middle.shape
-    quarter = count // 4
-    rows, pair, lanes = row_block(quarter, width), row_block(quarter, TOP), row_block(quarter, 128)
+    half = count // 2
+    rows, pair, lanes = row_block(half, width), row_block(half, TOP), row_block(half, 128)
     narrow = jax.ShapeDtypeStruct((count, width), NARROW_TYPE)
     return stepped(
         middle_kernel,
-        4,
-        (back, dots, columns, routes, gates, grad_shared, middle, attention, mods, out_grad, weights, weights),
-        [whole_block(back), whole_block(dots), pair, pair, pair, rows, rows, rows]
-        + [mods_block(mods), rows]
+        2,
+        (left, right, dots, columns, routes, gates, grad_shared, middle, attention, mods, out_grad, weights, weights),
+        [whole_block(left), whole_block(right), whole_block(dots), pair, pair, pair, rows, rows, rows]
+        + [mods_block(mods, 2), rows]
         + [column_block(weights, width, 3), column_block(weights, 128, 4 * width // 128)],
-        [rows, rows, rows, lanes, sums_block(3, width)],
+        [rows, rows, rows, lanes, sums_block(3, width, 2)],
         [
             jax.ShapeDtypeStruct((count, width), WIDE_TYPE),
             narrow,
@@ -967,24 +1033,28 @@
 def output_kernel(
     result_ref, columns_ref, shared_ref, middle_ref, mods_ref, grad_ref, out_ref, sums_ref
 ):
-    quarter = middle_ref.shape[0]
-    slot = lax.broadcasted_iota(jnp.int32, (quarter, result_ref.shape[0]), 1)
+    count = middle_ref.shape[0]
+    quarters = mods_ref.shape[0]
+    slot = lax.broadcasted_iota(jnp.int32, (count, result_ref.shape[0]), 1)
     takes = [slot == columns_ref[:, k : k + 1] for k in range(TOP)]
     mixture = shared_ref[...] + contract(one(jnp.logical_or(*takes)), result_ref[...], 1, 0)
-    out_ref[...] = (middle_ref[...] + mods_ref[0, 5:6, :] * mixture).astype(NARROW_TYPE)
-    sums_ref[0] = jnp.sum(grad_ref[...].astype(WIDE_TYPE) * mixture, axis=0, keepdims=True)
+    gate = mods_rows(mods_ref, 5, count // quarters)
+    out_ref[...] = (middle_ref[...] + gate * mixture).astype(NARROW_TYPE)
+    totals = quarter_sums(grad_ref[...].astype(WIDE_TYPE) * mixture, quarters)
+    for part in range(quarters):
+        sums_ref[part] = totals[part]
 
 
 def block_output(result, columns, shared, middle, mods, out_grad, after):
     count, width = middle.shape
-    quarter = count // 4
-    rows, pair = row_block(quarter, width), row_block(quarter, TOP)
+    half = count // 2
+    rows, pair = row_block(half, width), row_block(half, TOP)
     return stepped(
         output_kernel,
-        4,
+        2,
         (result, columns, shared, middle, mods, out_grad),
-        [whole_block(result), pair, rows, rows, mods_block(mods), rows],
-        [rows, sums_block(1, width)],
+        [whole_block(result), pair, rows, rows, mods_block(mods, 2), rows],
+        [rows, sums_block(1, width, 2)],
         [
             jax.ShapeDtypeStruct((count, width), NARROW_TYPE),
             jax.ShapeDtypeStruct((4, 1, width), WIDE_TYPE),
@@ -1059,7 +1129,7 @@
         expert_sums_kernel,
         1,
         (early, late),
-        [whole_block(early), whole_block(late)],
+        [whole_block(early), column_block(late, hidden, 0)],
         [
             pl.BlockSpec((local, hidden), lambda step: (0, 0)),
             pl.BlockSpec((4 * local, width), lambda step: (0, 0)),
@@ -1197,28 +1267,31 @@
         second_in, grad_shared, rest, local, (slot_rows,)
     )
     sent, slots_there = together(sent, slots_there)
-    gates_there = jnp.sum(slots_there[:, capacity : capacity + 3, :capacity].astype(WIDE_TYPE), axis=1)
-    routed = (
-        slots_there[:, :capacity].reshape(slots, width),
-        mixture_slots[:, :capacity].reshape(slots, width),
-        gates_there.reshape(slots, 1),
-    )
+    routed = (slots_there, mixture_slots)
     silu_all = mixture_slots[:, capacity:, : silu_parts.size // SPARE]
     silu_all = silu_all.reshape(experts, depth, cond_rows, local)
     silu_all = jnp.transpose(silu_all, (1, 0, 2, 3)).reshape(depth * experts * cond_rows, local)
-    result_rows, grad_rows, gate_dots, units, grad_units = routed_expert(
-        *routed, expert_weights, ()
-    )
-    grad_rows_back = exchange(grad_rows.reshape(experts, capacity, width)).reshape(slots, width)
+    middle_own, *middle_sides = pair_sum(kept, flip(sent, CORE))
+    middle_sides = side_flips(middle_sides)
+    result_rows, *grad_rows, gate_dots, units, grad_units = routed_expert(
+        *routed, expert_weights, (middle_own,)
+    )
+    *middle_sides, left, right = together(*middle_sides, *grad_rows)
+    left_back = exchange(left.reshape(experts, capacity, width // 2))
+    left_back, gate_dots = together(left_back, gate_dots)
+    left_back = left_back.reshape(slots, width // 2)
     gate_dots_back = exchange(gate_dots.reshape(experts, 1, capacity)).reshape(1, slots)
     early_sums = routed_sums(*routed, units, grad_units, 0, ())
-    early_sums, gate_dots_back = together(early_sums, gate_dots_back)
+    early_sums, left_back = together(early_sums, left_back)
     early_final = lax.psum_scatter(early_sums, "dp", scatter_dimension=0, tiled=True)
-    late_sums = routed_sums(*routed, units, grad_units, 1, (early_sums,))
-    middle_own, *middle_sides = pair_sum(kept, flip(sent, CORE), (late_sums,))
+    middle_sum = side_sum(middle_own, *middle_sides, after=(early_sums,))
+    right, middle_sum = together(right, middle_sum)
+    right_back = exchange(right.reshape(experts, capacity, width // 2)).reshape(slots, width // 2)
+    late_sums = routed_sums(*routed, units, grad_units, 1, (early_sums,), (middle_sum,))
 
     grad_middle, grad_attention, grad_attended, grad_logits, middle_sums = middle_back(
-        grad_rows_back,
+        left_back,
+        right_back,
         gate_dots_back,
         columns,
         routes,
@@ -1231,14 +1304,13 @@
         first_full,
         (silu_all,),
     )
-    late_sums, *middle_sides, grad_attended = together(late_sums, *middle_sides, grad_attended)
+    late_sums, grad_attended = together(late_sums, grad_attended)
     late_final = lax.psum_scatter(late_sums, "dp", scatter_dimension=0, tiled=True)
     result_back = exchange(result_rows.reshape(experts, capacity, width)).reshape(slots, width)
     grad_joined = attend_back(long_pack, joined, log_total, grad_attended, ())
     last_parts = last_gradients(
-        grad_joined, first_in, grad_attention, attended, grad_logits, second_in
-    )
-    middle_sum = side_sum(middle_own, *middle_sides, after=(grad_joined,))
+        grad_joined, first_in, grad_attention, attended, grad_logits, second_in, (result_back,)
+    )
     block_out, output_sums = block_output(
         result_back,
         columns,
@@ -1246,20 +1318,13 @@
         middle,
         mods,
         out_grad,
-        (*last_parts, middle_sum, early_final),
-    )
-    middle_final = lax.psum_scatter(middle_sum, "dp", scatter_dimension=0, tiled=True)
-    middle_final = middle_final.astype(WIDE_TYPE)
-    shared_up_grad = middle_final[:, : hidden // experts]
-    shared_down_grad = jnp.transpose(
-        middle_final[:, hidden // experts :].reshape(local, 4, width // experts), (1, 0, 2)
-    ).reshape(4 * local, width // experts)
-
-    last_pair = pair_sum(last_parts[0], flip(last_parts[1], CORE))
+        (*last_parts, early_final),
+    )
+    last_pair = pair_sum(last_parts[0], flip(last_parts[1], CORE), (output_sums,))
     patches_grad, start_sums = start_back(
         grad_joined, first_full, patches, mods, grad_middle, tuple(last_pair)
     )
-    last_sum = side_sum(*last_pair)
+    last_sides = side_flips(last_pair[1:])
     grad_chosen = jnp.concatenate([start_sums, middle_sums, output_sums], axis=1)
     grad_chosen = grad_chosen.reshape(1, 4, 6 * width)
     long_total = jnp.sum(grad_chosen, axis=1, keepdims=True)
@@ -1269,6 +1334,8 @@
     everyone = ("dp",) + PLANE
     columns = 6 * width // experts
     grad_columns = jnp.transpose(grad_modulation.reshape(cond_rows, experts, columns), (1, 0, 2))
+    *last_sides, grad_columns = together(*last_sides, grad_columns)
+    last_sum = side_sum(last_pair[0], *last_sides)
     grad_columns = jnp.broadcast_to(grad_columns[None], (depth, experts, cond_rows, columns))
     grad_columns = lax.all_to_all(
         grad_columns.reshape(depth * experts, cond_rows, columns),
@@ -1277,9 +1344,10 @@
         concat_axis=0,
         tiled=True,
     ).reshape(depth * experts * cond_rows, columns)
+    grad_columns, last_sum = together(grad_columns, last_sum)
     ada_weight_grad = product_left_operand(silu_all, grad_columns)
     own_ada = lax.dynamic_slice_in_dim(ada_weight, plane_index * columns, columns, 1)
-    silu_back, last_sum = together(product_right_operand(grad_columns, own_ada), last_sum)
+    silu_back = product_right_operand(grad_columns, own_ada)
     silu_back = lax.all_to_all(
         silu_back.reshape(depth * experts, cond_rows, local),
         everyone,
@@ -1287,6 +1355,7 @@
         concat_axis=0,
         tiled=True,
     )
+    silu_back, late_final = together(silu_back, late_final)
     silu_back = jnp.sum(silu_back.reshape(depth, experts, cond_rows, local), axis=1)
     grad_silu = jnp.transpose(silu_back, (1, 0, 2)).reshape(cond_rows, width)
     cond_grad = jax.vjp(jax.nn.silu, cond_wide)[1](grad_silu)[0]
@@ -1296,6 +1365,11 @@
     out_weight_grad = last_final[:, edge_one:edge_two]
     router_weight_grad = last_final[:, edge_two : edge_two + 1]
 
+    middle_final = late_final[:, hidden:].astype(WIDE_TYPE)
+    shared_up_grad = middle_final[:, : hidden // experts]
+    shared_down_grad = jnp.transpose(
+        middle_final[:, hidden // experts :].reshape(local, 4, width // experts), (1, 0, 2)
+    ).reshape(4 * local, width // experts)
     expert_up_grad, expert_down_grad = expert_sums(early_final, late_final)
     return (
         block_out,

time: 625 us -> 585 us (0.936)
  local copies, waits for them, and re-layouts: 44.7 us -> 22.6 us
  waiting for transfers between devices: 123 us -> 104 us
    all_to_all x5 -> x6, waiting for transfers between devices: 22.4 us -> 8.37 us  [exchange(): return lax.all_to_all(rows, PLANE, split_axis=0, concat_axis=0, tiled=True)]
    ppermute x3, waiting for transfers between devices: 23.7 us -> 10.1 us  [depth_shift(): lax.ppermute(value, 'dp', [(index, (index + shift) % depth) for index in...]
    unnamed x51 -> x33, local copies, waits for them, and re-layouts: 18.4 us -> 6.72 us
    slice x3 -> x1, local copies, waits for them, and re-layouts: 9.03 us -> 0.29 us  [the longest x1 4.43 us: on_device(): mixture_slots[:, :capacity].reshape(slots, width)]
    all_to_all x1, waiting for transfers between devices: 0.01 us -> 8.44 us  [on_device(): lax.all_to_all(grad_columns.reshape(depth * experts, cond_rows, columns),...]
    pallas_call x1, Pallas kernels: 33.5 us -> 26.1 us  [attend(): pl.pallas_call(attend_kernel, grid=(width // 128,), in_specs=[pl.BlockSpe...]
    all_to_all x5 -> x6, starting transfers between devices: 22.6 us -> 25.9 us  [exchange(): return lax.all_to_all(rows, PLANE, split_axis=0, concat_axis=0, tiled=True)]
  transfers between devices with their start and end apart: 33 -> 33, of which waited for: 16 -> 16; matrix products, arithmetic and copies ran while one was open for 6% -> 4% of each run, Pallas kernels for 46% -> 61%
where the time goes in v3:
time: 585 us; the launch traced here: 577 us
  Pallas kernels  357 us (61%)
  waiting for transfers between devices  104 us (18%)
  starting transfers between devices  65.6 us (11%)
  local copies, waits for them, and re-layouts  22.6 us (4%)
  between operations  15.2 us (3%)
  other arithmetic  8.38 us (1%)
    pallas_call x13, Pallas kernels, stepped(): pl.pallas_call(body, grid=(steps,), in_specs=list(in_specs) + [ANYWHERE]...  190 us
    ppermute x16, waiting for transfers between devices, flip(): lax.ppermute(value, PLANE, [(index, index ^ mask) for index in range(coun...  59.7 us
    pallas_call x1, Pallas kernels, shared_expert(): pl.pallas_call(kernel, grid_spec=pltpu.PrefetchScalarGridSpec(num_scalar_...  44.3 us
    pallas_call x1, Pallas kernels, attend_back(): pl.pallas_call(attend_back_kernel, grid=(width // 128,), in_specs=[pl.Blo...  40.7 us
    pallas_call x1, Pallas kernels, attend(): pl.pallas_call(attend_kernel, grid=(width // 128,), in_specs=[pl.BlockSpe...  26.1 us
    all_to_all x6, starting transfers between devices, exchange(): return lax.all_to_all(rows, PLANE, split_axis=0, concat_axis=0, tiled=True)  25.9 us
    ppermute x16, starting transfers between devices, flip(): lax.ppermute(value, PLANE, [(index, index ^ mask) for index in range(coun...  15.2 us
    pallas_call x2, Pallas kernels, plane_gather(): pl.pallas_call(place_kernel, grid_spec=pltpu.PrefetchScalarGridSpec(num_s...  14.7 us
  transfers between devices with their start and end apart: 33, of which 16 were waited for; matrix products, arithmetic and copies ran while one was open for 4% of the time, Pallas kernels for 61%

profile of v3, /device:TPU:0, one launch (start us, length us, event | category | flops | bytes accessed | tf_op | source)
XLA Modules:
  0.0 576.6 jit_solution(14182662269051856101)
XLA Ops:
  10.6 6.3 %all-to-all-start = ((bf16[4,24,3456]{2,1,0:T(8,128)(2,1)}), bf16[4,24,3456]{2,1,0:T(8,128)(2,1)S(1)}, u32[]{:S(2)}, u32[]{:S(2)}) async-start(bf16[4,24,3456]{2,1,0:T(8,128)(2,1)} %first_payload.1), calls=%async_computation | async-start | bytes 1327104 | tf_op jit(solution)/shard_map/all_to_all | solution.py:1195
  17.7 2.3 reduce-window.6
  25.0 3.4 expert_payload.1.refs_2_
  28.4 6.0 %all-to-all-done.refs_0_ = bf16[4,24,3456]{2,1,0:T(8,128)(2,1)S(1)} async-done(((bf16[4,24,3456]{2,1,0:T(8,128)(2,1)}), bf16[4,24,3456]{2,1,0:T(8,128)(2,1)S(1)}, u32[]{:S(2)}, u32[]{:S(2)}) %all-to-all-start) | async-done | bytes 663584 | tf_op jit(solution)/shard_map/all_to_all | solution.py:1195
  38.9 3.5 all-to-all-start.1
  47.2 10.0 %all-to-all-done.1 = f32[4,4,4608]{2,1,0:T(4,128)S(1)} async-done(((f32[4,4,4608]{2,1,0:T(4,128)}), f32[4,4,4608]{2,1,0:T(4,128)S(1)}, u32[]{:S(2)}, u32[]{:S(2)}) %all-to-all-start.1) | async-done | bytes 294944 | tf_op jit(solution)/shard_map/all_to_all | solution.py:1235
  58.1 8.2 %spread_mixture.1 = (bf16[1024,768]{1,0:T(8,128)(2,1)}, bf16[8,336,768]{2,1,0:T(8,128)(2,1)}) custom-call(bf16[1024,768]{1,0:T(8,128)(2,1)} %refs_5_.1, f32[4,6,768]{2,1,0:T(8,128)} %broadcast_select_fusion.refs_1_.refs_2_.refs_9_.refs_4_.refs_3_, s32[2,1024]{1,0:T(2,128)} %copy.108.refs_2_.refs_1_, bf16[16,192]{1,0:T(8,128)(2,1)} %reshape.178.refs_3_), custom_call_target="tpu_custom_call" | custom-call | tf_op jit(solution)/shard_map/spread_mixture/pallas_call | solution.py:406
  66.3 4.5 all-to-all-start.2
  71.1 13.4 %collective-permute-done.1.refs_2_ = bf16[4,24,3456]{2,1,0:T(8,128)(2,1)} collective-permute-done((bf16[4,24,3456]{2,1,0:T(8,128)(2,1)S(1)}, bf16[4,24,3456]{2,1,0:T(8,128)(2,1)}, u32[]{:S(2)}, u32[]{:S(2)}) %collective-permute-start.1) | collective-permute-done | bytes 663584 | tf_op jit(solution)/shard_map/ppermute | solution.py:375
  84.5 4.0 stack_sides.2.near_ref
  88.7 2.9 collective-permute-start.5
  93.9 6.4 %place_slices.2 = bf16[4,8,24,3456]{3,2,1,0:T(8,128)(2,1)} custom-call(s32[5]{0:T(128)} %stack.26.order_ref, bf16[4,4,24,3456]{3,2,1,0:T(8,128)(2,1)} %stack_sides.2.near_ref, bf16[4,4,24,3456]{3,2,1,0:T(8,128)(2,1)} %collective-permute-done.3.far_ref), custom_call_target="tpu_custom_call" | custom-call | tf_op jit(solution)/shard_map/place_slices/pallas_call | solution.py:463
  100.3 8.8 %first_half.1 = (bf16[1024,768]{1,0:T(8,128)(2,1)}, bf16[3,1024,768]{2,1,0:T(8,128)(2,1)}) custom-call(bf16[1024,768]{1,0:T(8,128)(2,1)} %refs_2_.1, f32[4,6,768]{2,1,0:T(8,128)} %broadcast_select_fusion.refs_1_.refs_2_.refs_9_.refs_4_.refs_3_, bf16[768,3456]{1,0:T(8,128)(2,1)} %bitcast.66), custom_call_target="tpu_custom_call" | custom-call | tf_op jit(solution)/shard_map/first_half/pallas_call | solution.py:406
  109.1 26.1 %attend.1 = (bf16[1024,768]{1,0:T(8,128)(2,1)}, f32[1024,768]{1,0:T(8,128)}) custom-call(s32[1]{0:T(128)S(6)} %copy.131.long_ref, bf16[3,1024,768]{2,1,0:T(8,128)(2,1)} %get-tuple-element.82.joined_ref), custom_call_target="tpu_custom_call" | custom-call | tf_op jit(solution)/shard_map/attend/pallas_call | solution.py:73
  135.2 7.3 %second_half.1 = (f32[1024,768]{1,0:T(8,128)}, f32[1024,768]{1,0:T(8,128)}, bf16[1024,768]{1,0:T(8,128)(2,1)}, f32[1024,2]{1,0:T(8,128)}, f32[2,1024]{1,0:T(2,128)}) custom-call(bf16[1024,768]{1,0:T(8,128)(2,1)} %get-tuple-element.84.refs_0_.refs_4_, bf16[1024,768]{1,0:T(8,128)(2,1)} %refs_2_.1, ...), custom_call_target="tpu_custom_call" | custom-call | tf_op jit(solution)/shard_map/second_half/pallas_call | solution.py:406
  142.4 8.6 %spread_second.1.refs_5_ = bf16[8,336,768]{2,1,0:T(8,128)(2,1)} custom-call(bf16[1024,768]{1,0:T(8,128)(2,1)} %get-tuple-element.85.refs_0_.refs_1_.refs_6_, s32[2,1024]{1,0:T(2,128)} %copy.108.refs_2_.refs_1_, f32[2,1024]{1,0:T(2,128)} %get-tuple-element.87.refs_2_), custom_call_target="tpu_custom_call" | custom-call | tf_op jit(solution)/shard_map/spread_second/pallas_call | solution.py:406
  151.1 18.8 %collective-permute-done.6.refs_3_ = bf16[4,24,6144]{2,1,0:T(8,128)(2,1)} collective-permute-done((bf16[4,24,6144]{2,1,0:T(8,128)(2,1)}, bf16[4,24,6144]{2,1,0:T(8,128)(2,1)}, u32[]{:S(2)}, u32[]{:S(2)}) %collective-permute-start.6) | collective-permute-done | bytes 1179680 | tf_op jit(solution)/shard_map/ppermute | solution.py:375
  169.8 5.0 stack_sides.3.near_ref
  174.8 4.6 all-to-all-start.3
  179.4 3.7 collective-permute-done.7.far_ref
  183.1 8.3 %place_slices.3 = bf16[4,8,24,6144]{3,2,1,0:T(8,128)(2,1)} custom-call(s32[5]{0:T(128)} %stack.26.order_ref, bf16[4,4,24,6144]{3,2,1,0:T(8,128)(2,1)} %stack_sides.3.near_ref, bf16[4,4,24,6144]{3,2,1,0:T(8,128)(2,1)} %collective-permute-done.7.far_ref), custom_call_target="tpu_custom_call" | custom-call | tf_op jit(solution)/shard_map/place_slices/pallas_call | solution.py:463
  191.4 44.3 %shared_expert.1 = (f32[1024,768]{1,0:T(8,128)}, f32[1024,768]{1,0:T(8,128)}, bf16[4,768,768]{2,1,0:T(8,128)(2,1)}, bf16[4,768,768]{2,1,0:T(8,128)(2,1)}) custom-call(s32[1]{0:T(128)} %bitcast.refs_0_, bf16[1024,768]{1,0:T(8,128)(2,1)} %get-tuple-element.85.refs_0_.refs_1_.refs_6_, bf16[1024,768]{1,0:T(8,128)(2,1)} %get-tuple-element.86.refs_2_, ...), custom_call_target="tpu_custom_call" | custom-call | tf_op jit(solution)/shard_map/shared_expert/pallas_call | solution.py:354
  235.9 8.1 %collective-permute-done.8.other_ref = bf16[4,768,768]{2,1,0:T(8,128)(2,1)} collective-permute-done((bf16[4,768,768]{2,1,0:T(8,128)(2,1)}, bf16[4,768,768]{2,1,0:T(8,128)(2,1)}, u32[]{:S(2)}, u32[]{:S(2)}) %collective-permute-start.8) | collective-permute-done | bytes 4718624 | tf_op jit(solution)/shard_map/ppermute | solution.py:375
  244.1 7.2 %pair_sum.2 = (f32[768,768]{1,0:T(8,128)}, bf16[768,768]{1,0:T(8,128)(2,1)}, bf16[768,768]{1,0:T(8,128)(2,1)}, bf16[768,768]{1,0:T(8,128)(2,1)}) custom-call(s32[1]{0:T(128)} %bitcast.4.place_ref, bf16[4,768,768]{2,1,0:T(8,128)(2,1)} %get-tuple-element.92.kept_ref, bf16[4,768,768]{2,1,0:T(8,128)(2,1)} %collective-permute-done.8.other_ref), custom_call_target="tpu_custom_call" | custom-call | tf_op jit(solution)/shard_map/pair_sum/pallas_call | solution.py:502
  256.3 61.4 %routed_expert.1 = (bf16[2560,768]{1,0:T(8,128)(2,1)}, bf16[2560,384]{1,0:T(8,128)(2,1)}, bf16[2560,384]{1,0:T(8,128)(2,1)}, f32[2560,1]{1,0:T(8,128)}, bf16[256...) custom-call(bf16[8,336,768]{2,1,0:T(8,128)(2,1)} %all-to-all-done.3.refs_0_, bf16[8,336,768]{2,1,0:T(8,128)(2,1)} %all-to-all-done.2.refs_1_, ...), custom_call_target="tpu_custom_call" | custom-call | tf_op jit(solution)/shard_map/routed_expert/pallas_call | solution.py:406
  318.7 4.3 all-to-all-start.5
  323.1 20.7 %routed_sums.2.refs_3_.refs_5_ = bf16[768,3072]{1,0:T(8,128)(2,1)} custom-call(bf16[8,336,768]{2,1,0:T(8,128)(2,1)} %all-to-all-done.3.refs_0_, bf16[8,336,768]{2,1,0:T(8,128)(2,1)} %all-to-all-done.2.refs_1_, bf16[2560,3072]{1,0:T(8,128)(2,1)} %get-tuple-element.99.refs_2_, bf16[2560,3072]{1,0:T(8,128)(2,1)} %get-tuple-element.100.refs_3_), custom_call_target="tpu_custom_call" | custom-call | tf_op jit(solution)/shard_map/routed_sums/pallas_call | solution.py:406
  343.9 3.6 all-to-all-done.5
  349.9 3.3 all-to-all-start.7
  353.2 4.7 side_sum.2.refs_4_
  357.9 4.3 all-to-all-start.6
  363.9 22.8 %routed_sums.3 = bf16[768,3840]{1,0:T(8,128)(2,1)} custom-call(bf16[8,336,768]{2,1,0:T(8,128)(2,1)} %all-to-all-done.3.refs_0_, bf16[8,336,768]{2,1,0:T(8,128)(2,1)} %all-to-all-done.2.refs_1_, bf16[2560,3072]{1,0:T(8,128)(2,1)} %get-tuple-element.99.refs_2_, bf16[2560,3072]{1,0:T(8,128)(2,1)} %get-tuple-element.100.refs_3_, ...), custom_call_target="tpu_custom_call" | custom-call | tf_op jit(solution)/shard_map/routed_sums/pallas_call | solution.py:406
  387.5 18.8 %middle_back.1 = (f32[1024,768]{1,0:T(8,128)}, bf16[1024,768]{1,0:T(8,128)(2,1)}, bf16[1024,768]{1,0:T(8,128)(2,1)}, bf16[1024,128]{1,0:T(8,128)(2,1)}, f32[4,3,768]{2,1,0:T(4,128)}) custom-call(bf16[2560,384]{1,0:T(8,128)(2,1)} %bitcast.19.refs_0_, bf16[2560,384]{1,0:T(8,128)(2,1)} %bitcast.21.refs_1_, f32[1,2560]{1,0:T(1,128)} %reshape.189.refs_2_, ...), custom_call_target="tpu_custom_call" | custom-call | tf_op jit(solution)/shard_map/middle_back/pallas_call | solution.py:406
  406.3 4.7 all-to-all-start.4
  411.0 40.7 %attend_back.1.refs_1_.refs_0_ = bf16[3,1024,768]{2,1,0:T(8,128)(2,1)} custom-call(s32[1]{0:T(128)S(6)} %copy.131.long_ref, bf16[3,1024,768]{2,1,0:T(8,128)(2,1)} %get-tuple-element.82.joined_ref, f32[1024,768]{1,0:T(8,128)} %get-tuple-element.98.total_ref, bf16[1024,768]{1,0:T(8,128)(2,1)} %get-tuple-element.122.grad_ref), custom_call_target="tpu_custom_call" | custom-call | tf_op jit(solution)/shard_map/attend_back/pallas_call | solution.py:121
  451.7 4.8 all-to-all-done.4
  456.4 13.8 %last_gradients.1 = (bf16[4,400,768]{2,1,0:T(8,128)(2,1)}, bf16[4,400,768]{2,1,0:T(8,128)(2,1)}) custom-call(s32[1]{0:T(128)} %bitcast.refs_0_, bf16[3,1024,768]{2,1,0:T(8,128)(2,1)} %attend_back.1.refs_1_.refs_0_, bf16[1024,768]{1,0:T(8,128)(2,1)} %get-tuple-element.123.refs_2_, bf16[1024,768]{1,0:T(8,128)(2,1)} %get-tuple-element.124.refs_3_, ...), custom_call_target="tpu_custom_call" | custom-call | tf_op jit(solution)/shard_map/last_gradients/pallas_call | solution.py:581
  470.2 10.6 %block_output.1 = (bf16[1024,768]{1,0:T(8,128)(2,1)}, f32[4,1,768]{2,1,0:T(1,128)}) custom-call(bf16[2560,768]{1,0:T(8,128)(2,1)} %bitcast.17.refs_7_.refs_0_, s32[1024,2]{1,0:T(8,128)} %copy-done.2, f32[1024,768]{1,0:T(8,128)} %get-tuple-element.96.refs_2_, f32[1024,768]{1,0:T(8,128)} %get-tuple-element.97.refs_7_.refs_3_, ...), custom_call_target="tpu_custom_call" | custom-call | tf_op jit(solution)/shard_map/block_output/pallas_call | solution.py:406
  480.8 4.9 pair_sum.3
  489.2 9.9 %start_back.1 = (f32[1024,768]{1,0:T(8,128)}, f32[4,2,768]{2,1,0:T(2,128)}) custom-call(bf16[3,1024,768]{2,1,0:T(8,128)(2,1)} %attend_back.1.refs_1_.refs_0_, bf16[768,3456]{1,0:T(8,128)(2,1)} %bitcast.71, bf16[1024,768]{1,0:T(8,128)(2,1)} %refs_2_.1, f32[4,6,768]{2,1,0:T(8,128)} %broadcast_select_fusion.refs_1_.refs_2_.refs_9_.refs_4_.refs_3_, ...), custom_call_target="tpu_custom_call" | custom-call | tf_op jit(solution)/shard_map/start_back/pallas_call | solution.py:406
  502.6 12.2 %collective-permute-done.14.refs_1_ = bf16[400,768]{1,0:T(8,128)(2,1)} collective-permute-done((bf16[400,768]{1,0:T(8,128)(2,1)}, bf16[400,768]{1,0:T(8,128)(2,1)}, u32[]{:S(2)}, u32[]{:S(2)}) %collective-permute-start.14) | collective-permute-done | bytes 614432 | tf_op jit(solution)/shard_map/ppermute | solution.py:375
  517.2 4.1 all-to-all-start.8
  521.3 3.7 side_sum.3
  525.1 8.4 %all-to-all-done.8 = bf16[32,4,576]{2,1,0:T(4,128)(2,1)S(1)} async-done(((bf16[32,4,576]{2,1,0:T(4,128)(2,1)}), bf16[32,4,576]{2,1,0:T(4,128)(2,1)S(1)}, u32[]{:S(2)}, u32[]{:S(2)}) %all-to-all-start.8) | async-done | bytes 147488 | tf_op jit(solution)/shard_map/all_to_all | solution.py:1340
  534.7 4.7 all-to-all-start.9
  543.4 2.4 collective-permute-start.17
  551.0 8.3 %collective-permute-done.17 = bf16[192,400]{0,1:T(8,128)(2,1)S(1)} collective-permute-done((bf16[192,400]{0,1:T(8,128)(2,1)}, bf16[192,400]{0,1:T(8,128)(2,1)S(1)}, u32[]{:S(2)}, u32[]{:S(2)}) %collective-permute-start.17) | collective-permute-done | bytes 153632 | tf_op jit(solution)/shard_map/ppermute | solution.py:609
  565.7 4.2 expert_sums.1
  (140 shorter events, 58.3 us)
Async XLA Ops:
  7.2 29.9 %copy-start = (bf16[192,4608]{1,0:T(8,128)(2,1)S(1)}, bf16[192,4608]{1,0:T(8,128)(2,1)}, u32[]{:S(2)}) copy-start(bf16[192,4608]{1,0:T(8,128)(2,1)} %param.17) | copy-start | bytes 5308420
  7.2 9.7 %copy-start.12 = (s32[1024,2]{0,1:T(2,128)S(1)}, s32[1024,2]{0,1:T(2,128)}, u32[]{:S(2)}) copy-start(s32[1024,2]{0,1:T(2,128)} %param.16) | copy-start | bytes 24580
  10.6 23.8 %all-to-all-start = ((bf16[4,24,3456]{2,1,0:T(8,128)(2,1)}), bf16[4,24,3456]{2,1,0:T(8,128)(2,1)S(1)}, u32[]{:S(2)}, u32[]{:S(2)}) async-start(bf16[4,24,3456]{2,1,0:T(8,128)(2,1)} %first_payload.1), calls=%async_computation | async-start | bytes 1327104 | tf_op jit(solution)/shard_map/all_to_all | solution.py:1195
  16.9 71.7 %all-gather.6.cloned.1.call-start = ((), (), s32[]{:S(2)}) async-start(), calls=%async_computation.15 | async-start | bytes 1474560 | tf_op jit(solution)/shard_map/all_gather | solution.py:1233
  17.2 7.0 %copy-start.1 = (s32[1024,2]{1,0:T(8,128)}, s32[1024,2]{1,0:T(8,128)S(1)}, u32[]{:S(2)}) copy-start(s32[1024,2]{1,0:T(8,128)S(1)} %copy.105.refs_3_.refs_4_) | copy-start | bytes 24580
  24.2 4.2 copy-start.2
  34.4 0.8 copy-start.3
  37.0 5.3 copy-start.4
  38.9 18.3 %all-to-all-start.1 = ((f32[4,4,4608]{2,1,0:T(4,128)}), f32[4,4,4608]{2,1,0:T(4,128)S(1)}, u32[]{:S(2)}, u32[]{:S(2)}) async-start(f32[4,4,4608]{2,1,0:T(4,128)} %fusion), calls=%async_computation.1 | async-start | bytes 589824 | tf_op jit(solution)/shard_map/all_to_all | solution.py:1235
  42.4 28.7 %collective-permute-start = (bf16[4,24,3456]{2,1,0:T(8,128)(2,1)S(1)}, bf16[4,24,3456]{2,1,0:T(8,128)(2,1)}, u32[]{:S(2)}, u32[]{:S(2)}) collective-permute-start(bf16[4,24,3456]{2,1,0:T(8,128)(2,1)S(1)} %copy-done.4), channel_id=1, source_target_pairs={{0,4},{1,5},{2,6},{3,7},{4,0},{5,1},{6,2},{7,3},{8,12},{9,13},{10,... | collective-permute-start | bytes 1990664 | tf_op jit(solution)/shard_map/ppermute | solution.py:375
  43.9 40.6 %collective-permute-start.1 = (bf16[4,24,3456]{2,1,0:T(8,128)(2,1)S(1)}, bf16[4,24,3456]{2,1,0:T(8,128)(2,1)}, u32[]{:S(2)}, u32[]{:S(2)}) collective-permute-start(bf16[4,24,3456]{2,1,0:T(8,128)(2,1)S(1)} %copy-done.4), channel_id=1, source_target_pairs={{0,1},{1,0},{2,3},{3,2},{4,5},{5,4},{6,7},{7,6},{8,9},{9,8},{10,11... | collective-permute-start | bytes 1990664 | tf_op jit(solution)/shard_map/ppermute | solution.py:375
  45.4 39.0 %collective-permute-start.2 = (bf16[4,24,3456]{2,1,0:T(8,128)(2,1)S(1)}, bf16[4,24,3456]{2,1,0:T(8,128)(2,1)}, u32[]{:S(2)}, u32[]{:S(2)}) collective-permute-start(bf16[4,24,3456]{2,1,0:T(8,128)(2,1)S(1)} %copy-done.4), channel_id=1, source_target_pairs={{0,5},{1,4},{2,7},{3,6},{4,1},{5,0},{6,3},{7,2},{8,13},{9,12},{10,... | collective-permute-start | bytes 1990664 | tf_op jit(solution)/shard_map/ppermute | solution.py:375
  66.3 68.9 %all-to-all-start.2 = ((bf16[8,336,768]{2,1,0:T(8,128)(2,1)}), bf16[8,336,768]{2,1,0:T(8,128)(2,1)}, u32[]{:S(2)}, u32[]{:S(2)}) async-start(bf16[8,336,768]{2,1,0:T(8,128)(2,1)} %get-tuple-element.80.refs_4_), calls=%async_computation.2 | async-start | bytes 8257536 | tf_op jit(solution)/shard_map/all_to_all | solution.py:1245
  70.8 185.5 %all-gather.4.cloned.1.call-start = ((), (), s32[]{:S(2)}) async-start(), calls=%async_computation.12 | async-start | bytes 11796480 | tf_op jit(solution)/shard_map/all_gather | solution.py:1252
  88.6 5.4 collective-permute-start.3
  88.7 62.4 %collective-permute-start.4 = (bf16[4,24,6144]{2,1,0:T(8,128)(2,1)}, bf16[4,24,6144]{2,1,0:T(8,128)(2,1)S(1)}, u32[]{:S(2)}, u32[]{:S(2)}) collective-permute-start(bf16[4,24,6144]{2,1,0:T(8,128)(2,1)} %bitcast.83), channel_id=1, source_target_pairs={{0,4},{1,5},{2,6},{3,7},{4,0},{5,1},{6,2},{7,3},{8,12},{9,13},{10,... | collective-permute-start | bytes 3538952 | tf_op jit(solution)/shard_map/ppermute | solution.py:375
  88.7 62.3 %collective-permute-start.5 = (bf16[4,24,6144]{2,1,0:T(8,128)(2,1)}, bf16[4,24,6144]{2,1,0:T(8,128)(2,1)}, u32[]{:S(2)}, u32[]{:S(2)}) collective-permute-start(bf16[4,24,6144]{2,1,0:T(8,128)(2,1)} %bitcast.84), channel_id=1, source_target_pairs={{0,1},{1,0},{2,3},{3,2},{4,5},{5,4},{6,7},{7,6},{8,9},{9,8},{10,11... | collective-permute-start | bytes 3538952 | tf_op jit(solution)/shard_map/ppermute | solution.py:375
  91.7 78.2 %collective-permute-start.6 = (bf16[4,24,6144]{2,1,0:T(8,128)(2,1)}, bf16[4,24,6144]{2,1,0:T(8,128)(2,1)}, u32[]{:S(2)}, u32[]{:S(2)}) collective-permute-start(bf16[4,24,6144]{2,1,0:T(8,128)(2,1)} %bitcast.85), channel_id=1, source_target_pairs={{0,5},{1,4},{2,7},{3,6},{4,1},{5,0},{6,3},{7,2},{8,13},{9,12},{10,... | collective-permute-start | bytes 3538952 | tf_op jit(solution)/shard_map/ppermute | solution.py:375
  151.1 18.8 %copy-start.7 = (bf16[4,24,6144]{2,1,0:T(8,128)(2,1)}, bf16[4,24,6144]{2,1,0:T(8,128)(2,1)S(1)}, u32[]{:S(2)}) copy-start(bf16[4,24,6144]{2,1,0:T(8,128)(2,1)S(1)} %collective-permute-done.4.refs_1_) | copy-start | bytes 3538948
  174.8 8.3 %collective-permute-start.7 = (bf16[4,4,24,6144]{3,2,1,0:T(8,128)(2,1)}, bf16[4,4,24,6144]{3,2,1,0:T(8,128)(2,1)}, u32[]{:S(2)}, u32[]{:S(2)}) collective-permute-start(bf16[4,4,24,6144]{3,2,1,0:T(8,128)(2,1)} %stack_sides.3.near_ref), channel_id=1, source_target_pairs={{0,2},{1,3},{2,0},{3,1},{4,6},{5,7},{6,4},{7,5},{8,10},{9,11},{10,... | collective-permute-start | bytes 14155784 | tf_op jit(solution)/shard_map/ppermute | solution.py:375
  174.8 60.9 %all-to-all-start.3 = ((bf16[8,336,768]{2,1,0:T(8,128)(2,1)}), bf16[8,336,768]{2,1,0:T(8,128)(2,1)}, u32[]{:S(2)}, u32[]{:S(2)}) async-start(bf16[8,336,768]{2,1,0:T(8,128)(2,1)} %spread_second.1.refs_5_), calls=%async_computation.3 | async-start | bytes 8257536 | tf_op jit(solution)/shard_map/all_to_all | solution.py:1245
  235.7 8.3 %collective-permute-start.8 = (bf16[4,768,768]{2,1,0:T(8,128)(2,1)}, bf16[4,768,768]{2,1,0:T(8,128)(2,1)}, u32[]{:S(2)}, u32[]{:S(2)}) collective-permute-start(bf16[4,768,768]{2,1,0:T(8,128)(2,1)} %get-tuple-element.93), channel_id=1, source_target_pairs={{0,2},{1,3},{2,0},{3,1},{4,6},{5,7},{6,4},{7,5},{8,10},{9,11},{10,... | collective-permute-start | bytes 14155784 | tf_op jit(solution)/shard_map/ppermute | solution.py:375
  251.3 66.4 %collective-permute-start.10 = (bf16[768,768]{1,0:T(8,128)(2,1)}, bf16[768,768]{1,0:T(8,128)(2,1)S(1)}, u32[]{:S(2)}, u32[]{:S(2)}) collective-permute-start(bf16[768,768]{1,0:T(8,128)(2,1)} %get-tuple-element.102), channel_id=1, source_target_pairs={{0,1},{1,0},{2,3},{3,2},{4,5},{5,4},{6,7},{7,6},{8,9},{9,8},{10,11... | collective-permute-start | bytes 3538952 | tf_op jit(solution)/shard_map/ppermute | solution.py:375
  251.8 65.9 %collective-permute-start.11 = (bf16[768,768]{1,0:T(8,128)(2,1)}, bf16[768,768]{1,0:T(8,128)(2,1)}, u32[]{:S(2)}, u32[]{:S(2)}) collective-permute-start(bf16[768,768]{1,0:T(8,128)(2,1)} %get-tuple-element.103), channel_id=1, source_target_pairs={{0,5},{1,4},{2,7},{3,6},{4,1},{5,0},{6,3},{7,2},{8,13},{9,12},{10,... | collective-permute-start | bytes 3538952 | tf_op jit(solution)/shard_map/ppermute | solution.py:375
  253.3 64.5 %collective-permute-start.9 = (bf16[768,768]{1,0:T(8,128)(2,1)}, bf16[768,768]{1,0:T(8,128)(2,1)}, u32[]{:S(2)}, u32[]{:S(2)}) collective-permute-start(bf16[768,768]{1,0:T(8,128)(2,1)} %get-tuple-element.101), channel_id=1, source_target_pairs={{0,4},{1,5},{2,6},{3,7},{4,0},{5,1},{6,2},{7,3},{8,12},{9,13},{10,... | collective-permute-start | bytes 3538952 | tf_op jit(solution)/shard_map/ppermute | solution.py:375
  317.7 1.1 copy-start.6
  318.7 28.7 %all-to-all-start.5 = ((bf16[8,320,384]{2,1,0:T(8,128)(2,1)}), bf16[8,320,384]{2,1,0:T(8,128)(2,1)}, u32[]{:S(2)}, u32[]{:S(2)}) async-start(bf16[8,320,384]{2,1,0:T(8,128)(2,1)} %bitcast.78), calls=%async_computation.5 | async-start | bytes 3932160 | tf_op jit(solution)/shard_map/all_to_all | solution.py:1245
  323.1 147.1 %reduce-scatter.3.cloned.1.call-start = ((), (), s32[]{:S(2)}) async-start(), calls=%async_computation.13 | async-start | bytes 5898240 | tf_op jit(solution)/shard_map/reduce_scatter | solution.py:1286
  347.5 1.3 copy-start.5
  349.9 8.0 %all-to-all-start.7 = ((f32[8,1,320]{2,1,0:T(1,128)}), f32[8,1,320]{2,1,0:T(1,128)S(1)}, u32[]{:S(2)}, u32[]{:S(2)}) async-start(f32[8,1,320]{2,1,0:T(1,128)} %reshape.204), calls=%async_computation.7 | async-start | bytes 24576 | tf_op jit(solution)/shard_map/all_to_all | solution.py:1245
  357.9 29.6 %all-to-all-start.6 = ((bf16[8,320,384]{2,1,0:T(8,128)(2,1)}), bf16[8,320,384]{2,1,0:T(8,128)(2,1)}, u32[]{:S(2)}, u32[]{:S(2)}) async-start(bf16[8,320,384]{2,1,0:T(8,128)(2,1)} %bitcast.77), calls=%async_computation.6 | async-start | bytes 3932160 | tf_op jit(solution)/shard_map/all_to_all | solution.py:1245
  362.3 199.4 %reduce-scatter.5.cloned.1.call-start = ((), (), s32[]{:S(2)}) async-start(), calls=%async_computation.14 | async-start | bytes 7372800 | tf_op jit(solution)/shard_map/reduce_scatter | solution.py:1308
  406.3 50.2 %all-to-all-start.4 = ((bf16[8,320,768]{2,1,0:T(8,128)(2,1)}), bf16[8,320,768]{2,1,0:T(8,128)(2,1)}, u32[]{:S(2)}, u32[]{:S(2)}) async-start(bf16[8,320,768]{2,1,0:T(8,128)(2,1)} %bitcast.75), calls=%async_computation.4 | async-start | bytes 7864320 | tf_op jit(solution)/shard_map/all_to_all | solution.py:1245
  470.2 10.6 %collective-permute-start.12 = (bf16[4,400,768]{2,1,0:T(8,128)(2,1)}, bf16[4,400,768]{2,1,0:T(8,128)(2,1)}, u32[]{:S(2)}, u32[]{:S(2)}) collective-permute-start(bf16[4,400,768]{2,1,0:T(8,128)(2,1)} %get-tuple-element.127.refs_7_), channel_id=1, source_target_pairs={{0,2},{1,3},{2,0},{3,1},{4,6},{5,7},{6,4},{7,5},{8,10},{9,11},{10,... | collective-permute-start | bytes 7372808 | tf_op jit(solution)/shard_map/ppermute | solution.py:375
  485.7 16.9 %collective-permute-start.13 = (bf16[400,768]{1,0:T(8,128)(2,1)}, bf16[400,768]{1,0:T(8,128)(2,1)S(1)}, u32[]{:S(2)}, u32[]{:S(2)}) collective-permute-start(bf16[400,768]{1,0:T(8,128)(2,1)} %get-tuple-element.132.refs_6_), channel_id=1, source_target_pairs={{0,4},{1,5},{2,6},{3,7},{4,0},{5,1},{6,2},{7,3},{8,12},{9,13},{10,... | collective-permute-start | bytes 1843208 | tf_op jit(solution)/shard_map/ppermute | solution.py:375
  487.2 27.6 %collective-permute-start.14 = (bf16[400,768]{1,0:T(8,128)(2,1)}, bf16[400,768]{1,0:T(8,128)(2,1)}, u32[]{:S(2)}, u32[]{:S(2)}) collective-permute-start(bf16[400,768]{1,0:T(8,128)(2,1)} %get-tuple-element.133.refs_7_), channel_id=1, source_target_pairs={{0,1},{1,0},{2,3},{3,2},{4,5},{5,4},{6,7},{7,6},{8,9},{9,8},{10,11... | collective-permute-start | bytes 1843208 | tf_op jit(solution)/shard_map/ppermute | solution.py:375
  487.7 28.7 %collective-permute-start.15 = (bf16[400,768]{1,0:T(8,128)(2,1)}, bf16[400,768]{1,0:T(8,128)(2,1)}, u32[]{:S(2)}, u32[]{:S(2)}) collective-permute-start(bf16[400,768]{1,0:T(8,128)(2,1)} %get-tuple-element.134.refs_8_), channel_id=1, source_target_pairs={{0,5},{1,4},{2,7},{3,6},{4,1},{5,0},{6,3},{7,2},{8,13},{9,12},{10,... | collective-permute-start | bytes 1843208 | tf_op jit(solution)/shard_map/ppermute | solution.py:375
  489.2 9.9 %copy-start.10 = (f32[4,3,768]{2,1,0:T(4,128)S(1)}, f32[4,3,768]{2,1,0:T(4,128)}, u32[]{:S(2)}) copy-start(f32[4,3,768]{2,1,0:T(4,128)} %get-tuple-element.137) | copy-start | bytes 110596
  489.2 9.9 %copy-start.11 = (f32[4,1,768]{2,1,0:T(1,128)S(1)}, f32[4,1,768]{2,1,0:T(1,128)}, u32[]{:S(2)}) copy-start(f32[4,1,768]{2,1,0:T(1,128)} %get-tuple-element.130.refs_0_) | copy-start | bytes 36868
  502.6 18.7 %copy-start.8 = (bf16[400,768]{1,0:T(8,128)(2,1)}, bf16[400,768]{1,0:T(8,128)(2,1)S(1)}, u32[]{:S(2)}) copy-start(bf16[400,768]{1,0:T(8,128)(2,1)S(1)} %collective-permute-done.13.refs_0_) | copy-start | bytes 1843204
  517.2 16.4 %all-to-all-start.8 = ((bf16[32,4,576]{2,1,0:T(4,128)(2,1)}), bf16[32,4,576]{2,1,0:T(4,128)(2,1)S(1)}, u32[]{:S(2)}, u32[]{:S(2)}) async-start(bf16[32,4,576]{2,1,0:T(4,128)(2,1)} %bitcast.24), calls=%async_computation.9 | async-start | bytes 327680 | tf_op jit(solution)/shard_map/all_to_all | solution.py:1340
  533.9 14.3 %copy-start.9 = (bf16[128,192]{1,0:T(8,128)(2,1)S(1)}, bf16[128,192]{1,0:T(8,128)(2,1)}, u32[]{:S(2)}) copy-start(bf16[128,192]{1,0:T(8,128)(2,1)} %reshape.191.refs_13_) | copy-start | bytes 147460
  534.7 27.0 %all-to-all-start.9 = ((f32[32,4,192]{2,1,0:T(4,128)}), f32[32,4,192]{2,1,0:T(4,128)S(1)}, u32[]{:S(2)}, u32[]{:S(2)}) async-start(f32[32,4,192]{2,1,0:T(4,128)} %reshape.195), calls=%async_computation.10 | async-start | bytes 262144 | tf_op jit(solution)/shard_map/all_to_all | solution.py:1351
  540.8 10.2 %collective-permute-start.16 = (bf16[192,400]{0,1:T(8,128)(2,1)S(1)}, bf16[192,400]{0,1:T(8,128)(2,1)S(1)}, u32[]{:S(2)}, u32[]{:S(2)}) collective-permute-start(bf16[192,400]{0,1:T(8,128)(2,1)S(1)} %bitcast.88), channel_id=1, source_target_pairs={{0,8},{8,16},{16,24},{24,0},{1,9},{9,17},{17,25},{25,1},{2,10},{10... | collective-permute-start | bytes 460808 | tf_op jit(solution)/shard_map/ppermute | solution.py:609
  543.4 15.9 %collective-permute-start.17 = (bf16[192,400]{0,1:T(8,128)(2,1)}, bf16[192,400]{0,1:T(8,128)(2,1)S(1)}, u32[]{:S(2)}, u32[]{:S(2)}) collective-permute-start(bf16[192,400]{0,1:T(8,128)(2,1)} %bitcast.30), channel_id=1, source_target_pairs={{0,16},{8,24},{16,0},{24,8},{1,17},{9,25},{17,1},{25,9},{2,18},{10... | collective-permute-start | bytes 460808 | tf_op jit(solution)/shard_map/ppermute | solution.py:609
  546.7 12.6 %collective-permute-start.18 = (bf16[192,400]{0,1:T(8,128)(2,1)}, bf16[192,400]{0,1:T(8,128)(2,1)S(1)}, u32[]{:S(2)}, u32[]{:S(2)}) collective-permute-start(bf16[192,400]{0,1:T(8,128)(2,1)} %bitcast.89), channel_id=1, source_target_pairs={{0,24},{8,0},{16,8},{24,16},{1,25},{9,1},{17,9},{25,17},{2,26},{10... | collective-permute-start | bytes 460808 | tf_op jit(solution)/shard_map/ppermute | solution.py:609
  562.7 2.4 copy-start.13
Sparse Core Ops, SparseCore 0:
  37.2 33.5 all-gather.5
  88.7 167.5 all-gather.3
  347.6 84.1 reduce-scatter.2
  434.0 107.5 reduce-scatter.4

commit v4 on v3

--- a/solution.py
+++ b/solution.py
@@ -1347,7 +1347,7 @@
     grad_columns, last_sum = together(grad_columns, last_sum)
     ada_weight_grad = product_left_operand(silu_all, grad_columns)
     own_ada = lax.dynamic_slice_in_dim(ada_weight, plane_index * columns, columns, 1)
-    silu_back = product_right_operand(grad_columns, own_ada)
+    silu_back, late_final = together(product_right_operand(grad_columns, own_ada), late_final)
     silu_back = lax.all_to_all(
         silu_back.reshape(depth * experts, cond_rows, local),
         everyone,
@@ -1355,7 +1355,6 @@
         concat_axis=0,
         tiled=True,
     )
-    silu_back, late_final = together(silu_back, late_final)
     silu_back = jnp.sum(silu_back.reshape(depth, experts, cond_rows, local), axis=1)
     grad_silu = jnp.transpose(silu_back, (1, 0, 2)).reshape(cond_rows, width)
     cond_grad = jax.vjp(jax.nn.silu, cond_wide)[1](grad_silu)[0]

time: 585 us -> 589 us (level)
  waiting for transfers between devices: 104 us -> 136 us
  Pallas kernels: 357 us -> 328 us
    pallas_call x1, Pallas kernels: 40.7 us -> 22.3 us  [attend_back(): pl.pallas_call(attend_back_kernel, grid=(width // 128,), in_specs=[pl.Blo...]
    all_to_all x6, waiting for transfers between devices: 8.37 us -> 26.7 us  [exchange(): return lax.all_to_all(rows, PLANE, split_axis=0, concat_axis=0, tiled=True)]
    ppermute x16, waiting for transfers between devices: 59.7 us -> 70.6 us  [flip(): lax.ppermute(value, PLANE, [(index, index ^ mask) for index in range(coun...]
    pallas_call x1, Pallas kernels: 26.1 us -> 15.2 us  [attend(): pl.pallas_call(attend_kernel, grid=(width // 128,), in_specs=[pl.BlockSpe...]
  transfers between devices with their start and end apart: 33 -> 33, of which waited for: 16 -> 18; matrix products, arithmetic and copies ran while one was open for 4% -> 5% of each run, Pallas kernels for 61% -> 56%
where the time goes in v4:
time: 589 us; the launch traced here: 583 us
  Pallas kernels  328 us (56%)
  waiting for transfers between devices  136 us (23%)
  starting transfers between devices  69.4 us (12%)
  local copies, waits for them, and re-layouts  23.3 us (4%)
  between operations  15.2 us (3%)
  other arithmetic  8.39 us (1%)
    pallas_call x13, Pallas kernels, stepped(): pl.pallas_call(body, grid=(steps,), in_specs=list(in_specs) + [ANYWHERE]...  190 us
    ppermute x16, waiting for transfers between devices, flip(): lax.ppermute(value, PLANE, [(index, index ^ mask) for index in range(coun...  70.6 us
    pallas_call x1, Pallas kernels, shared_expert(): pl.pallas_call(kernel, grid_spec=pltpu.PrefetchScalarGridSpec(num_scalar_...  44.3 us
    all_to_all x6, waiting for transfers between devices, exchange(): return lax.all_to_all(rows, PLANE, split_axis=0, concat_axis=0, tiled=True)  26.7 us
    all_to_all x6, starting transfers between devices, exchange(): return lax.all_to_all(rows, PLANE, split_axis=0, concat_axis=0, tiled=True)  25.9 us
    pallas_call x1, Pallas kernels, attend_back(): pl.pallas_call(attend_back_kernel, grid=(width // 128,), in_specs=[pl.Blo...  22.3 us
    pallas_call x1, Pallas kernels, attend(): pl.pallas_call(attend_kernel, grid=(width // 128,), in_specs=[pl.BlockSpe...  15.2 us
    ppermute x16, starting transfers between devices, flip(): lax.ppermute(value, PLANE, [(index, index ^ mask) for index in range(coun...  15.2 us
  transfers between devices with their start and end apart: 33, of which 18 were waited for; matrix products, arithmetic and copies ran while one was open for 5% of the time, Pallas kernels for 56%

profile of v4, /device:TPU:0, one launch (start us, length us, event | category | flops | bytes accessed | tf_op | source)
XLA Modules:
  0.0 583.2 jit_solution(6232672862864263240)
XLA Ops:
  10.6 6.3 %all-to-all-start = ((bf16[4,24,3456]{2,1,0:T(8,128)(2,1)}), bf16[4,24,3456]{2,1,0:T(8,128)(2,1)S(1)}, u32[]{:S(2)}, u32[]{:S(2)}) async-start(bf16[4,24,3456]{2,1,0:T(8,128)(2,1)} %first_payload.1), calls=%async_computation | async-start | bytes 1327104 | tf_op jit(solution)/shard_map/all_to_all | solution.py:1195
  25.0 3.4 expert_payload.1.refs_2_
  28.4 6.0 %all-to-all-done.refs_0_ = bf16[4,24,3456]{2,1,0:T(8,128)(2,1)S(1)} async-done(((bf16[4,24,3456]{2,1,0:T(8,128)(2,1)}), bf16[4,24,3456]{2,1,0:T(8,128)(2,1)S(1)}, u32[]{:S(2)}, u32[]{:S(2)}) %all-to-all-start) | async-done | bytes 663584 | tf_op jit(solution)/shard_map/all_to_all | solution.py:1195
  38.9 3.5 all-to-all-start.1
  47.2 10.0 %all-to-all-done.1 = f32[4,4,4608]{2,1,0:T(4,128)S(1)} async-done(((f32[4,4,4608]{2,1,0:T(4,128)}), f32[4,4,4608]{2,1,0:T(4,128)S(1)}, u32[]{:S(2)}, u32[]{:S(2)}) %all-to-all-start.1) | async-done | bytes 294944 | tf_op jit(solution)/shard_map/all_to_all | solution.py:1235
  58.1 8.2 %spread_mixture.1 = (bf16[1024,768]{1,0:T(8,128)(2,1)}, bf16[8,336,768]{2,1,0:T(8,128)(2,1)}) custom-call(bf16[1024,768]{1,0:T(8,128)(2,1)} %refs_5_.1, f32[4,6,768]{2,1,0:T(8,128)} %broadcast_select_fusion.refs_1_.refs_2_.refs_9_.refs_4_.refs_3_, s32[2,1024]{1,0:T(2,128)} %copy.108.refs_2_.refs_1_, bf16[16,192]{1,0:T(8,128)(2,1)} %reshape.178.refs_3_), custom_call_target="tpu_custom_call" | custom-call | tf_op jit(solution)/shard_map/spread_mixture/pallas_call | solution.py:406
  66.3 4.5 all-to-all-start.2
  71.1 13.4 %collective-permute-done.1.refs_2_ = bf16[4,24,3456]{2,1,0:T(8,128)(2,1)} collective-permute-done((bf16[4,24,3456]{2,1,0:T(8,128)(2,1)S(1)}, bf16[4,24,3456]{2,1,0:T(8,128)(2,1)}, u32[]{:S(2)}, u32[]{:S(2)}) %collective-permute-start.1) | collective-permute-done | bytes 663584 | tf_op jit(solution)/shard_map/ppermute | solution.py:375
  84.5 4.0 stack_sides.2.near_ref
  88.7 2.9 collective-permute-start.5
  93.9 6.4 %place_slices.2 = bf16[4,8,24,3456]{3,2,1,0:T(8,128)(2,1)} custom-call(s32[5]{0:T(128)} %stack.26.order_ref, bf16[4,4,24,3456]{3,2,1,0:T(8,128)(2,1)} %stack_sides.2.near_ref, bf16[4,4,24,3456]{3,2,1,0:T(8,128)(2,1)} %collective-permute-done.3.far_ref), custom_call_target="tpu_custom_call" | custom-call | tf_op jit(solution)/shard_map/place_slices/pallas_call | solution.py:463
  100.3 8.8 %first_half.1 = (bf16[1024,768]{1,0:T(8,128)(2,1)}, bf16[3,1024,768]{2,1,0:T(8,128)(2,1)}) custom-call(bf16[1024,768]{1,0:T(8,128)(2,1)} %refs_2_.1, f32[4,6,768]{2,1,0:T(8,128)} %broadcast_select_fusion.refs_1_.refs_2_.refs_9_.refs_4_.refs_3_, bf16[768,3456]{1,0:T(8,128)(2,1)} %bitcast.66), custom_call_target="tpu_custom_call" | custom-call | tf_op jit(solution)/shard_map/first_half/pallas_call | solution.py:406
  109.1 15.2 %attend.1 = (bf16[1024,768]{1,0:T(8,128)(2,1)}, f32[1024,768]{1,0:T(8,128)}) custom-call(s32[1]{0:T(128)S(6)} %copy.130.long_ref, bf16[3,1024,768]{2,1,0:T(8,128)(2,1)} %get-tuple-element.82.joined_ref), custom_call_target="tpu_custom_call" | custom-call | tf_op jit(solution)/shard_map/attend/pallas_call | solution.py:73
  124.3 7.2 %second_half.1 = (f32[1024,768]{1,0:T(8,128)}, f32[1024,768]{1,0:T(8,128)}, bf16[1024,768]{1,0:T(8,128)(2,1)}, f32[1024,2]{1,0:T(8,128)}, f32[2,1024]{1,0:T(2,128)}) custom-call(bf16[1024,768]{1,0:T(8,128)(2,1)} %get-tuple-element.84.refs_0_.refs_4_, bf16[1024,768]{1,0:T(8,128)(2,1)} %refs_2_.1, ...), custom_call_target="tpu_custom_call" | custom-call | tf_op jit(solution)/shard_map/second_half/pallas_call | solution.py:406
  131.5 8.6 %spread_second.1.refs_5_ = bf16[8,336,768]{2,1,0:T(8,128)(2,1)} custom-call(bf16[1024,768]{1,0:T(8,128)(2,1)} %get-tuple-element.85.refs_0_.refs_1_.refs_6_, s32[2,1024]{1,0:T(2,128)} %copy.108.refs_2_.refs_1_, f32[2,1024]{1,0:T(2,128)} %get-tuple-element.87.refs_2_), custom_call_target="tpu_custom_call" | custom-call | tf_op jit(solution)/shard_map/spread_second/pallas_call | solution.py:406
  140.2 3.9 collective-permute-done.4.refs_1_
  144.0 25.8 %collective-permute-done.6.refs_3_ = bf16[4,24,6144]{2,1,0:T(8,128)(2,1)} collective-permute-done((bf16[4,24,6144]{2,1,0:T(8,128)(2,1)}, bf16[4,24,6144]{2,1,0:T(8,128)(2,1)}, u32[]{:S(2)}, u32[]{:S(2)}) %collective-permute-start.6) | collective-permute-done | bytes 1179680 | tf_op jit(solution)/shard_map/ppermute | solution.py:375
  169.8 5.0 stack_sides.3.near_ref
  174.8 4.6 all-to-all-start.3
  179.4 3.7 collective-permute-done.7.far_ref
  183.1 8.3 %place_slices.3 = bf16[4,8,24,6144]{3,2,1,0:T(8,128)(2,1)} custom-call(s32[5]{0:T(128)} %stack.26.order_ref, bf16[4,4,24,6144]{3,2,1,0:T(8,128)(2,1)} %stack_sides.3.near_ref, bf16[4,4,24,6144]{3,2,1,0:T(8,128)(2,1)} %collective-permute-done.7.far_ref), custom_call_target="tpu_custom_call" | custom-call | tf_op jit(solution)/shard_map/place_slices/pallas_call | solution.py:463
  191.4 44.3 %shared_expert.1 = (f32[1024,768]{1,0:T(8,128)}, f32[1024,768]{1,0:T(8,128)}, bf16[4,768,768]{2,1,0:T(8,128)(2,1)}, bf16[4,768,768]{2,1,0:T(8,128)(2,1)}) custom-call(s32[1]{0:T(128)} %bitcast.refs_0_, bf16[1024,768]{1,0:T(8,128)(2,1)} %get-tuple-element.85.refs_0_.refs_1_.refs_6_, bf16[1024,768]{1,0:T(8,128)(2,1)} %get-tuple-element.86.refs_2_, ...), custom_call_target="tpu_custom_call" | custom-call | tf_op jit(solution)/shard_map/shared_expert/pallas_call | solution.py:354
  235.9 8.1 %collective-permute-done.8.other_ref = bf16[4,768,768]{2,1,0:T(8,128)(2,1)} collective-permute-done((bf16[4,768,768]{2,1,0:T(8,128)(2,1)}, bf16[4,768,768]{2,1,0:T(8,128)(2,1)}, u32[]{:S(2)}, u32[]{:S(2)}) %collective-permute-start.8) | collective-permute-done | bytes 4718624 | tf_op jit(solution)/shard_map/ppermute | solution.py:375
  244.1 7.2 %pair_sum.2 = (f32[768,768]{1,0:T(8,128)}, bf16[768,768]{1,0:T(8,128)(2,1)}, bf16[768,768]{1,0:T(8,128)(2,1)}, bf16[768,768]{1,0:T(8,128)(2,1)}) custom-call(s32[1]{0:T(128)} %bitcast.4.place_ref, bf16[4,768,768]{2,1,0:T(8,128)(2,1)} %get-tuple-element.92.kept_ref, bf16[4,768,768]{2,1,0:T(8,128)(2,1)} %collective-permute-done.8.other_ref), custom_call_target="tpu_custom_call" | custom-call | tf_op jit(solution)/shard_map/pair_sum/pallas_call | solution.py:502
  256.3 61.4 %routed_expert.1 = (bf16[2560,768]{1,0:T(8,128)(2,1)}, bf16[2560,384]{1,0:T(8,128)(2,1)}, bf16[2560,384]{1,0:T(8,128)(2,1)}, f32[2560,1]{1,0:T(8,128)}, bf16[256...) custom-call(bf16[8,336,768]{2,1,0:T(8,128)(2,1)} %all-to-all-done.3.refs_0_, bf16[8,336,768]{2,1,0:T(8,128)(2,1)} %all-to-all-done.2.refs_1_, ...), custom_call_target="tpu_custom_call" | custom-call | tf_op jit(solution)/shard_map/routed_expert/pallas_call | solution.py:406
  318.7 4.3 all-to-all-start.5
  323.1 20.7 %routed_sums.2.refs_3_.refs_5_ = bf16[768,3072]{1,0:T(8,128)(2,1)} custom-call(bf16[8,336,768]{2,1,0:T(8,128)(2,1)} %all-to-all-done.3.refs_0_, bf16[8,336,768]{2,1,0:T(8,128)(2,1)} %all-to-all-done.2.refs_1_, bf16[2560,3072]{1,0:T(8,128)(2,1)} %get-tuple-element.99.refs_2_, bf16[2560,3072]{1,0:T(8,128)(2,1)} %get-tuple-element.100.refs_3_), custom_call_target="tpu_custom_call" | custom-call | tf_op jit(solution)/shard_map/routed_sums/pallas_call | solution.py:406
  343.9 3.6 all-to-all-done.5
  349.9 3.3 all-to-all-start.7
  353.2 4.7 side_sum.2.refs_4_
  357.9 4.3 all-to-all-start.6
  363.9 22.8 %routed_sums.3 = bf16[768,3840]{1,0:T(8,128)(2,1)} custom-call(bf16[8,336,768]{2,1,0:T(8,128)(2,1)} %all-to-all-done.3.refs_0_, bf16[8,336,768]{2,1,0:T(8,128)(2,1)} %all-to-all-done.2.refs_1_, bf16[2560,3072]{1,0:T(8,128)(2,1)} %get-tuple-element.99.refs_2_, bf16[2560,3072]{1,0:T(8,128)(2,1)} %get-tuple-element.100.refs_3_, ...), custom_call_target="tpu_custom_call" | custom-call | tf_op jit(solution)/shard_map/routed_sums/pallas_call | solution.py:406
  387.5 18.8 %middle_back.1 = (f32[1024,768]{1,0:T(8,128)}, bf16[1024,768]{1,0:T(8,128)(2,1)}, bf16[1024,768]{1,0:T(8,128)(2,1)}, bf16[1024,128]{1,0:T(8,128)(2,1)}, f32[4,3,768]{2,1,0:T(4,128)}) custom-call(bf16[2560,384]{1,0:T(8,128)(2,1)} %bitcast.19.refs_0_, bf16[2560,384]{1,0:T(8,128)(2,1)} %bitcast.21.refs_1_, f32[1,2560]{1,0:T(1,128)} %reshape.189.refs_2_, ...), custom_call_target="tpu_custom_call" | custom-call | tf_op jit(solution)/shard_map/middle_back/pallas_call | solution.py:406
  406.3 4.7 all-to-all-start.4
  411.0 22.3 %attend_back.1.refs_1_.refs_0_ = bf16[3,1024,768]{2,1,0:T(8,128)(2,1)} custom-call(s32[1]{0:T(128)S(6)} %copy.130.long_ref, bf16[3,1024,768]{2,1,0:T(8,128)(2,1)} %get-tuple-element.82.joined_ref, f32[1024,768]{1,0:T(8,128)} %get-tuple-element.98.total_ref, bf16[1024,768]{1,0:T(8,128)(2,1)} %get-tuple-element.122.grad_ref), custom_call_target="tpu_custom_call" | custom-call | tf_op jit(solution)/shard_map/attend_back/pallas_call | solution.py:121
  433.3 23.1 %all-to-all-done.4 = bf16[8,320,768]{2,1,0:T(8,128)(2,1)} async-done(((bf16[8,320,768]{2,1,0:T(8,128)(2,1)}), bf16[8,320,768]{2,1,0:T(8,128)(2,1)}, u32[]{:S(2)}, u32[]{:S(2)}) %all-to-all-start.4) | async-done | bytes 3932192 | tf_op jit(solution)/shard_map/all_to_all | solution.py:1245
  456.4 13.8 %last_gradients.1 = (bf16[4,400,768]{2,1,0:T(8,128)(2,1)}, bf16[4,400,768]{2,1,0:T(8,128)(2,1)}) custom-call(s32[1]{0:T(128)} %bitcast.refs_0_, bf16[3,1024,768]{2,1,0:T(8,128)(2,1)} %attend_back.1.refs_1_.refs_0_, bf16[1024,768]{1,0:T(8,128)(2,1)} %get-tuple-element.123.refs_2_, bf16[1024,768]{1,0:T(8,128)(2,1)} %get-tuple-element.124.refs_3_, ...), custom_call_target="tpu_custom_call" | custom-call | tf_op jit(solution)/shard_map/last_gradients/pallas_call | solution.py:581
  470.2 10.6 %block_output.1 = (bf16[1024,768]{1,0:T(8,128)(2,1)}, f32[4,1,768]{2,1,0:T(1,128)}) custom-call(bf16[2560,768]{1,0:T(8,128)(2,1)} %bitcast.17.refs_7_.refs_0_, s32[1024,2]{1,0:T(8,128)} %copy-done.2, f32[1024,768]{1,0:T(8,128)} %get-tuple-element.96.refs_2_, f32[1024,768]{1,0:T(8,128)} %get-tuple-element.97.refs_7_.refs_3_, ...), custom_call_target="tpu_custom_call" | custom-call | tf_op jit(solution)/shard_map/block_output/pallas_call | solution.py:406
  480.8 4.9 pair_sum.3
  489.2 9.9 %start_back.1 = (f32[1024,768]{1,0:T(8,128)}, f32[4,2,768]{2,1,0:T(2,128)}) custom-call(bf16[3,1024,768]{2,1,0:T(8,128)(2,1)} %attend_back.1.refs_1_.refs_0_, bf16[768,3456]{1,0:T(8,128)(2,1)} %bitcast.71, bf16[1024,768]{1,0:T(8,128)(2,1)} %refs_2_.1, f32[4,6,768]{2,1,0:T(8,128)} %broadcast_select_fusion.refs_1_.refs_2_.refs_9_.refs_4_.refs_3_, ...), custom_call_target="tpu_custom_call" | custom-call | tf_op jit(solution)/shard_map/start_back/pallas_call | solution.py:406
  502.6 12.2 %collective-permute-done.14.refs_1_ = bf16[400,768]{1,0:T(8,128)(2,1)} collective-permute-done((bf16[400,768]{1,0:T(8,128)(2,1)}, bf16[400,768]{1,0:T(8,128)(2,1)}, u32[]{:S(2)}, u32[]{:S(2)}) %collective-permute-start.14) | collective-permute-done | bytes 614432 | tf_op jit(solution)/shard_map/ppermute | solution.py:375
  517.2 4.1 all-to-all-start.8
  521.3 3.7 side_sum.3
  525.1 8.4 %all-to-all-done.8 = bf16[32,4,576]{2,1,0:T(4,128)(2,1)S(1)} async-done(((bf16[32,4,576]{2,1,0:T(4,128)(2,1)}), bf16[32,4,576]{2,1,0:T(4,128)(2,1)S(1)}, u32[]{:S(2)}, u32[]{:S(2)}) %all-to-all-start.8) | async-done | bytes 147488 | tf_op jit(solution)/shard_map/all_to_all | solution.py:1340
  540.7 2.9 collective-permute-start.18
  546.8 8.2 %collective-permute-done.17 = bf16[192,400]{0,1:T(8,128)(2,1)S(1)} collective-permute-done((bf16[192,400]{0,1:T(8,128)(2,1)}, bf16[192,400]{0,1:T(8,128)(2,1)S(1)}, u32[]{:S(2)}, u32[]{:S(2)}) %collective-permute-start.17) | collective-permute-done | bytes 153632 | tf_op jit(solution)/shard_map/ppermute | solution.py:609
  559.1 7.9 %all-to-all-start.9 = ((f32[32,4,192]{2,1,0:T(4,128)}), f32[32,4,192]{2,1,0:T(4,128)S(1)}, u32[]{:S(2)}, u32[]{:S(2)}) async-start(f32[32,4,192]{2,1,0:T(4,128)} %reshape.195), calls=%async_computation.11 | async-start | bytes 262144 | tf_op jit(solution)/shard_map/all_to_all | solution.py:1351
  569.3 4.2 expert_sums.1
  (141 shorter events, 63.6 us)
Async XLA Ops:
  7.2 29.9 %copy-start = (bf16[192,4608]{1,0:T(8,128)(2,1)S(1)}, bf16[192,4608]{1,0:T(8,128)(2,1)}, u32[]{:S(2)}) copy-start(bf16[192,4608]{1,0:T(8,128)(2,1)} %param.17) | copy-start | bytes 5308420
  7.2 9.7 %copy-start.12 = (s32[1024,2]{0,1:T(2,128)S(1)}, s32[1024,2]{0,1:T(2,128)}, u32[]{:S(2)}) copy-start(s32[1024,2]{0,1:T(2,128)} %param.16) | copy-start | bytes 24580
  10.6 23.8 %all-to-all-start = ((bf16[4,24,3456]{2,1,0:T(8,128)(2,1)}), bf16[4,24,3456]{2,1,0:T(8,128)(2,1)S(1)}, u32[]{:S(2)}, u32[]{:S(2)}) async-start(bf16[4,24,3456]{2,1,0:T(8,128)(2,1)} %first_payload.1), calls=%async_computation | async-start | bytes 1327104 | tf_op jit(solution)/shard_map/all_to_all | solution.py:1195
  16.9 71.7 %all-gather.6.cloned.1.call-start = ((), (), s32[]{:S(2)}) async-start(), calls=%async_computation.15 | async-start | bytes 1474560 | tf_op jit(solution)/shard_map/all_gather | solution.py:1233
  17.2 7.0 %copy-start.1 = (s32[1024,2]{1,0:T(8,128)}, s32[1024,2]{1,0:T(8,128)S(1)}, u32[]{:S(2)}) copy-start(s32[1024,2]{1,0:T(8,128)S(1)} %copy.105.refs_3_.refs_4_) | copy-start | bytes 24580
  24.2 4.2 copy-start.2
  34.4 0.8 copy-start.3
  37.0 5.3 copy-start.4
  38.9 18.3 %all-to-all-start.1 = ((f32[4,4,4608]{2,1,0:T(4,128)}), f32[4,4,4608]{2,1,0:T(4,128)S(1)}, u32[]{:S(2)}, u32[]{:S(2)}) async-start(f32[4,4,4608]{2,1,0:T(4,128)} %fusion), calls=%async_computation.1 | async-start | bytes 589824 | tf_op jit(solution)/shard_map/all_to_all | solution.py:1235
  42.4 28.7 %collective-permute-start = (bf16[4,24,3456]{2,1,0:T(8,128)(2,1)S(1)}, bf16[4,24,3456]{2,1,0:T(8,128)(2,1)}, u32[]{:S(2)}, u32[]{:S(2)}) collective-permute-start(bf16[4,24,3456]{2,1,0:T(8,128)(2,1)S(1)} %copy-done.4), channel_id=1, source_target_pairs={{0,4},{1,5},{2,6},{3,7},{4,0},{5,1},{6,2},{7,3},{8,12},{9,13},{10,... | collective-permute-start | bytes 1990664 | tf_op jit(solution)/shard_map/ppermute | solution.py:375
  43.9 40.6 %collective-permute-start.1 = (bf16[4,24,3456]{2,1,0:T(8,128)(2,1)S(1)}, bf16[4,24,3456]{2,1,0:T(8,128)(2,1)}, u32[]{:S(2)}, u32[]{:S(2)}) collective-permute-start(bf16[4,24,3456]{2,1,0:T(8,128)(2,1)S(1)} %copy-done.4), channel_id=1, source_target_pairs={{0,1},{1,0},{2,3},{3,2},{4,5},{5,4},{6,7},{7,6},{8,9},{9,8},{10,11... | collective-permute-start | bytes 1990664 | tf_op jit(solution)/shard_map/ppermute | solution.py:375
  45.4 39.0 %collective-permute-start.2 = (bf16[4,24,3456]{2,1,0:T(8,128)(2,1)S(1)}, bf16[4,24,3456]{2,1,0:T(8,128)(2,1)}, u32[]{:S(2)}, u32[]{:S(2)}) collective-permute-start(bf16[4,24,3456]{2,1,0:T(8,128)(2,1)S(1)} %copy-done.4), channel_id=1, source_target_pairs={{0,5},{1,4},{2,7},{3,6},{4,1},{5,0},{6,3},{7,2},{8,13},{9,12},{10,... | collective-permute-start | bytes 1990664 | tf_op jit(solution)/shard_map/ppermute | solution.py:375
  66.3 58.0 %all-to-all-start.2 = ((bf16[8,336,768]{2,1,0:T(8,128)(2,1)}), bf16[8,336,768]{2,1,0:T(8,128)(2,1)}, u32[]{:S(2)}, u32[]{:S(2)}) async-start(bf16[8,336,768]{2,1,0:T(8,128)(2,1)} %get-tuple-element.80.refs_4_), calls=%async_computation.2 | async-start | bytes 8257536 | tf_op jit(solution)/shard_map/all_to_all | solution.py:1245
  70.8 185.5 %all-gather.4.cloned.1.call-start = ((), (), s32[]{:S(2)}) async-start(), calls=%async_computation.12 | async-start | bytes 11796480 | tf_op jit(solution)/shard_map/all_gather | solution.py:1252
  88.6 5.4 collective-permute-start.3
  88.7 55.4 %collective-permute-start.4 = (bf16[4,24,6144]{2,1,0:T(8,128)(2,1)}, bf16[4,24,6144]{2,1,0:T(8,128)(2,1)S(1)}, u32[]{:S(2)}, u32[]{:S(2)}) collective-permute-start(bf16[4,24,6144]{2,1,0:T(8,128)(2,1)} %bitcast.83), channel_id=1, source_target_pairs={{0,4},{1,5},{2,6},{3,7},{4,0},{5,1},{6,2},{7,3},{8,12},{9,13},{10,... | collective-permute-start | bytes 3538952 | tf_op jit(solution)/shard_map/ppermute | solution.py:375
  88.7 55.3 %collective-permute-start.5 = (bf16[4,24,6144]{2,1,0:T(8,128)(2,1)}, bf16[4,24,6144]{2,1,0:T(8,128)(2,1)}, u32[]{:S(2)}, u32[]{:S(2)}) collective-permute-start(bf16[4,24,6144]{2,1,0:T(8,128)(2,1)} %bitcast.84), channel_id=1, source_target_pairs={{0,1},{1,0},{2,3},{3,2},{4,5},{5,4},{6,7},{7,6},{8,9},{9,8},{10,11... | collective-permute-start | bytes 3538952 | tf_op jit(solution)/shard_map/ppermute | solution.py:375
  91.7 78.2 %collective-permute-start.6 = (bf16[4,24,6144]{2,1,0:T(8,128)(2,1)}, bf16[4,24,6144]{2,1,0:T(8,128)(2,1)}, u32[]{:S(2)}, u32[]{:S(2)}) collective-permute-start(bf16[4,24,6144]{2,1,0:T(8,128)(2,1)} %bitcast.85), channel_id=1, source_target_pairs={{0,5},{1,4},{2,7},{3,6},{4,1},{5,0},{6,3},{7,2},{8,13},{9,12},{10,... | collective-permute-start | bytes 3538952 | tf_op jit(solution)/shard_map/ppermute | solution.py:375
  144.0 25.8 %copy-start.7 = (bf16[4,24,6144]{2,1,0:T(8,128)(2,1)}, bf16[4,24,6144]{2,1,0:T(8,128)(2,1)S(1)}, u32[]{:S(2)}) copy-start(bf16[4,24,6144]{2,1,0:T(8,128)(2,1)S(1)} %collective-permute-done.4.refs_1_) | copy-start | bytes 3538948
  174.8 8.3 %collective-permute-start.7 = (bf16[4,4,24,6144]{3,2,1,0:T(8,128)(2,1)}, bf16[4,4,24,6144]{3,2,1,0:T(8,128)(2,1)}, u32[]{:S(2)}, u32[]{:S(2)}) collective-permute-start(bf16[4,4,24,6144]{3,2,1,0:T(8,128)(2,1)} %stack_sides.3.near_ref), channel_id=1, source_target_pairs={{0,2},{1,3},{2,0},{3,1},{4,6},{5,7},{6,4},{7,5},{8,10},{9,11},{10,... | collective-permute-start | bytes 14155784 | tf_op jit(solution)/shard_map/ppermute | solution.py:375
  174.8 60.9 %all-to-all-start.3 = ((bf16[8,336,768]{2,1,0:T(8,128)(2,1)}), bf16[8,336,768]{2,1,0:T(8,128)(2,1)}, u32[]{:S(2)}, u32[]{:S(2)}) async-start(bf16[8,336,768]{2,1,0:T(8,128)(2,1)} %spread_second.1.refs_5_), calls=%async_computation.3 | async-start | bytes 8257536 | tf_op jit(solution)/shard_map/all_to_all | solution.py:1245
  235.7 8.3 %collective-permute-start.8 = (bf16[4,768,768]{2,1,0:T(8,128)(2,1)}, bf16[4,768,768]{2,1,0:T(8,128)(2,1)}, u32[]{:S(2)}, u32[]{:S(2)}) collective-permute-start(bf16[4,768,768]{2,1,0:T(8,128)(2,1)} %get-tuple-element.93), channel_id=1, source_target_pairs={{0,2},{1,3},{2,0},{3,1},{4,6},{5,7},{6,4},{7,5},{8,10},{9,11},{10,... | collective-permute-start | bytes 14155784 | tf_op jit(solution)/shard_map/ppermute | solution.py:375
  251.3 66.4 %collective-permute-start.10 = (bf16[768,768]{1,0:T(8,128)(2,1)}, bf16[768,768]{1,0:T(8,128)(2,1)S(1)}, u32[]{:S(2)}, u32[]{:S(2)}) collective-permute-start(bf16[768,768]{1,0:T(8,128)(2,1)} %get-tuple-element.102), channel_id=1, source_target_pairs={{0,1},{1,0},{2,3},{3,2},{4,5},{5,4},{6,7},{7,6},{8,9},{9,8},{10,11... | collective-permute-start | bytes 3538952 | tf_op jit(solution)/shard_map/ppermute | solution.py:375
  251.8 65.9 %collective-permute-start.11 = (bf16[768,768]{1,0:T(8,128)(2,1)}, bf16[768,768]{1,0:T(8,128)(2,1)}, u32[]{:S(2)}, u32[]{:S(2)}) collective-permute-start(bf16[768,768]{1,0:T(8,128)(2,1)} %get-tuple-element.103), channel_id=1, source_target_pairs={{0,5},{1,4},{2,7},{3,6},{4,1},{5,0},{6,3},{7,2},{8,13},{9,12},{10,... | collective-permute-start | bytes 3538952 | tf_op jit(solution)/shard_map/ppermute | solution.py:375
  253.3 64.5 %collective-permute-start.9 = (bf16[768,768]{1,0:T(8,128)(2,1)}, bf16[768,768]{1,0:T(8,128)(2,1)}, u32[]{:S(2)}, u32[]{:S(2)}) collective-permute-start(bf16[768,768]{1,0:T(8,128)(2,1)} %get-tuple-element.101), channel_id=1, source_target_pairs={{0,4},{1,5},{2,6},{3,7},{4,0},{5,1},{6,2},{7,3},{8,12},{9,13},{10,... | collective-permute-start | bytes 3538952 | tf_op jit(solution)/shard_map/ppermute | solution.py:375
  317.7 1.1 copy-start.6
  318.7 28.7 %all-to-all-start.5 = ((bf16[8,320,384]{2,1,0:T(8,128)(2,1)}), bf16[8,320,384]{2,1,0:T(8,128)(2,1)}, u32[]{:S(2)}, u32[]{:S(2)}) async-start(bf16[8,320,384]{2,1,0:T(8,128)(2,1)} %bitcast.78), calls=%async_computation.5 | async-start | bytes 3932160 | tf_op jit(solution)/shard_map/all_to_all | solution.py:1245
  323.1 147.1 %reduce-scatter.3.cloned.1.call-start = ((), (), s32[]{:S(2)}) async-start(), calls=%async_computation.13 | async-start | bytes 5898240 | tf_op jit(solution)/shard_map/reduce_scatter | solution.py:1286
  347.5 1.3 copy-start.5
  349.9 8.0 %all-to-all-start.7 = ((f32[8,1,320]{2,1,0:T(1,128)}), f32[8,1,320]{2,1,0:T(1,128)S(1)}, u32[]{:S(2)}, u32[]{:S(2)}) async-start(f32[8,1,320]{2,1,0:T(1,128)} %reshape.204), calls=%async_computation.7 | async-start | bytes 24576 | tf_op jit(solution)/shard_map/all_to_all | solution.py:1245
  357.9 29.6 %all-to-all-start.6 = ((bf16[8,320,384]{2,1,0:T(8,128)(2,1)}), bf16[8,320,384]{2,1,0:T(8,128)(2,1)}, u32[]{:S(2)}, u32[]{:S(2)}) async-start(bf16[8,320,384]{2,1,0:T(8,128)(2,1)} %bitcast.77), calls=%async_computation.6 | async-start | bytes 3932160 | tf_op jit(solution)/shard_map/all_to_all | solution.py:1245
  362.3 195.1 %reduce-scatter.5.cloned.1.call-start = ((), (), s32[]{:S(2)}) async-start(), calls=%async_computation.14 | async-start | bytes 7372800 | tf_op jit(solution)/shard_map/reduce_scatter | solution.py:1308
  406.3 50.2 %all-to-all-start.4 = ((bf16[8,320,768]{2,1,0:T(8,128)(2,1)}), bf16[8,320,768]{2,1,0:T(8,128)(2,1)}, u32[]{:S(2)}, u32[]{:S(2)}) async-start(bf16[8,320,768]{2,1,0:T(8,128)(2,1)} %bitcast.75), calls=%async_computation.4 | async-start | bytes 7864320 | tf_op jit(solution)/shard_map/all_to_all | solution.py:1245
  470.2 10.6 %collective-permute-start.12 = (bf16[4,400,768]{2,1,0:T(8,128)(2,1)}, bf16[4,400,768]{2,1,0:T(8,128)(2,1)}, u32[]{:S(2)}, u32[]{:S(2)}) collective-permute-start(bf16[4,400,768]{2,1,0:T(8,128)(2,1)} %get-tuple-element.127.refs_7_), channel_id=1, source_target_pairs={{0,2},{1,3},{2,0},{3,1},{4,6},{5,7},{6,4},{7,5},{8,10},{9,11},{10,... | collective-permute-start | bytes 7372808 | tf_op jit(solution)/shard_map/ppermute | solution.py:375
  485.7 16.9 %collective-permute-start.13 = (bf16[400,768]{1,0:T(8,128)(2,1)}, bf16[400,768]{1,0:T(8,128)(2,1)S(1)}, u32[]{:S(2)}, u32[]{:S(2)}) collective-permute-start(bf16[400,768]{1,0:T(8,128)(2,1)} %get-tuple-element.132.refs_6_), channel_id=1, source_target_pairs={{0,4},{1,5},{2,6},{3,7},{4,0},{5,1},{6,2},{7,3},{8,12},{9,13},{10,... | collective-permute-start | bytes 1843208 | tf_op jit(solution)/shard_map/ppermute | solution.py:375
  487.2 27.6 %collective-permute-start.14 = (bf16[400,768]{1,0:T(8,128)(2,1)}, bf16[400,768]{1,0:T(8,128)(2,1)}, u32[]{:S(2)}, u32[]{:S(2)}) collective-permute-start(bf16[400,768]{1,0:T(8,128)(2,1)} %get-tuple-element.133.refs_7_), channel_id=1, source_target_pairs={{0,1},{1,0},{2,3},{3,2},{4,5},{5,4},{6,7},{7,6},{8,9},{9,8},{10,11... | collective-permute-start | bytes 1843208 | tf_op jit(solution)/shard_map/ppermute | solution.py:375
  487.7 28.7 %collective-permute-start.15 = (bf16[400,768]{1,0:T(8,128)(2,1)}, bf16[400,768]{1,0:T(8,128)(2,1)}, u32[]{:S(2)}, u32[]{:S(2)}) collective-permute-start(bf16[400,768]{1,0:T(8,128)(2,1)} %get-tuple-element.134.refs_8_), channel_id=1, source_target_pairs={{0,5},{1,4},{2,7},{3,6},{4,1},{5,0},{6,3},{7,2},{8,13},{9,12},{10,... | collective-permute-start | bytes 1843208 | tf_op jit(solution)/shard_map/ppermute | solution.py:375
  489.2 9.9 %copy-start.10 = (f32[4,3,768]{2,1,0:T(4,128)S(1)}, f32[4,3,768]{2,1,0:T(4,128)}, u32[]{:S(2)}) copy-start(f32[4,3,768]{2,1,0:T(4,128)} %get-tuple-element.137) | copy-start | bytes 110596
  489.2 9.9 %copy-start.11 = (f32[4,1,768]{2,1,0:T(1,128)S(1)}, f32[4,1,768]{2,1,0:T(1,128)}, u32[]{:S(2)}) copy-start(f32[4,1,768]{2,1,0:T(1,128)} %get-tuple-element.130.refs_0_) | copy-start | bytes 36868
  502.6 18.8 %copy-start.8 = (bf16[400,768]{1,0:T(8,128)(2,1)}, bf16[400,768]{1,0:T(8,128)(2,1)S(1)}, u32[]{:S(2)}) copy-start(bf16[400,768]{1,0:T(8,128)(2,1)S(1)} %collective-permute-done.13.refs_0_) | copy-start | bytes 1843204
  517.2 16.4 %all-to-all-start.8 = ((bf16[32,4,576]{2,1,0:T(4,128)(2,1)}), bf16[32,4,576]{2,1,0:T(4,128)(2,1)S(1)}, u32[]{:S(2)}, u32[]{:S(2)}) async-start(bf16[32,4,576]{2,1,0:T(4,128)(2,1)} %bitcast.24), calls=%async_computation.9 | async-start | bytes 327680 | tf_op jit(solution)/shard_map/all_to_all | solution.py:1340
  525.1 18.6 %copy-start.9 = (bf16[128,192]{1,0:T(8,128)(2,1)S(1)}, bf16[128,192]{1,0:T(8,128)(2,1)}, u32[]{:S(2)}) copy-start(bf16[128,192]{1,0:T(8,128)(2,1)} %reshape.191.refs_13_) | copy-start | bytes 147460
  535.7 11.1 %collective-permute-start.16 = (bf16[192,400]{0,1:T(8,128)(2,1)}, bf16[192,400]{0,1:T(8,128)(2,1)S(1)}, u32[]{:S(2)}, u32[]{:S(2)}) collective-permute-start(bf16[192,400]{0,1:T(8,128)(2,1)} %bitcast.29), channel_id=1, source_target_pairs={{0,8},{8,16},{16,24},{24,0},{1,9},{9,17},{17,25},{25,1},{2,10},{10... | collective-permute-start | bytes 460808 | tf_op jit(solution)/shard_map/ppermute | solution.py:609
  537.5 17.5 %collective-permute-start.17 = (bf16[192,400]{0,1:T(8,128)(2,1)}, bf16[192,400]{0,1:T(8,128)(2,1)S(1)}, u32[]{:S(2)}, u32[]{:S(2)}) collective-permute-start(bf16[192,400]{0,1:T(8,128)(2,1)} %bitcast.30), channel_id=1, source_target_pairs={{0,16},{8,24},{16,0},{24,8},{1,17},{9,25},{17,1},{25,9},{2,18},{10... | collective-permute-start | bytes 460808 | tf_op jit(solution)/shard_map/ppermute | solution.py:609
  540.7 14.4 %collective-permute-start.18 = (bf16[192,400]{0,1:T(8,128)(2,1)}, bf16[192,400]{0,1:T(8,128)(2,1)S(1)}, u32[]{:S(2)}, u32[]{:S(2)}) collective-permute-start(bf16[192,400]{0,1:T(8,128)(2,1)} %bitcast.31), channel_id=1, source_target_pairs={{0,24},{8,0},{16,8},{24,16},{1,25},{9,1},{17,9},{25,17},{2,26},{10... | collective-permute-start | bytes 460808 | tf_op jit(solution)/shard_map/ppermute | solution.py:609
  559.1 16.5 %all-to-all-start.9 = ((f32[32,4,192]{2,1,0:T(4,128)}), f32[32,4,192]{2,1,0:T(4,128)S(1)}, u32[]{:S(2)}, u32[]{:S(2)}) async-start(f32[32,4,192]{2,1,0:T(4,128)} %reshape.195), calls=%async_computation.11 | async-start | bytes 262144 | tf_op jit(solution)/shard_map/all_to_all | solution.py:1351
  568.3 7.5 %copy-start.13 = (bf16[4,768]{1,0:T(4,128)(2,1)S(1)}, bf16[4,768]{1,0:T(4,128)(2,1)}, u32[]{:S(2)}) copy-start(bf16[4,768]{1,0:T(4,128)(2,1)} %cond_ref.1) | copy-start | bytes 18436
Sparse Core Ops, SparseCore 0:
  37.2 33.5 all-gather.5
  88.7 167.5 all-gather.3
  347.6 84.1 reduce-scatter.2
  434.0 107.5 reduce-scatter.4

commit v5 on v3

--- a/solution.py
+++ b/solution.py
@@ -1202,8 +1202,9 @@
         first_end = 4 * width + 128
         silu_parts = first_stack[:, :cond_rows, first_end : first_end + local]
         rest_piece = rest_payload(
-            shared_up, shared_down, slice_rows, (first_stack, places, expert_piece)
+            shared_up, shared_down, slice_rows, (places, expert_piece)
         )
+        rest_piece, first_stack = together(rest_piece, first_stack)
     else:
         silu_cond = jax.nn.silu(cond_wide).astype(NARROW_TYPE)
         silu_parts = lax.all_to_all(
@@ -1247,8 +1248,8 @@
     grad_shared, mixture_slots = spread_mixture(
         out_grad, mods, places, silu_parts.reshape(SPARE, -1), ()
     )
+    expert_piece, *first_sides = together(expert_piece, *first_sides)
     first_near = near_slices(first_sides, (mixture_slots,))
-    expert_piece, first_near = together(expert_piece, first_near)
     expert_weights = lax.all_gather(expert_piece, "dp", axis=0, tiled=True)
     mixture_slots = exchange(mixture_slots)
     first_full = plane_gather(first_near)

time: 585 us -> 580 us (level)
  Pallas kernels: 357 us -> 328 us
  waiting for transfers between devices: 104 us -> 131 us
    all_to_all x6, waiting for transfers between devices: 8.37 us -> 26.8 us  [exchange(): return lax.all_to_all(rows, PLANE, split_axis=0, concat_axis=0, tiled=True)]
    pallas_call x1, Pallas kernels: 40.7 us -> 22.4 us  [attend_back(): pl.pallas_call(attend_back_kernel, grid=(width // 128,), in_specs=[pl.Blo...]
    ppermute x16, waiting for transfers between devices: 59.7 us -> 71.1 us  [flip(): lax.ppermute(value, PLANE, [(index, index ^ mask) for index in range(coun...]
    pallas_call x1, Pallas kernels: 26.1 us -> 15.2 us  [attend(): pl.pallas_call(attend_kernel, grid=(width // 128,), in_specs=[pl.BlockSpe...]
  transfers between devices with their start and end apart: 33 -> 33, of which waited for: 16 -> 15; matrix products, arithmetic and copies ran while one was open for 4% -> 4% of each run, Pallas kernels for 61% -> 56%
where the time goes in v5:
time: 580 us; the launch traced here: 572 us
  Pallas kernels  328 us (57%)
  waiting for transfers between devices  131 us (23%)
  starting transfers between devices  65.8 us (11%)
  local copies, waits for them, and re-layouts  21.7 us (4%)
  between operations  15.2 us (3%)
  other arithmetic  8.38 us (1%)
    pallas_call x13, Pallas kernels, stepped(): pl.pallas_call(body, grid=(steps,), in_specs=list(in_specs) + [ANYWHERE]...  190 us
    ppermute x16, waiting for transfers between devices, flip(): lax.ppermute(value, PLANE, [(index, index ^ mask) for index in range(coun...  71.1 us
    pallas_call x1, Pallas kernels, shared_expert(): pl.pallas_call(kernel, grid_spec=pltpu.PrefetchScalarGridSpec(num_scalar_...  44.3 us
    all_to_all x6, waiting for transfers between devices, exchange(): return lax.all_to_all(rows, PLANE, split_axis=0, concat_axis=0, tiled=True)  26.8 us
    all_to_all x6, starting transfers between devices, exchange(): return lax.all_to_all(rows, PLANE, split_axis=0, concat_axis=0, tiled=True)  25.9 us
    pallas_call x1, Pallas kernels, attend_back(): pl.pallas_call(attend_back_kernel, grid=(width // 128,), in_specs=[pl.Blo...  22.4 us
    pallas_call x1, Pallas kernels, attend(): pl.pallas_call(attend_kernel, grid=(width // 128,), in_specs=[pl.BlockSpe...  15.2 us
    ppermute x16, starting transfers between devices, flip(): lax.ppermute(value, PLANE, [(index, index ^ mask) for index in range(coun...  15 us
  transfers between devices with their start and end apart: 33, of which 15 were waited for; matrix products, arithmetic and copies ran while one was open for 4% of the time, Pallas kernels for 56%

profile of v5, /device:TPU:0, one launch (start us, length us, event | category | flops | bytes accessed | tf_op | source)
XLA Modules:
  0.0 572.4 jit_solution(3553722981958630928)
XLA Ops:
  10.6 6.3 %all-to-all-start = ((bf16[4,24,3456]{2,1,0:T(8,128)(2,1)}), bf16[4,24,3456]{2,1,0:T(8,128)(2,1)S(1)}, u32[]{:S(2)}, u32[]{:S(2)}) async-start(bf16[4,24,3456]{2,1,0:T(8,128)(2,1)} %first_payload.1), calls=%async_computation | async-start | bytes 1327104 | tf_op jit(solution)/shard_map/all_to_all | solution.py:1195
  25.0 3.4 expert_payload.1.refs_1_
  30.1 4.3 all-to-all-done.refs_0_
  35.5 3.5 all-to-all-start.1
  43.8 10.0 %all-to-all-done.1 = f32[4,4,4608]{2,1,0:T(4,128)S(1)} async-done(((f32[4,4,4608]{2,1,0:T(4,128)}), f32[4,4,4608]{2,1,0:T(4,128)S(1)}, u32[]{:S(2)}, u32[]{:S(2)}) %all-to-all-start.1) | async-done | bytes 294944 | tf_op jit(solution)/shard_map/all_to_all | solution.py:1236
  54.6 8.2 %spread_mixture.1 = (bf16[1024,768]{1,0:T(8,128)(2,1)}, bf16[8,336,768]{2,1,0:T(8,128)(2,1)}) custom-call(bf16[1024,768]{1,0:T(8,128)(2,1)} %refs_5_.1, f32[4,6,768]{2,1,0:T(8,128)} %broadcast_select_fusion.refs_1_.refs_2_.refs_9_.refs_4_.refs_3_, s32[2,1024]{1,0:T(2,128)} %copy.108.refs_0_.refs_2_.refs_1_, bf16[16,192]{1,0:T(8,128)(2,1)} %reshape.179.refs_3_), custom_call_target="tpu_custom_call" | custom-call | tf_op jit(solution)/shard_map/spread_mixture/pallas_call | solution.py:406
  62.8 4.6 all-to-all-start.2
  67.6 13.6 %collective-permute-done.1.refs_2_ = bf16[4,24,3456]{2,1,0:T(8,128)(2,1)} collective-permute-done((bf16[4,24,3456]{2,1,0:T(8,128)(2,1)S(1)}, bf16[4,24,3456]{2,1,0:T(8,128)(2,1)}, u32[]{:S(2)}, u32[]{:S(2)}) %collective-permute-start.1) | collective-permute-done | bytes 663584 | tf_op jit(solution)/shard_map/ppermute | solution.py:375
  81.3 4.1 stack_sides.2.near_ref
  85.4 2.8 collective-permute-start.5
  90.6 6.4 %place_slices.2 = bf16[4,8,24,3456]{3,2,1,0:T(8,128)(2,1)} custom-call(s32[5]{0:T(128)} %stack.26.order_ref, bf16[4,4,24,3456]{3,2,1,0:T(8,128)(2,1)} %stack_sides.2.near_ref, bf16[4,4,24,3456]{3,2,1,0:T(8,128)(2,1)} %collective-permute-done.3.far_ref), custom_call_target="tpu_custom_call" | custom-call | tf_op jit(solution)/shard_map/place_slices/pallas_call | solution.py:463
  97.1 8.5 %first_half.1 = (bf16[1024,768]{1,0:T(8,128)(2,1)}, bf16[3,1024,768]{2,1,0:T(8,128)(2,1)}) custom-call(bf16[1024,768]{1,0:T(8,128)(2,1)} %refs_2_.1, f32[4,6,768]{2,1,0:T(8,128)} %broadcast_select_fusion.refs_1_.refs_2_.refs_9_.refs_4_.refs_3_, bf16[768,3456]{1,0:T(8,128)(2,1)} %bitcast.66), custom_call_target="tpu_custom_call" | custom-call | tf_op jit(solution)/shard_map/first_half/pallas_call | solution.py:406
  105.5 15.2 %attend.1 = (bf16[1024,768]{1,0:T(8,128)(2,1)}, f32[1024,768]{1,0:T(8,128)}) custom-call(s32[1]{0:T(128)S(6)} %copy.131.long_ref, bf16[3,1024,768]{2,1,0:T(8,128)(2,1)} %get-tuple-element.91.joined_ref), custom_call_target="tpu_custom_call" | custom-call | tf_op jit(solution)/shard_map/attend/pallas_call | solution.py:73
  120.7 7.3 %second_half.1 = (f32[1024,768]{1,0:T(8,128)}, f32[1024,768]{1,0:T(8,128)}, bf16[1024,768]{1,0:T(8,128)(2,1)}, f32[1024,2]{1,0:T(8,128)}, f32[2,1024]{1,0:T(2,128)}) custom-call(bf16[1024,768]{1,0:T(8,128)(2,1)} %get-tuple-element.93.refs_0_.refs_4_, bf16[1024,768]{1,0:T(8,128)(2,1)} %refs_2_.1, ...), custom_call_target="tpu_custom_call" | custom-call | tf_op jit(solution)/shard_map/second_half/pallas_call | solution.py:406
  128.0 8.6 %spread_second.1.refs_5_ = bf16[8,336,768]{2,1,0:T(8,128)(2,1)} custom-call(bf16[1024,768]{1,0:T(8,128)(2,1)} %get-tuple-element.94.refs_0_.refs_1_.refs_6_, s32[2,1024]{1,0:T(2,128)} %copy.108.refs_0_.refs_2_.refs_1_, f32[2,1024]{1,0:T(2,128)} %get-tuple-element.97.refs_2_), custom_call_target="tpu_custom_call" | custom-call | tf_op jit(solution)/shard_map/spread_second/pallas_call | solution.py:406
  136.6 4.0 collective-permute-done.4.refs_1_
  140.6 25.8 %collective-permute-done.6.refs_3_ = bf16[4,24,6144]{2,1,0:T(8,128)(2,1)} collective-permute-done((bf16[4,24,6144]{2,1,0:T(8,128)(2,1)}, bf16[4,24,6144]{2,1,0:T(8,128)(2,1)}, u32[]{:S(2)}, u32[]{:S(2)}) %collective-permute-start.6) | collective-permute-done | bytes 1179680 | tf_op jit(solution)/shard_map/ppermute | solution.py:375
  166.4 5.0 stack_sides.3.near_ref
  171.3 4.6 all-to-all-start.3
  175.9 3.7 collective-permute-done.7.far_ref
  179.6 8.3 %place_slices.3 = bf16[4,8,24,6144]{3,2,1,0:T(8,128)(2,1)} custom-call(s32[5]{0:T(128)} %stack.26.order_ref, bf16[4,4,24,6144]{3,2,1,0:T(8,128)(2,1)} %stack_sides.3.near_ref, bf16[4,4,24,6144]{3,2,1,0:T(8,128)(2,1)} %collective-permute-done.7.far_ref), custom_call_target="tpu_custom_call" | custom-call | tf_op jit(solution)/shard_map/place_slices/pallas_call | solution.py:463
  187.9 44.3 %shared_expert.1 = (f32[1024,768]{1,0:T(8,128)}, f32[1024,768]{1,0:T(8,128)}, bf16[4,768,768]{2,1,0:T(8,128)(2,1)}, bf16[4,768,768]{2,1,0:T(8,128)(2,1)}) custom-call(s32[1]{0:T(128)} %bitcast.refs_0_, bf16[1024,768]{1,0:T(8,128)(2,1)} %get-tuple-element.94.refs_0_.refs_1_.refs_6_, bf16[1024,768]{1,0:T(8,128)(2,1)} %get-tuple-element.95.refs_2_, ...), custom_call_target="tpu_custom_call" | custom-call | tf_op jit(solution)/shard_map/shared_expert/pallas_call | solution.py:354
  232.4 8.1 %collective-permute-done.8.other_ref = bf16[4,768,768]{2,1,0:T(8,128)(2,1)} collective-permute-done((bf16[4,768,768]{2,1,0:T(8,128)(2,1)}, bf16[4,768,768]{2,1,0:T(8,128)(2,1)}, u32[]{:S(2)}, u32[]{:S(2)}) %collective-permute-start.8) | collective-permute-done | bytes 4718624 | tf_op jit(solution)/shard_map/ppermute | solution.py:375
  240.5 7.3 %pair_sum.2 = (f32[768,768]{1,0:T(8,128)}, bf16[768,768]{1,0:T(8,128)(2,1)}, bf16[768,768]{1,0:T(8,128)(2,1)}, bf16[768,768]{1,0:T(8,128)(2,1)}) custom-call(s32[1]{0:T(128)} %bitcast.4.place_ref, bf16[4,768,768]{2,1,0:T(8,128)(2,1)} %get-tuple-element.102.kept_ref, bf16[4,768,768]{2,1,0:T(8,128)(2,1)} %collective-permute-done.8.other_ref), custom_call_target="tpu_custom_call" | custom-call | tf_op jit(solution)/shard_map/pair_sum/pallas_call | solution.py:502
  251.3 61.4 %routed_expert.1 = (bf16[2560,768]{1,0:T(8,128)(2,1)}, bf16[2560,384]{1,0:T(8,128)(2,1)}, bf16[2560,384]{1,0:T(8,128)(2,1)}, f32[2560,1]{1,0:T(8,128)}, bf16[256...) custom-call(bf16[8,336,768]{2,1,0:T(8,128)(2,1)} %all-to-all-done.3.refs_0_, bf16[8,336,768]{2,1,0:T(8,128)(2,1)} %all-to-all-done.2.refs_1_, ...), custom_call_target="tpu_custom_call" | custom-call | tf_op jit(solution)/shard_map/routed_expert/pallas_call | solution.py:406
  313.8 4.3 all-to-all-start.5
  318.2 20.6 %routed_sums.2.refs_3_.refs_5_ = bf16[768,3072]{1,0:T(8,128)(2,1)} custom-call(bf16[8,336,768]{2,1,0:T(8,128)(2,1)} %all-to-all-done.3.refs_0_, bf16[8,336,768]{2,1,0:T(8,128)(2,1)} %all-to-all-done.2.refs_1_, bf16[2560,3072]{1,0:T(8,128)(2,1)} %get-tuple-element.109.refs_2_, bf16[2560,3072]{1,0:T(8,128)(2,1)} %get-tuple-element.110.refs_3_), custom_call_target="tpu_custom_call" | custom-call | tf_op jit(solution)/shard_map/routed_sums/pallas_call | solution.py:406
  338.8 3.7 all-to-all-done.5
  344.9 3.3 all-to-all-start.7
  348.3 5.1 side_sum.2.refs_4_
  353.3 4.4 all-to-all-start.6
  359.4 22.7 %routed_sums.3 = bf16[768,3840]{1,0:T(8,128)(2,1)} custom-call(bf16[8,336,768]{2,1,0:T(8,128)(2,1)} %all-to-all-done.3.refs_0_, bf16[8,336,768]{2,1,0:T(8,128)(2,1)} %all-to-all-done.2.refs_1_, bf16[2560,3072]{1,0:T(8,128)(2,1)} %get-tuple-element.109.refs_2_, bf16[2560,3072]{1,0:T(8,128)(2,1)} %get-tuple-element.110.refs_3_, ...), custom_call_target="tpu_custom_call" | custom-call | tf_op jit(solution)/shard_map/routed_sums/pallas_call | solution.py:406
  382.7 18.7 %middle_back.1 = (f32[1024,768]{1,0:T(8,128)}, bf16[1024,768]{1,0:T(8,128)(2,1)}, bf16[1024,768]{1,0:T(8,128)(2,1)}, bf16[1024,128]{1,0:T(8,128)(2,1)}, f32[4,3,768]{2,1,0:T(4,128)}) custom-call(bf16[2560,384]{1,0:T(8,128)(2,1)} %bitcast.19.refs_0_, bf16[2560,384]{1,0:T(8,128)(2,1)} %bitcast.21.refs_1_, f32[1,2560]{1,0:T(1,128)} %reshape.189.refs_2_, ...), custom_call_target="tpu_custom_call" | custom-call | tf_op jit(solution)/shard_map/middle_back/pallas_call | solution.py:406
  401.5 4.7 all-to-all-start.4
  406.2 22.4 %attend_back.1.refs_1_.refs_0_ = bf16[3,1024,768]{2,1,0:T(8,128)(2,1)} custom-call(s32[1]{0:T(128)S(6)} %copy.131.long_ref, bf16[3,1024,768]{2,1,0:T(8,128)(2,1)} %get-tuple-element.91.joined_ref, f32[1024,768]{1,0:T(8,128)} %get-tuple-element.108.total_ref, bf16[1024,768]{1,0:T(8,128)(2,1)} %get-tuple-element.132.grad_ref), custom_call_target="tpu_custom_call" | custom-call | tf_op jit(solution)/shard_map/attend_back/pallas_call | solution.py:121
  428.5 23.1 %all-to-all-done.4 = bf16[8,320,768]{2,1,0:T(8,128)(2,1)} async-done(((bf16[8,320,768]{2,1,0:T(8,128)(2,1)}), bf16[8,320,768]{2,1,0:T(8,128)(2,1)}, u32[]{:S(2)}, u32[]{:S(2)}) %all-to-all-start.4) | async-done | bytes 3932192 | tf_op jit(solution)/shard_map/all_to_all | solution.py:1246
  451.6 13.8 %last_gradients.1 = (bf16[4,400,768]{2,1,0:T(8,128)(2,1)}, bf16[4,400,768]{2,1,0:T(8,128)(2,1)}) custom-call(s32[1]{0:T(128)} %bitcast.refs_0_, bf16[3,1024,768]{2,1,0:T(8,128)(2,1)} %attend_back.1.refs_1_.refs_0_, bf16[1024,768]{1,0:T(8,128)(2,1)} %get-tuple-element.133.refs_2_, bf16[1024,768]{1,0:T(8,128)(2,1)} %get-tuple-element.134.refs_3_, ...), custom_call_target="tpu_custom_call" | custom-call | tf_op jit(solution)/shard_map/last_gradients/pallas_call | solution.py:581
  465.4 10.6 %block_output.1 = (bf16[1024,768]{1,0:T(8,128)(2,1)}, f32[4,1,768]{2,1,0:T(1,128)}) custom-call(bf16[2560,768]{1,0:T(8,128)(2,1)} %bitcast.17.refs_7_.refs_0_, s32[1024,2]{1,0:T(8,128)} %copy-done.2, f32[1024,768]{1,0:T(8,128)} %get-tuple-element.106.refs_2_, f32[1024,768]{1,0:T(8,128)} %get-tuple-element.107.refs_7_.refs_3_, ...), custom_call_target="tpu_custom_call" | custom-call | tf_op jit(solution)/shard_map/block_output/pallas_call | solution.py:406
  476.0 4.9 pair_sum.3
  484.4 9.9 %start_back.1 = (f32[1024,768]{1,0:T(8,128)}, f32[4,2,768]{2,1,0:T(2,128)}) custom-call(bf16[3,1024,768]{2,1,0:T(8,128)(2,1)} %attend_back.1.refs_1_.refs_0_, bf16[768,3456]{1,0:T(8,128)(2,1)} %bitcast.71, bf16[1024,768]{1,0:T(8,128)(2,1)} %refs_2_.1, f32[4,6,768]{2,1,0:T(8,128)} %broadcast_select_fusion.refs_1_.refs_2_.refs_9_.refs_4_.refs_3_, ...), custom_call_target="tpu_custom_call" | custom-call | tf_op jit(solution)/shard_map/start_back/pallas_call | solution.py:406
  497.8 13.9 %collective-permute-done.14.refs_1_ = bf16[400,768]{1,0:T(8,128)(2,1)} collective-permute-done((bf16[400,768]{1,0:T(8,128)(2,1)}, bf16[400,768]{1,0:T(8,128)(2,1)}, u32[]{:S(2)}, u32[]{:S(2)}) %collective-permute-start.14) | collective-permute-done | bytes 614432 | tf_op jit(solution)/shard_map/ppermute | solution.py:375
  512.4 4.6 all-to-all-start.8
  517.1 3.8 side_sum.3
  520.9 8.6 %all-to-all-done.8 = bf16[32,4,576]{2,1,0:T(4,128)(2,1)S(1)} async-done(((bf16[32,4,576]{2,1,0:T(4,128)(2,1)}), bf16[32,4,576]{2,1,0:T(4,128)(2,1)S(1)}, u32[]{:S(2)}, u32[]{:S(2)}) %all-to-all-start.8) | async-done | bytes 147488 | tf_op jit(solution)/shard_map/all_to_all | solution.py:1341
  530.6 4.5 all-to-all-start.9
  539.2 2.4 collective-permute-start.17
  546.8 8.3 %collective-permute-done.17 = bf16[192,400]{0,1:T(8,128)(2,1)S(1)} collective-permute-done((bf16[192,400]{0,1:T(8,128)(2,1)}, bf16[192,400]{0,1:T(8,128)(2,1)S(1)}, u32[]{:S(2)}, u32[]{:S(2)}) %collective-permute-start.17) | collective-permute-done | bytes 153632 | tf_op jit(solution)/shard_map/ppermute | solution.py:609
  561.4 4.2 expert_sums.1
  (138 shorter events, 55.8 us)
Async XLA Ops:
  7.2 27.3 %copy-start = (bf16[192,4608]{1,0:T(8,128)(2,1)S(1)}, bf16[192,4608]{1,0:T(8,128)(2,1)}, u32[]{:S(2)}) copy-start(bf16[192,4608]{1,0:T(8,128)(2,1)} %param.17) | copy-start | bytes 5308420
  7.2 9.7 %copy-start.11 = (s32[1024,2]{0,1:T(2,128)S(1)}, s32[1024,2]{0,1:T(2,128)}, u32[]{:S(2)}) copy-start(s32[1024,2]{0,1:T(2,128)} %param.16) | copy-start | bytes 24580
  10.6 23.8 %all-to-all-start = ((bf16[4,24,3456]{2,1,0:T(8,128)(2,1)}), bf16[4,24,3456]{2,1,0:T(8,128)(2,1)S(1)}, u32[]{:S(2)}, u32[]{:S(2)}) async-start(bf16[4,24,3456]{2,1,0:T(8,128)(2,1)} %first_payload.1), calls=%async_computation | async-start | bytes 1327104 | tf_op jit(solution)/shard_map/all_to_all | solution.py:1195
  16.9 68.4 %all-gather.6.cloned.1.call-start = ((), (), s32[]{:S(2)}) async-start(), calls=%async_computation.15 | async-start | bytes 1474560 | tf_op jit(solution)/shard_map/all_gather | solution.py:1234
  17.2 7.0 %copy-start.1 = (s32[1024,2]{1,0:T(8,128)}, s32[1024,2]{1,0:T(8,128)S(1)}, u32[]{:S(2)}) copy-start(s32[1024,2]{1,0:T(8,128)S(1)} %copy.105.refs_3_.refs_4_) | copy-start | bytes 24580
  24.2 4.2 copy-start.2
  34.4 28.4 %copy-start.3 = (bf16[4,24,3456]{2,1,0:T(8,128)(2,1)}, bf16[4,24,3456]{2,1,0:T(8,128)(2,1)S(1)}, u32[]{:S(2)}) copy-start(bf16[4,24,3456]{2,1,0:T(8,128)(2,1)S(1)} %all-to-all-done.refs_0_) | copy-start | bytes 1990660
  35.5 18.3 %all-to-all-start.1 = ((f32[4,4,4608]{2,1,0:T(4,128)}), f32[4,4,4608]{2,1,0:T(4,128)S(1)}, u32[]{:S(2)}, u32[]{:S(2)}) async-start(f32[4,4,4608]{2,1,0:T(4,128)} %fusion), calls=%async_computation.1 | async-start | bytes 589824 | tf_op jit(solution)/shard_map/all_to_all | solution.py:1236
  39.0 28.7 %collective-permute-start = (bf16[4,24,3456]{2,1,0:T(8,128)(2,1)S(1)}, bf16[4,24,3456]{2,1,0:T(8,128)(2,1)}, u32[]{:S(2)}, u32[]{:S(2)}) collective-permute-start(bf16[4,24,3456]{2,1,0:T(8,128)(2,1)S(1)} %all-to-all-done.refs_0_), channel_id=1, source_target_pairs={{0,4},{1,5},{2,6},{3,7},{4,0},{5,1},{6,2},{7,3},{8,12},{9,13},{10,... | collective-permute-start | bytes 1990664 | tf_op jit(solution)/shard_map/ppermute | solution.py:375
  40.5 40.7 %collective-permute-start.1 = (bf16[4,24,3456]{2,1,0:T(8,128)(2,1)S(1)}, bf16[4,24,3456]{2,1,0:T(8,128)(2,1)}, u32[]{:S(2)}, u32[]{:S(2)}) collective-permute-start(bf16[4,24,3456]{2,1,0:T(8,128)(2,1)S(1)} %all-to-all-done.refs_0_), channel_id=1, source_target_pairs={{0,1},{1,0},{2,3},{3,2},{4,5},{5,4},{6,7},{7,6},{8,9},{9,8},{10,11... | collective-permute-start | bytes 1990664 | tf_op jit(solution)/shard_map/ppermute | solution.py:375
  42.0 39.2 %collective-permute-start.2 = (bf16[4,24,3456]{2,1,0:T(8,128)(2,1)S(1)}, bf16[4,24,3456]{2,1,0:T(8,128)(2,1)}, u32[]{:S(2)}, u32[]{:S(2)}) collective-permute-start(bf16[4,24,3456]{2,1,0:T(8,128)(2,1)S(1)} %all-to-all-done.refs_0_), channel_id=1, source_target_pairs={{0,5},{1,4},{2,7},{3,6},{4,1},{5,0},{6,3},{7,2},{8,13},{9,12},{10,... | collective-permute-start | bytes 1990664 | tf_op jit(solution)/shard_map/ppermute | solution.py:375
  62.8 57.9 %all-to-all-start.2 = ((bf16[8,336,768]{2,1,0:T(8,128)(2,1)}), bf16[8,336,768]{2,1,0:T(8,128)(2,1)}, u32[]{:S(2)}, u32[]{:S(2)}) async-start(bf16[8,336,768]{2,1,0:T(8,128)(2,1)} %get-tuple-element.90.refs_4_), calls=%async_computation.2 | async-start | bytes 8257536 | tf_op jit(solution)/shard_map/all_to_all | solution.py:1246
  67.3 184.0 %all-gather.4.cloned.1.call-start = ((), (), s32[]{:S(2)}) async-start(), calls=%async_computation.12 | async-start | bytes 11796480 | tf_op jit(solution)/shard_map/all_gather | solution.py:1253
  85.3 5.3 collective-permute-start.3
  85.4 55.2 %collective-permute-start.4 = (bf16[4,24,6144]{2,1,0:T(8,128)(2,1)}, bf16[4,24,6144]{2,1,0:T(8,128)(2,1)S(1)}, u32[]{:S(2)}, u32[]{:S(2)}) collective-permute-start(bf16[4,24,6144]{2,1,0:T(8,128)(2,1)} %bitcast.83), channel_id=1, source_target_pairs={{0,4},{1,5},{2,6},{3,7},{4,0},{5,1},{6,2},{7,3},{8,12},{9,13},{10,... | collective-permute-start | bytes 3538952 | tf_op jit(solution)/shard_map/ppermute | solution.py:375
  85.4 55.1 %collective-permute-start.5 = (bf16[4,24,6144]{2,1,0:T(8,128)(2,1)}, bf16[4,24,6144]{2,1,0:T(8,128)(2,1)}, u32[]{:S(2)}, u32[]{:S(2)}) collective-permute-start(bf16[4,24,6144]{2,1,0:T(8,128)(2,1)} %bitcast.84), channel_id=1, source_target_pairs={{0,1},{1,0},{2,3},{3,2},{4,5},{5,4},{6,7},{7,6},{8,9},{9,8},{10,11... | collective-permute-start | bytes 3538952 | tf_op jit(solution)/shard_map/ppermute | solution.py:375
  88.2 78.1 %collective-permute-start.6 = (bf16[4,24,6144]{2,1,0:T(8,128)(2,1)}, bf16[4,24,6144]{2,1,0:T(8,128)(2,1)}, u32[]{:S(2)}, u32[]{:S(2)}) collective-permute-start(bf16[4,24,6144]{2,1,0:T(8,128)(2,1)} %bitcast.85), channel_id=1, source_target_pairs={{0,5},{1,4},{2,7},{3,6},{4,1},{5,0},{6,3},{7,2},{8,13},{9,12},{10,... | collective-permute-start | bytes 3538952 | tf_op jit(solution)/shard_map/ppermute | solution.py:375
  140.5 25.8 %copy-start.6 = (bf16[4,24,6144]{2,1,0:T(8,128)(2,1)}, bf16[4,24,6144]{2,1,0:T(8,128)(2,1)S(1)}, u32[]{:S(2)}) copy-start(bf16[4,24,6144]{2,1,0:T(8,128)(2,1)S(1)} %collective-permute-done.4.refs_1_) | copy-start | bytes 3538948
  171.3 8.3 %collective-permute-start.7 = (bf16[4,4,24,6144]{3,2,1,0:T(8,128)(2,1)}, bf16[4,4,24,6144]{3,2,1,0:T(8,128)(2,1)}, u32[]{:S(2)}, u32[]{:S(2)}) collective-permute-start(bf16[4,4,24,6144]{3,2,1,0:T(8,128)(2,1)} %stack_sides.3.near_ref), channel_id=1, source_target_pairs={{0,2},{1,3},{2,0},{3,1},{4,6},{5,7},{6,4},{7,5},{8,10},{9,11},{10,... | collective-permute-start | bytes 14155784 | tf_op jit(solution)/shard_map/ppermute | solution.py:375
  171.3 60.9 %all-to-all-start.3 = ((bf16[8,336,768]{2,1,0:T(8,128)(2,1)}), bf16[8,336,768]{2,1,0:T(8,128)(2,1)}, u32[]{:S(2)}, u32[]{:S(2)}) async-start(bf16[8,336,768]{2,1,0:T(8,128)(2,1)} %spread_second.1.refs_5_), calls=%async_computation.3 | async-start | bytes 8257536 | tf_op jit(solution)/shard_map/all_to_all | solution.py:1246
  232.2 8.3 %collective-permute-start.8 = (bf16[4,768,768]{2,1,0:T(8,128)(2,1)}, bf16[4,768,768]{2,1,0:T(8,128)(2,1)}, u32[]{:S(2)}, u32[]{:S(2)}) collective-permute-start(bf16[4,768,768]{2,1,0:T(8,128)(2,1)} %get-tuple-element.103), channel_id=1, source_target_pairs={{0,2},{1,3},{2,0},{3,1},{4,6},{5,7},{6,4},{7,5},{8,10},{9,11},{10,... | collective-permute-start | bytes 14155784 | tf_op jit(solution)/shard_map/ppermute | solution.py:375
  247.8 64.9 %collective-permute-start.10 = (bf16[768,768]{1,0:T(8,128)(2,1)}, bf16[768,768]{1,0:T(8,128)(2,1)S(1)}, u32[]{:S(2)}, u32[]{:S(2)}) collective-permute-start(bf16[768,768]{1,0:T(8,128)(2,1)} %get-tuple-element.112), channel_id=1, source_target_pairs={{0,1},{1,0},{2,3},{3,2},{4,5},{5,4},{6,7},{7,6},{8,9},{9,8},{10,11... | collective-permute-start | bytes 3538952 | tf_op jit(solution)/shard_map/ppermute | solution.py:375
  248.4 64.4 %collective-permute-start.11 = (bf16[768,768]{1,0:T(8,128)(2,1)}, bf16[768,768]{1,0:T(8,128)(2,1)}, u32[]{:S(2)}, u32[]{:S(2)}) collective-permute-start(bf16[768,768]{1,0:T(8,128)(2,1)} %get-tuple-element.113), channel_id=1, source_target_pairs={{0,5},{1,4},{2,7},{3,6},{4,1},{5,0},{6,3},{7,2},{8,13},{9,12},{10,... | collective-permute-start | bytes 3538952 | tf_op jit(solution)/shard_map/ppermute | solution.py:375
  249.8 62.9 %collective-permute-start.9 = (bf16[768,768]{1,0:T(8,128)(2,1)}, bf16[768,768]{1,0:T(8,128)(2,1)}, u32[]{:S(2)}, u32[]{:S(2)}) collective-permute-start(bf16[768,768]{1,0:T(8,128)(2,1)} %get-tuple-element.111), channel_id=1, source_target_pairs={{0,4},{1,5},{2,6},{3,7},{4,0},{5,1},{6,2},{7,3},{8,12},{9,13},{10,... | collective-permute-start | bytes 3538952 | tf_op jit(solution)/shard_map/ppermute | solution.py:375
  312.8 1.0 copy-start.5
  313.8 28.7 %all-to-all-start.5 = ((bf16[8,320,384]{2,1,0:T(8,128)(2,1)}), bf16[8,320,384]{2,1,0:T(8,128)(2,1)}, u32[]{:S(2)}, u32[]{:S(2)}) async-start(bf16[8,320,384]{2,1,0:T(8,128)(2,1)} %bitcast.78), calls=%async_computation.5 | async-start | bytes 3932160 | tf_op jit(solution)/shard_map/all_to_all | solution.py:1246
  318.2 147.3 %reduce-scatter.3.cloned.1.call-start = ((), (), s32[]{:S(2)}) async-start(), calls=%async_computation.13 | async-start | bytes 5898240 | tf_op jit(solution)/shard_map/reduce_scatter | solution.py:1287
  342.5 1.3 copy-start.4
  344.9 8.4 %all-to-all-start.7 = ((f32[8,1,320]{2,1,0:T(1,128)}), f32[8,1,320]{2,1,0:T(1,128)S(1)}, u32[]{:S(2)}, u32[]{:S(2)}) async-start(f32[8,1,320]{2,1,0:T(1,128)} %reshape.204), calls=%async_computation.7 | async-start | bytes 24576 | tf_op jit(solution)/shard_map/all_to_all | solution.py:1246
  353.3 29.4 %all-to-all-start.6 = ((bf16[8,320,384]{2,1,0:T(8,128)(2,1)}), bf16[8,320,384]{2,1,0:T(8,128)(2,1)}, u32[]{:S(2)}, u32[]{:S(2)}) async-start(bf16[8,320,384]{2,1,0:T(8,128)(2,1)} %bitcast.77), calls=%async_computation.6 | async-start | bytes 3932160 | tf_op jit(solution)/shard_map/all_to_all | solution.py:1246
  357.7 199.7 %reduce-scatter.5.cloned.1.call-start = ((), (), s32[]{:S(2)}) async-start(), calls=%async_computation.14 | async-start | bytes 7372800 | tf_op jit(solution)/shard_map/reduce_scatter | solution.py:1309
  401.5 50.2 %all-to-all-start.4 = ((bf16[8,320,768]{2,1,0:T(8,128)(2,1)}), bf16[8,320,768]{2,1,0:T(8,128)(2,1)}, u32[]{:S(2)}, u32[]{:S(2)}) async-start(bf16[8,320,768]{2,1,0:T(8,128)(2,1)} %bitcast.75), calls=%async_computation.4 | async-start | bytes 7864320 | tf_op jit(solution)/shard_map/all_to_all | solution.py:1246
  465.4 10.6 %collective-permute-start.12 = (bf16[4,400,768]{2,1,0:T(8,128)(2,1)}, bf16[4,400,768]{2,1,0:T(8,128)(2,1)}, u32[]{:S(2)}, u32[]{:S(2)}) collective-permute-start(bf16[4,400,768]{2,1,0:T(8,128)(2,1)} %get-tuple-element.137.refs_7_), channel_id=1, source_target_pairs={{0,2},{1,3},{2,0},{3,1},{4,6},{5,7},{6,4},{7,5},{8,10},{9,11},{10,... | collective-permute-start | bytes 7372808 | tf_op jit(solution)/shard_map/ppermute | solution.py:375
  480.9 16.9 %collective-permute-start.13 = (bf16[400,768]{1,0:T(8,128)(2,1)}, bf16[400,768]{1,0:T(8,128)(2,1)S(1)}, u32[]{:S(2)}, u32[]{:S(2)}) collective-permute-start(bf16[400,768]{1,0:T(8,128)(2,1)} %get-tuple-element.142.refs_6_), channel_id=1, source_target_pairs={{0,4},{1,5},{2,6},{3,7},{4,0},{5,1},{6,2},{7,3},{8,12},{9,13},{10,... | collective-permute-start | bytes 1843208 | tf_op jit(solution)/shard_map/ppermute | solution.py:375
  482.3 29.4 %collective-permute-start.14 = (bf16[400,768]{1,0:T(8,128)(2,1)}, bf16[400,768]{1,0:T(8,128)(2,1)}, u32[]{:S(2)}, u32[]{:S(2)}) collective-permute-start(bf16[400,768]{1,0:T(8,128)(2,1)} %get-tuple-element.143.refs_7_), channel_id=1, source_target_pairs={{0,1},{1,0},{2,3},{3,2},{4,5},{5,4},{6,7},{7,6},{8,9},{9,8},{10,11... | collective-permute-start | bytes 1843208 | tf_op jit(solution)/shard_map/ppermute | solution.py:375
  482.9 28.8 %collective-permute-start.15 = (bf16[400,768]{1,0:T(8,128)(2,1)}, bf16[400,768]{1,0:T(8,128)(2,1)}, u32[]{:S(2)}, u32[]{:S(2)}) collective-permute-start(bf16[400,768]{1,0:T(8,128)(2,1)} %get-tuple-element.144.refs_8_), channel_id=1, source_target_pairs={{0,5},{1,4},{2,7},{3,6},{4,1},{5,0},{6,3},{7,2},{8,13},{9,12},{10,... | collective-permute-start | bytes 1843208 | tf_op jit(solution)/shard_map/ppermute | solution.py:375
  484.4 9.9 %copy-start.9 = (f32[4,3,768]{2,1,0:T(4,128)S(1)}, f32[4,3,768]{2,1,0:T(4,128)}, u32[]{:S(2)}) copy-start(f32[4,3,768]{2,1,0:T(4,128)} %get-tuple-element.147) | copy-start | bytes 110596
  484.4 9.9 %copy-start.10 = (f32[4,1,768]{2,1,0:T(1,128)S(1)}, f32[4,1,768]{2,1,0:T(1,128)}, u32[]{:S(2)}) copy-start(f32[4,1,768]{2,1,0:T(1,128)} %get-tuple-element.140.refs_0_) | copy-start | bytes 36868
  497.8 19.3 %copy-start.7 = (bf16[400,768]{1,0:T(8,128)(2,1)}, bf16[400,768]{1,0:T(8,128)(2,1)S(1)}, u32[]{:S(2)}) copy-start(bf16[400,768]{1,0:T(8,128)(2,1)S(1)} %collective-permute-done.13.refs_0_) | copy-start | bytes 1843204
  512.4 17.1 %all-to-all-start.8 = ((bf16[32,4,576]{2,1,0:T(4,128)(2,1)}), bf16[32,4,576]{2,1,0:T(4,128)(2,1)S(1)}, u32[]{:S(2)}, u32[]{:S(2)}) async-start(bf16[32,4,576]{2,1,0:T(4,128)(2,1)} %bitcast.24), calls=%async_computation.9 | async-start | bytes 327680 | tf_op jit(solution)/shard_map/all_to_all | solution.py:1341
  529.9 14.1 %copy-start.8 = (bf16[128,192]{1,0:T(8,128)(2,1)S(1)}, bf16[128,192]{1,0:T(8,128)(2,1)}, u32[]{:S(2)}) copy-start(bf16[128,192]{1,0:T(8,128)(2,1)} %reshape.191.refs_13_) | copy-start | bytes 147460
  530.6 26.8 %all-to-all-start.9 = ((f32[32,4,192]{2,1,0:T(4,128)}), f32[32,4,192]{2,1,0:T(4,128)S(1)}, u32[]{:S(2)}, u32[]{:S(2)}) async-start(f32[32,4,192]{2,1,0:T(4,128)} %reshape.195), calls=%async_computation.10 | async-start | bytes 262144 | tf_op jit(solution)/shard_map/all_to_all | solution.py:1352
  536.6 10.2 %collective-permute-start.16 = (bf16[192,400]{0,1:T(8,128)(2,1)S(1)}, bf16[192,400]{0,1:T(8,128)(2,1)S(1)}, u32[]{:S(2)}, u32[]{:S(2)}) collective-permute-start(bf16[192,400]{0,1:T(8,128)(2,1)S(1)} %bitcast.88), channel_id=1, source_target_pairs={{0,8},{8,16},{16,24},{24,0},{1,9},{9,17},{17,25},{25,1},{2,10},{10... | collective-permute-start | bytes 460808 | tf_op jit(solution)/shard_map/ppermute | solution.py:609
  539.2 15.9 %collective-permute-start.17 = (bf16[192,400]{0,1:T(8,128)(2,1)}, bf16[192,400]{0,1:T(8,128)(2,1)S(1)}, u32[]{:S(2)}, u32[]{:S(2)}) collective-permute-start(bf16[192,400]{0,1:T(8,128)(2,1)} %bitcast.30), channel_id=1, source_target_pairs={{0,16},{8,24},{16,0},{24,8},{1,17},{9,25},{17,1},{25,9},{2,18},{10... | collective-permute-start | bytes 460808 | tf_op jit(solution)/shard_map/ppermute | solution.py:609
  542.5 12.7 %collective-permute-start.18 = (bf16[192,400]{0,1:T(8,128)(2,1)}, bf16[192,400]{0,1:T(8,128)(2,1)S(1)}, u32[]{:S(2)}, u32[]{:S(2)}) collective-permute-start(bf16[192,400]{0,1:T(8,128)(2,1)} %bitcast.89), channel_id=1, source_target_pairs={{0,24},{8,0},{16,8},{24,16},{1,25},{9,1},{17,9},{25,17},{2,26},{10... | collective-permute-start | bytes 460808 | tf_op jit(solution)/shard_map/ppermute | solution.py:609
  558.5 2.4 copy-start.12
Sparse Core Ops, SparseCore 0:
  34.5 32.7 all-gather.5
  81.4 168.2 all-gather.3
  342.7 85.0 reduce-scatter.2
  430.0 107.5 reduce-scatter.4
